TPU v7x, 512 devices: a whole 4x4x16 slice. The times are simulated.
512 devices in a mesh: seq: 64 (over z, y), head: 4 (over x), dp: 2 (over core).
Axes of the slice: x: 4, y: 4, z: 16, core: 2. Of those that a mesh axis runs over, the one named last changes fastest.
Arguments:
- queries: bfloat16 [2, 8192, 4096], P('dp', 'seq', 'head'), may hold values from -0.23925781 to 0.23925781
- key_rows: bfloat16 [2, 8192, 4096], P('dp', 'seq', 'head'), may hold values from -0.23925781 to 0.23925781
- values: bfloat16 [2, 8192, 4096], P('dp', 'seq', 'head'), may hold values from -6 to 6
- out_grad: bfloat16 [2, 8192, 4096], P('dp', 'seq', 'head'), may hold values from -6 to 6
- decay_rate: float32 [32], P('head'), may hold values from 4e-05 to 0.025, as said below
- rotation: float32 [4, 4096], P(None, 'head')
- refusal: float32 [4096, 2], P('head')
- proj_weight: float32 [4, 4096], P(None, 'head'), may hold values from -0.09375 to 0.09375
- proj_bias: float32 [4], replicated, may hold values from -4 to 4
- positions: int32 [2, 16], P('dp'), may hold values from 0 to 8191, as said below
Outputs:
- attended: bfloat16 [2, 8192, 4096], P('dp', 'seq', 'head')
- grad_query: bfloat16 [2, 8192, 4096], P('dp', 'seq', 'head')
- grad_key: bfloat16 [2, 8192, 4096], P('dp', 'seq', 'head')
- grad_value: bfloat16 [2, 8192, 4096], P('dp', 'seq', 'head')
- grad_rotation: float32 [4, 4096], P(None, 'head')
- grad_weight: float32 [4, 4096], P(None, 'head')
- grad_bias: float32 [4], replicated
Inputs may be any that keep to these rules, and one draw needn't show every extreme that they name: 16 distinct positions in ascending order; among them always 0, 4096 and 8191. `decay_rate`: one rate per head, the same at every position.
All inputs are finite; a program needn't handle non-finite values.
Results may differ from a plain program's by a relative error of at most 0.0032.
Values sent between devices are 32-bit elements; how exact they have to be, the bound alone decides.
No kernel may reach another device: no remote copies, remote signals or barrier semaphores. Data moves between devices by JAX's collectives and lax.ppermute only.
A program may use at most 128 MiB of HBM per device.

v0:
```python
import jax
import jax.numpy as jnp
from jax import lax
from jax.sharding import PartitionSpec as P

highest = lax.Precision.HIGHEST


def carried_in(x, axis, combine, identity, reverse):
    peers, place = (lax.axis_size(axis), lax.axis_index(axis))
    everything = jax.tree.map(lambda part: lax.all_gather(part, axis), x)
    start = jax.tree.map(
        lambda part, zero: jnp.broadcast_to(jnp.asarray(zero, part.dtype), part.shape), x, identity
    )

    def lap(k, before):
        at = peers - 1 - k if reverse else k
        reached = at > place if reverse else at < place
        new = combine(before, jax.tree.map(lambda part: part[at], everything))
        return jax.tree.map(lambda a, b: jnp.where(reached, a, b), new, before)

    return lax.fori_loop(0, peers, lap, start)


def decay_table(log_decay, count):
    offsets = jnp.arange(count)
    between = offsets[:, None] - offsets[None, :]
    powers = jnp.exp(jnp.maximum(between, 0).astype(jnp.float32)[None] * log_decay[:, None, None])
    return jnp.where(between[None] >= 0, powers, 0.0)


def gram_inverse(gram):
    determinant = gram[0, 0] * gram[1, 1] - gram[0, 1] * gram[1, 0]
    adjugate = jnp.stack(
        [jnp.stack([gram[1, 1], -gram[0, 1]]), jnp.stack([-gram[1, 0], gram[0, 0]])]
    )
    return adjugate / determinant


def chain_combine(earlier, later):
    return (earlier[0] * later[0], later[0][:, None, None] * earlier[1] + later[1])


def shards(
    queries,
    key_rows,
    values,
    out_grad,
    decay_rate,
    rotation,
    refusal,
    proj_weight,
    proj_bias,
    positions,
):
    group = queries.shape[1]
    local_width = queries.shape[2]
    local_heads = decay_rate.shape[0]
    head_size = local_width // local_heads
    query_heads = queries[0].reshape(group, local_heads, head_size)
    key_heads = key_rows[0].reshape(group, local_heads, head_size)
    grad_heads = out_grad[0].reshape(group, local_heads, head_size)
    places = lax.axis_index("seq") * group + jnp.arange(group, dtype=jnp.int32)
    selector = places[:, None] == positions[0][None, :]
    select_low = selector.astype(jnp.bfloat16)
    select_full = selector.astype(jnp.float32)
    picked = jnp.dot(select_low.T, values[0], preferred_element_type=jnp.float32)
    gram_part = jnp.dot(refusal.T, refusal, precision=highest)
    coupling_part = jnp.dot(rotation, refusal, precision=highest)
    gram, coupling = lax.psum((gram_part, coupling_part), "head")
    inverse = gram_inverse(gram)
    rotated = rotation - jnp.dot(
        jnp.dot(coupling, inverse, precision=highest), refusal.T, precision=highest
    )
    code = (
        lax.psum(jnp.dot(picked, (proj_weight - rotated).T, precision=highest), "head") + proj_bias
    )
    shift_rows = jnp.dot(code, rotated, precision=highest)
    moved = (
        values[0].astype(jnp.float32) + jnp.dot(select_full, shift_rows, precision=highest)
    ).astype(jnp.bfloat16)
    moved_heads = moved.reshape(group, local_heads, head_size)
    log_decay = jnp.log1p(-decay_rate)
    table = decay_table(log_decay, group)
    offsets = jnp.arange(group).astype(jnp.float32)
    enter = jnp.exp((offsets + 1.0)[:, None] * log_decay[None, :])
    leave = jnp.exp((group - offsets)[:, None] * log_decay[None, :])
    start_weight = jnp.exp(offsets[:, None] * log_decay[None, :])
    end_weight = jnp.exp((group - 1.0 - offsets)[:, None] * log_decay[None, :])
    keep = jnp.exp(group * log_decay)
    query_full = query_heads.astype(jnp.float32)
    key_full = key_heads.astype(jnp.float32)
    moved_full = moved_heads.astype(jnp.float32)
    grad_full = grad_heads.astype(jnp.float32)
    local_state = jnp.einsum(
        "shd,she->hde", key_full * end_weight[:, :, None], moved_full, precision=highest
    )
    local_grad = jnp.einsum(
        "thd,the->hde", query_full * start_weight[:, :, None], grad_full, precision=highest
    )
    blank = (jnp.ones_like(keep), jnp.zeros_like(local_state))
    entering = carried_in((keep, local_state), "seq", chain_combine, blank, False)[1]
    leaving = carried_in((keep, local_grad), "seq", chain_combine, blank, True)[1]
    scores = jnp.einsum("thd,shd->hts", query_heads, key_heads, preferred_element_type=jnp.float32)
    mixing = (scores * table).astype(jnp.bfloat16)
    inner = jnp.einsum("hts,she->the", mixing, moved_heads, preferred_element_type=jnp.float32)
    outer = enter[:, :, None] * jnp.einsum("thd,hde->the", query_full, entering, precision=highest)
    attended = (inner + outer).astype(jnp.bfloat16).reshape(1, group, local_width)
    grad_scores = jnp.einsum(
        "the,she->hts", grad_heads, moved_heads, preferred_element_type=jnp.float32
    )
    grad_mixing = (grad_scores * table).astype(jnp.bfloat16)
    grad_query = jnp.einsum(
        "hts,shd->thd", grad_mixing, key_heads, preferred_element_type=jnp.float32
    )
    grad_query = grad_query + enter[:, :, None] * jnp.einsum(
        "the,hde->thd", grad_full, entering, precision=highest
    )
    grad_key = jnp.einsum(
        "hts,thd->shd", grad_mixing, query_heads, preferred_element_type=jnp.float32
    )
    grad_key = grad_key + leave[:, :, None] * jnp.einsum(
        "she,hde->shd", moved_full, leaving, precision=highest
    )
    grad_moved = jnp.einsum("hts,the->she", mixing, grad_heads, preferred_element_type=jnp.float32)
    grad_moved = grad_moved + leave[:, :, None] * jnp.einsum(
        "shd,hde->she", key_full, leaving, precision=highest
    )
    grad_moved = grad_moved.reshape(group, local_width)
    picked_grad = jnp.dot(select_full.T, grad_moved, precision=highest)
    code_grad = lax.psum(jnp.dot(picked_grad, rotated.T, precision=highest), "head")
    rotated_grad = jnp.dot(code.T, picked_grad, precision=highest) - jnp.dot(
        code_grad.T, picked, precision=highest
    )
    projected = lax.psum(jnp.dot(rotated_grad, refusal, precision=highest), "head")
    rotation_part = rotated_grad - jnp.dot(
        jnp.dot(projected, inverse, precision=highest), refusal.T, precision=highest
    )
    weight_part = jnp.dot(code_grad.T, picked, precision=highest)
    bias_part = jnp.sum(code_grad, axis=0)
    grad_weight, grad_bias, grad_rotation = lax.psum(
        (weight_part, bias_part, rotation_part), ("seq", "dp")
    )
    value_fix = jnp.dot(code_grad, proj_weight - rotated, precision=highest)
    grad_value = (
        (grad_moved + jnp.dot(select_full, value_fix, precision=highest))
        .astype(jnp.bfloat16)
        .reshape(1, group, local_width)
    )
    grad_query = grad_query.astype(jnp.bfloat16).reshape(1, group, local_width)
    grad_key = grad_key.astype(jnp.bfloat16).reshape(1, group, local_width)
    return (attended, grad_query, grad_key, grad_value, grad_rotation, grad_weight, grad_bias)


def solution(mesh):
    return jax.shard_map(
        shards,
        mesh=mesh,
        in_specs=(
            P("dp", "seq", "head"),
            P("dp", "seq", "head"),
            P("dp", "seq", "head"),
            P("dp", "seq", "head"),
            P("head"),
            P(None, "head"),
            P("head", None),
            P(None, "head"),
            P(),
            P("dp", None),
        ),
        out_specs=(
            P("dp", "seq", "head"),
            P("dp", "seq", "head"),
            P("dp", "seq", "head"),
            P("dp", "seq", "head"),
            P(None, "head"),
            P(None, "head"),
            P(),
        ),
        check_vma=False,
    )
```

profile of v0, /device:TPU:1, one launch (start us, length us, event | category | flops | bytes accessed | tf_op | source)
XLA Modules:
  0.0 1003.9 jit_solution(10857134564750874823)
XLA Ops:
  9.5 1.3 dynamic-slice
  12.3 1.5 fusion.20
  14.9 9.3 all-reduce.3
  27.4 123.5 %all-reduce = f32[512]{0:T(512)S(1)} all-reduce(f32[512]{0:T(512)S(1)} %get-tuple-element.328), channel_id=2, replica_groups=mesh['seq'=64,'head'=4,'dp'=2] {'seq'}, use_global_device_ids=true, to_apply=%add | all-reduce | flops 512 | bytes 4096
  153.6 1.4 maximum_bitcast_fusion
  156.7 1.2 fusion.30
  159.2 154.9 %all-gather.8.cloned.1.call-done = f32[512,128,128]{2,1,0:T(8,128)} async-done(((f32[8,128,128]{2,1,0:T(8,128)}), f32[512,128,128]{2,1,0:T(8,128)}) %all-gather.8.cloned.1.call-update) | async-done | bytes 33554448 | tf_op jit(solution)/shard_map/all_gather | solution.py:11
  314.1 78.5 %while.31 = (s32[]{:T(128)}, f32[8,128,128]{2,1,0:T(8,128)S(1)}, s32[]{:T(128)}, f32[64,8]{1,0:T(8,128)S(1)}, f32[64,8,128,128]{3,2,1,0:T(8,128)}, /*index=5*/s32[]{:T(128)}, s32[]{:T(128)}, s32[]{:T(128)}, s32[]{:T(128)}) while((s32[]{:T(128)}, f32[8,128,128]{2,1,0:T(8,128)S(1)}, s32[]{:T(128)}, f32[64,8]{1,0:T(8,128)S(1)}, ...), condition=%wide.region_6.7_spmd.clone, body=%wide.region_5.6_spmd.clone.sunk | while | flops 524296 | bytes 1573127 | solution.py:22
  315.3 1.2 fusion.114
  316.6 1.2 fusion.114
  317.8 1.2 fusion.114
  319.0 1.2 fusion.114
  320.2 1.2 fusion.114
  321.5 1.2 fusion.114
  322.7 1.2 fusion.114
  323.9 1.2 fusion.114
  325.1 1.2 fusion.114
  326.4 1.2 fusion.114
  327.6 1.2 fusion.114
  328.8 1.2 fusion.114
  330.1 1.2 fusion.114
  331.3 1.2 fusion.114
  332.5 1.2 fusion.114
  333.7 1.2 fusion.114
  335.0 1.2 fusion.114
  336.2 1.2 fusion.114
  337.4 1.2 fusion.114
  338.6 1.2 fusion.114
  339.9 1.2 fusion.114
  341.1 1.2 fusion.114
  342.3 1.2 fusion.114
  343.6 1.2 fusion.114
  344.8 1.2 fusion.114
  346.0 1.2 fusion.114
  347.2 1.2 fusion.114
  355.8 1.2 fusion.114
  362.0 1.2 fusion.114
  370.6 1.2 fusion.114
  379.1 1.2 fusion.114
  385.3 1.2 fusion.114
  394.7 8.5 all-reduce.2
  404.2 1.4 fusion.19
  405.6 1.2 fusion.23
  408.0 6.0 psum.60
  414.4 1.2 fusion.16
  418.4 494.9 %all-reduce.1 = (f32[4,1024]{1,0:T(4,128)}, f32[4,1024]{1,0:T(4,128)}, f32[4]{0:T(128)}) all-reduce(f32[4,1024]{1,0:T(4,128)S(1)} %convolution_subtract_fusion, f32[4,1024]{1,0:T(4,128)S(1)} %fusion.67, f32[4]{0:T(128)S(1)} %reduce_sum.9), channel_id=1, replica_groups=mesh['seq'=64,'head'=4,'dp'=2] {'seq','dp'}, use_global_device_ids=true, to_apply=%region_9.10 | all-reduce | flops 8196 | bytes 65568 | tf_op jit(solution)/shard_map/psum | solution.py:141
  914.3 1.8 fusion.18
  916.1 77.7 %while.30 = (s32[]{:T(128)}, f32[8,128,128]{2,1,0:T(8,128)S(1)}, s32[]{:T(128)}, f32[64,8]{1,0:T(8,128)S(1)}, f32[64,8,128,128]{3,2,1,0:T(8,128)}, /*index=5*/s32[]{:T(128)}, s32[]{:T(128)}) while((s32[]{:T(128)}, f32[8,128,128]{2,1,0:T(8,128)S(1)}, s32[]{:T(128)}, f32[64,8]{1,0:T(8,128)S(1)}, f32[64,8,128,128]{3,2,1,0:T(8,128)}, ...), condition=%wide.region_4.5_spmd.clone, body=%wide.region_3.4_spmd.clone.sunk | while | flops 524292 | bytes 1573065 | solution.py:22
  (289 shorter events, 134.7 us)
Async XLA Ops:
  7.2 6.7 copy-start
  7.2 306.9 %all-gather.8.cloned.1.call-start = ((), (), s32[]{:S(2)}) async-start(), calls=%async_computation.1 | async-start | bytes 34078720 | tf_op jit(solution)/shard_map/all_gather | solution.py:11
  12.2 301.9 %copy-start.5 = (f32[8]{0:T(128)}, f32[8]{0:T(128)S(1)}, u32[]{:S(2)}) copy-start(f32[8]{0:T(128)S(1)} %get-tuple-element.327) | copy-start | bytes 100
  13.8 902.3 %all-gather.6.cloned.1.call-start = ((), (), s32[]{:S(2)}) async-start(), calls=%async_computation | async-start | bytes 34078720 | tf_op jit(solution)/shard_map/all_gather | solution.py:11
  153.6 260.5 %copy-start.4 = (s32[128]{0:T(128)}, s32[128]{0:T(128)S(1)}, u32[]{:S(2)}) copy-start(s32[128]{0:T(128)S(1)} %iota_add_fusion) | copy-start | bytes 1540
  155.0 0.6 copy-start.6
  155.0 259.0 %copy-start.3 = (pred[128,128]{1,0:T(8,128)(4,1)}, pred[128,128]{1,0:T(8,128)(4,1)S(1)}, u32[]{:S(2)}) copy-start(pred[128,128]{1,0:T(8,128)(4,1)S(1)} %fusion.43) | copy-start | bytes 49156
  155.0 3.8 copy-start.1
  403.2 10.9 %copy-start.2 = (f32[16,4]{0,1:T(4,128)}, f32[16,4]{0,1:T(4,128)S(1)}, u32[]{:S(2)}) copy-start(f32[16,4]{0,1:T(4,128)S(1)} %get-tuple-element.316) | copy-start | bytes 772
Sparse Core Ops, SparseCore 0:
  13.9 300.1 all-gather.7
  406.9 291.9 all-gather.5
where the time goes:
time: 1020 us; the launch traced here: 1000 us
  blocking collectives  642 us (63%)
  waiting for transfers between devices  155 us (15%)
  other arithmetic  153 us (15%)
  matrix products  20.5 us (2%)
  between operations  18.9 us (2%)
    psum x1, blocking collectives, shards(): lax.psum((weight_part, bias_part, rotation_part), ('seq', 'dp'))  495 us
    all_gather x2, waiting for transfers between devices, carried_in(): everything = jax.tree.map(lambda part: lax.all_gather(part, axis), x)  155 us
    select_n x128, other arithmetic, lap(): return jax.tree.map(lambda a, b: jnp.where(reached, a, b), new, before)  150 us
    unnamed x1, blocking collectives  124 us
  transfers between devices with their start and end apart: 2, of which 1 were waited for; matrix products, arithmetic and copies ran while one was open for 2% of the time, Pallas kernels for 0%

commit v1 on v0

v1 whole, which is shorter than its diff:
```python
import functools
import jax
import jax.numpy as jnp
from jax import lax
from jax.experimental import pallas as pl
from jax.experimental.pallas import tpu as pltpu
from jax.sharding import Mesh, PartitionSpec as P

highest = lax.Precision.HIGHEST
f32, bf16 = jnp.float32, jnp.bfloat16
BLOCK = 128
HEADS = 8
SIZE = 128
WIDE = HEADS * SIZE
NPOS = 16
NEAR = ("zl", "y")
SMEM = pl.BlockSpec(memory_space=pltpu.SMEM)
VMEM = pl.BlockSpec(memory_space=pltpu.VMEM)


def nn(a, b):
    return lax.dot_general(a, b, (((1,), (0,)), ((), ())), preferred_element_type=f32)


def nt(a, b):
    return lax.dot_general(a, b, (((1,), (1,)), ((), ())), preferred_element_type=f32)


def tn(a, b):
    return lax.dot_general(a, b, (((0,), (0,)), ((), ())), preferred_element_type=f32)


def full_nt(a, b):
    return lax.dot_general(
        a, b, (((1,), (1,)), ((), ())), preferred_element_type=f32, precision=highest
    )


def full_tn(a, b):
    return lax.dot_general(
        a, b, (((0,), (0,)), ((), ())), preferred_element_type=f32, precision=highest
    )


def split(x):
    high = x.astype(bf16)
    return high, (x - high.astype(f32)).astype(bf16)


def log_keep(rate):
    total = jnp.float32(1.0 / 8.0)
    for n in range(7, 0, -1):
        total = total * rate + jnp.float32(1.0 / n)
    return -rate * total


def powers(rate, exponents):
    return jnp.exp(exponents * log_keep(rate))


def rows_iota(shape=(BLOCK, SIZE)):
    return lax.broadcasted_iota(jnp.int32, shape, 0)


def cols_iota(shape=(BLOCK, SIZE)):
    return lax.broadcasted_iota(jnp.int32, shape, 1)


def selector(positions, start):
    row = rows_iota((NPOS, BLOCK))
    place = cols_iota((NPOS, BLOCK)) + start
    wanted = jnp.full((NPOS, BLOCK), -1, jnp.int32)
    for j in range(NPOS):
        wanted = jnp.where(row == j, positions[0, j], wanted)
    return (wanted == place).astype(f32)


def head_cols(h):
    return slice(h * SIZE, (h + 1) * SIZE)


def decayed_state(weighted, other):
    high, low = split(weighted)
    return tn(other, high) + tn(other, low)


def query_state(meta, rate, positions, q, grad, v, rot, ref, proj, state, small, picked):
    offset = rows_iota().astype(f32)
    for h in range(HEADS):
        c = head_cols(h)
        weighted = q[:, c].astype(f32) * powers(rate[h], offset)
        out = decayed_state(weighted, grad[:, c])
        state[2 * h] = out[:64]
        state[2 * h + 1] = out[64:]
    select = selector(positions, meta[0])
    chosen = nn(select.astype(bf16), v[...])
    picked[...] = chosen
    left = jnp.concatenate([chosen, ref[...], rot[...], jnp.zeros((2, WIDE), f32)], axis=0)
    right = jnp.concatenate(
        [proj[...] - rot[...], ref[...], rot[...], jnp.zeros((6, WIDE), f32)], axis=0
    )
    small[...] = jnp.zeros((24, 128), f32)
    small[:, 0:16] = full_nt(left, right)


def inverse_of(small):
    g00, g01 = small[16:17, 4:5], small[16:17, 5:6]
    g10, g11 = small[17:18, 4:5], small[17:18, 5:6]
    det = g00 * g11 - g01 * g10
    return g11 / det, -g01 / det, -g10 / det, g00 / det


def key_state(meta, rate, positions, small, v, k, rot, ref, bias, moved, state, basis, code):
    i00, i01, i10, i11 = inverse_of(small)
    c0, c1 = small[18:22, 4:5], small[18:22, 5:6]
    rotated = (
        rot[...]
        - (c0 * i00 + c1 * i10) * ref[0:1, :]
        - (c0 * i01 + c1 * i11) * ref[1:2, :]
    )
    basis[...] = jnp.concatenate([rotated, ref[...], jnp.zeros((2, WIDE), f32)], axis=0)
    turned = pltpu.roll(small[16:24, :], 122, 1)
    t0, t1 = turned[0:1], turned[1:2]
    full = (
        small[0:16, :]
        + bias[...]
        + small[0:16, 4:5] * (t0 * i00 + t1 * i10)
        + small[0:16, 5:6] * (t0 * i01 + t1 * i11)
    )
    full = jnp.where(cols_iota((NPOS, 128)) < 4, full, 0.0)
    code[...] = full
    shift = jnp.zeros((NPOS, WIDE), f32)
    for r in range(4):
        shift = shift + full[:, r : r + 1] * rotated[r : r + 1, :]
    select = selector(positions, meta[0])
    offset = rows_iota().astype(f32)
    for h in range(HEADS):
        c = head_cols(h)
        new = (v[:, c].astype(f32) + full_tn(select, shift[:, c])).astype(bf16)
        moved[:, c] = new
        weighted = k[:, c].astype(f32) * powers(rate[h], BLOCK - 1.0 - offset)
        out = decayed_state(weighted, new)
        state[2 * h] = out[:64]
        state[2 * h + 1] = out[64:]


def inside(rate, q, k, moved, grad, attended, grad_q, grad_k, grad_m):
    between = rows_iota() - cols_iota()
    lower = between >= 0
    distance = jnp.maximum(between, 0).astype(f32)
    for h in range(HEADS):
        c = head_cols(h)
        table = jnp.where(lower, powers(rate[h], distance), 0.0)
        qh, kh, mh, gh = q[:, c], k[:, c], moved[:, c], grad[:, c]
        mixing = (nt(qh, kh) * table).astype(bf16)
        grad_mixing = (nt(gh, mh) * table).astype(bf16)
        attended[:, c] = nn(mixing, mh)
        grad_q[:, c] = nn(grad_mixing, kh)
        grad_k[:, c] = tn(grad_mixing, qh)
        grad_m[:, c] = tn(mixing, gh)


def group_totals(meta, rate, later, earlier, out):
    far, near = meta[1], meta[2]
    keep = powers(rate[near // 2], jnp.full((64, 128), float(BLOCK), f32))
    forward = earlier[0]
    backward = later[15]
    for b in range(1, 16):
        forward = forward * keep + earlier[b]
        backward = backward * keep + later[15 - b]
    for z in range(4):
        out[z] = jnp.where(far < z, forward, backward)


def carried(meta, rate, later, earlier, others, leaving, entering):
    far, near = meta[1], meta[2]
    exponent = jnp.full((64, 128), float(BLOCK), f32)
    keep = powers(rate[near // 2], exponent)
    keep_group = powers(rate[near // 2], exponent * 16.0)
    forward = jnp.zeros((64, 128), f32)
    backward = jnp.zeros((64, 128), f32)
    for z in range(3):
        forward = jnp.where(far > z, forward * keep_group + others[z], forward)
        backward = jnp.where(far < 3 - z, backward * keep_group + others[3 - z], backward)
    for b in range(16):
        entering[b] = forward
        forward = forward * keep + earlier[b]
        leaving[15 - b] = backward
        backward = backward * keep + later[15 - b]


def backward_rest(
    meta, rate, positions, k, moved, state, grad_k_in, grad_m_in, basis, grad_k, grad_m, picked, small
):
    offset = rows_iota().astype(f32)
    select = selector(positions, meta[0])
    for h in range(HEADS):
        c = head_cols(h)
        leave = powers(rate[h], BLOCK - offset)
        high, low = split(jnp.concatenate([state[2 * h], state[2 * h + 1]], axis=0))
        mh, kh = moved[:, c], k[:, c]
        grad_k[:, c] = (grad_k_in[:, c] + leave * (nn(mh, high) + nn(mh, low))).astype(bf16)
        out = grad_m_in[:, c] + leave * (nt(kh, high) + nt(kh, low))
        grad_m[:, c] = out
        picked[:, c] = lax.dot_general(
            select, out, (((1,), (0,)), ((), ())), preferred_element_type=f32, precision=highest
        )
    small[...] = jnp.zeros((NPOS, 128), f32)
    small[:, 0:8] = full_nt(picked[...], basis[...])


def forward_rest(rate, q, grad, state, attended_in, grad_q_in, attended, grad_q):
    offset = rows_iota().astype(f32)
    for h in range(HEADS):
        c = head_cols(h)
        enter = powers(rate[h], offset + 1.0)
        high, low = split(jnp.concatenate([state[2 * h], state[2 * h + 1]], axis=0))
        qh, gh = q[:, c], grad[:, c]
        attended[:, c] = (attended_in[:, c] + enter * (nt(qh, high) + nt(qh, low))).astype(bf16)
        grad_q[:, c] = (grad_q_in[:, c] + enter * (nn(gh, high) + nn(gh, low))).astype(bf16)


def value_rest(
    meta, positions, small_grad, small, code, picked, picked_grad, grad_m, proj, basis, grad_v, parts
):
    code_grad = jnp.where(cols_iota((NPOS, 128)) < 4, small_grad[...], 0.0)
    lift = proj[...] - basis[0:4, :]
    fix = jnp.zeros((NPOS, WIDE), f32)
    for r in range(4):
        fix = fix + code_grad[:, r : r + 1] * lift[r : r + 1, :]
    select = selector(positions, meta[0])
    for h in range(HEADS):
        c = head_cols(h)
        grad_v[:, c] = (grad_m[:, c] + full_tn(select, fix[:, c])).astype(bf16)
    weight = full_tn(code_grad, picked[...])
    turn = full_tn(code[...], picked_grad[...])
    along = full_tn(code[...], small_grad[...]) - full_tn(code_grad, small[0:16, :])
    bias = full_tn(code_grad, jnp.ones((NPOS, 128), f32))
    lane = cols_iota((4, 128))
    extra = jnp.where(lane < 4, bias[0:4], along[0:4])
    for i in range(8):
        c = head_cols(i)
        parts[i] = jnp.concatenate([weight[0:4, c], extra], axis=0)
        parts[8 + i] = jnp.concatenate([turn[0:4, c], extra], axis=0)


def finish(small, ref, parts, grad_rotation, grad_weight, grad_bias):
    i00, i01, i10, i11 = inverse_of(small)
    extra = parts[0]
    a0, a1 = extra[4:8, 4:5], extra[4:8, 5:6]
    b0 = a0 * i00 + a1 * i10
    b1 = a0 * i01 + a1 * i11
    for i in range(8):
        c = head_cols(i)
        weight = parts[i][0:4]
        grad_weight[:, c] = weight
        grad_rotation[:, c] = (
            parts[8 + i][0:4] - weight - b0 * ref[0:1, c] - b1 * ref[1:2, c]
        )
    grad_bias[...] = extra[4:8, :]


def call(kernel, specs, outs, flops=1e8, bytes_accessed=2e6):
    return pl.pallas_call(
        kernel,
        in_specs=[SMEM if s == "s" else VMEM for s in specs],
        out_specs=[VMEM] * len(outs),
        out_shape=[jax.ShapeDtypeStruct(s, d) for s, d in outs],
        compiler_params=pltpu.CompilerParams(vmem_limit_bytes=40 * 1024 * 1024),
        cost_estimate=pl.CostEstimate(
            flops=int(flops), bytes_accessed=int(bytes_accessed), transcendentals=0
        ),
    )


def swap(x, axes):
    return lax.all_to_all(x, axes, 0, 0, tiled=False)


def shards(queries, key_rows, values, out_grad, rate, rotation, refusal, proj_weight, proj_bias, positions):
    q, k, v, grad = queries[0], key_rows[0], values[0], out_grad[0]
    ref = refusal.T
    far, near = lax.axis_index("zh"), lax.axis_index(NEAR)
    meta = jnp.stack([(far * 16 + near) * BLOCK, far, near]).astype(jnp.int32)
    bias = jnp.pad(proj_bias, (0, 124))[None, :]
    rows = (BLOCK, WIDE)
    pieces = (16, 64, 128)

    grad_state, small, picked = call(
        query_state, "sssvvvvvv", [(pieces, f32), ((24, 128), f32), ((NPOS, WIDE), f32)]
    )(meta, rate, positions, q, grad, v, rotation, ref, proj_weight)
    grad_pieces = swap(grad_state, NEAR)
    small = lax.psum(small, "head")
    moved, state, basis, code = call(
        key_state,
        "sssvvvvvv",
        [(rows, bf16), (pieces, f32), ((8, WIDE), f32), ((NPOS, 128), f32)],
    )(meta, rate, positions, small, v, k, rotation, ref, bias)
    pieces_in = swap(state, NEAR)
    attended_in, grad_q_in, grad_k_in, grad_m_in = call(inside, "svvvv", [(rows, f32)] * 4)(
        rate, q, k, moved, grad
    )
    (totals,) = call(group_totals, "ssvv", [((4, 64, 128), f32)])(meta, rate, grad_pieces, pieces_in)
    others = swap(totals, "zh")
    leaving, entering = call(carried, "ssvvv", [(pieces, f32)] * 2)(
        meta, rate, grad_pieces, pieces_in, others
    )
    leaving = swap(leaving, NEAR)
    grad_k, grad_m, picked_grad, small_grad = call(
        backward_rest,
        "sssvvvvvv",
        [(rows, bf16), (rows, f32), ((NPOS, WIDE), f32), ((NPOS, 128), f32)],
    )(meta, rate, positions, k, moved, leaving, grad_k_in, grad_m_in, basis)
    entering = swap(entering, NEAR)
    small_grad = lax.psum(small_grad, "head")
    grad_v, parts = call(value_rest, "ssvvvvvvvv", [(rows, bf16), ((16, 8, 128), f32)])(
        meta, positions, small_grad, small, code, picked, picked_grad, grad_m, proj_weight, basis
    )
    part = jnp.sum(swap(parts, NEAR), axis=0)
    attended, grad_q = call(forward_rest, "svvvvv", [(rows, bf16)] * 2)(
        rate, q, grad, entering, attended_in, grad_q_in
    )
    part = lax.psum(lax.psum(part, "zh"), "dp")
    parts = swap(jnp.broadcast_to(part[None], (16, 8, 128)), NEAR)
    grad_rotation, grad_weight, grad_bias = call(
        finish, "vvv", [((4, WIDE), f32), ((4, WIDE), f32), ((4, 128), f32)]
    )(small, ref, parts)
    return (
        attended[None],
        grad_q[None],
        grad_k[None],
        grad_v[None],
        grad_rotation,
        grad_weight,
        grad_bias[:, 0],
    )


def solution(mesh):
    own = Mesh(mesh.devices.reshape(4, 4, 4, 4, 2), ("zh", "zl", "y", "head", "dp"))
    seq = ("zh", "zl", "y")
    stream = P("dp", seq, "head")
    return jax.shard_map(
        shards,
        mesh=own,
        in_specs=(
            stream,
            stream,
            stream,
            stream,
            P("head"),
            P(None, "head"),
            P("head", None),
            P(None, "head"),
            P(),
            P("dp", None),
        ),
        out_specs=(stream, stream, stream, stream, P(None, "head"), P(None, "head"), P()),
        check_vma=False,
    )
```

time: 1020 us -> 165 us (0.16); the launches traced: 1000 us -> 164 us
  blocking collectives: 642 us -> 98.6 us
  other arithmetic: 153 us -> 0.1 us
  waiting for transfers between devices: 155 us -> 12.3 us
  starting transfers between devices: 0.08 us -> 26 us
  matrix products: 20.5 us -> 0 us
  between operations: 18.9 us -> 0.81 us
  Pallas kernels: 0 us -> 17.9 us
    psum x4, blocking collectives: 519 us -> 46.2 us  [the longest x2 24.7 us: shards(): part = lax.psum(lax.psum(part, 'zh'), 'dp')]
    all_gather x2 -> x0, waiting for transfers between devices: 155 us -> none  [carried_in(): everything = jax.tree.map(lambda part: lax.all_gather(part, axis), x)]
    select_n x128 -> x0, other arithmetic: 150 us -> none  [lap(): return jax.tree.map(lambda a, b: jnp.where(reached, a, b), new, before)]
    unnamed x1 -> x0, blocking collectives: 124 us -> none
    all_to_all x0 -> x3, blocking collectives: none -> 52.4 us  [swap(): return lax.all_to_all(x, axes, 0, 0, tiled=False)]
    all_to_all x0 -> x4, starting transfers between devices: none -> 26 us  [swap(): return lax.all_to_all(x, axes, 0, 0, tiled=False)]
    dot_general x29 -> x0, matrix products: 20.5 us -> none  [the longest x1 1.79 us: shards(): jnp.dot(select_full, value_fix, precision=highest)]
    pallas_call x0 -> x9, Pallas kernels: none -> 17.9 us  [the longest x1 3.38 us: shards(): call(key_state, 'sssvvvvvv', [(rows, bf16), (pieces, f32), ((8, WIDE), f3...]
  transfers between devices with their start and end apart: 2 -> 4, of which waited for: 1 -> 2; matrix products, arithmetic and copies ran while one was open for 2% -> 0% of each run, Pallas kernels for 0% -> 5%
where the time goes in v1:
time: 165 us; the launch traced here: 164 us
  blocking collectives  98.6 us (60%)
  starting transfers between devices  26 us (16%)
  Pallas kernels  17.9 us (11%)
  waiting for transfers between devices  12.3 us (7%)
  local copies, waits for them, and re-layouts  8.5 us (5%)
    all_to_all x3, blocking collectives, swap(): return lax.all_to_all(x, axes, 0, 0, tiled=False)  52.4 us
    all_to_all x4, starting transfers between devices, swap(): return lax.all_to_all(x, axes, 0, 0, tiled=False)  26 us
    psum x2, blocking collectives, shards(): part = lax.psum(lax.psum(part, 'zh'), 'dp')  24.7 us
    psum x1, blocking collectives, shards(): small = lax.psum(small, 'head')  14 us
    all_to_all x4, waiting for transfers between devices, swap(): return lax.all_to_all(x, axes, 0, 0, tiled=False)  12.3 us
    psum x1, blocking collectives, shards(): small_grad = lax.psum(small_grad, 'head')  7.54 us
    unnamed x34, local copies, waits for them, and re-layouts  7.25 us
    pallas_call x1, Pallas kernels, shards(): call(key_state, 'sssvvvvvv', [(rows, bf16), (pieces, f32), ((8, WIDE), f3...  3.38 us
  transfers between devices with their start and end apart: 4, of which 2 were waited for; matrix products, arithmetic and copies ran while one was open for 0% of the time, Pallas kernels for 5%

profile of v1, /device:TPU:1, one launch (start us, length us, event | category | flops | bytes accessed | tf_op | source)
XLA Modules:
  0.0 164.2 jit_solution(15223599498103514729)
XLA Ops:
  0.6 0.0 copy-start.13
  0.6 0.0 copy-start.14
  0.7 0.0 copy-start.15
  0.7 0.0 copy-start.11
  0.7 0.0 copy-start.12
  0.7 0.1 pad_add_fusion.meta
  0.8 0.6 copy-done.13
  1.3 0.0 copy-done.14
  1.3 0.0 copy-done.15
  1.3 0.1 copy-done.11
  1.4 0.0 copy-done.12
  1.4 0.9 copy-done.1
  2.4 0.9 copy-done.3
  3.3 0.9 copy-done.5
  4.3 1.7 %shard_map.153 = (f32[16,64,128]{2,1,0:T(8,128)}, f32[24,128]{1,0:T(8,128)S(1)}, f32[16,1024]{1,0:T(8,128)S(1)}) custom-call(s32[3]{0:T(128)S(1)} %pad_add_fusion.meta, f32[8]{0:T(128)S(1)} %copy-done.14, s32[1,16]{1,0:T(1,128)S(1)} %copy-done.15, bf16[128,1024]{1,0:T(8,128)(2,1)S(1)} %bitcast.17, bf16[128,1024]{1,0:T(8,128)(2,1)S(1)} %bitcast.20, ...), custom_call_target="tpu_custom_call" | custom-call | flops 100000000 | bytes 2000000 | tf_op jit(solution)/shard_map/pallas_call | solution.py:289
  6.0 9.3 %all-to-all-start = ((f32[16,64,128]{2,1,0:T(8,128)}), f32[16,64,128]{2,1,0:T(8,128)S(1)}, u32[]{:S(2)}, u32[]{:S(2)}) async-start(f32[16,64,128]{2,1,0:T(8,128)} %get-tuple-element.31), calls=%async_computation | async-start | bytes 1048576 | tf_op jit(solution)/shard_map/all_to_all | solution.py:277
  15.3 0.0 copy-start.16
  15.3 14.0 %psum.28.small = f32[24,128]{1,0:T(8,128)S(1)} all-reduce(f32[24,128]{1,0:T(8,128)S(1)} %get-tuple-element.32), channel_id=1, replica_groups=mesh['zh'=4,'zl'=4,'y'=4,'head'=4,'dp'=2] {'head'}, use_global_device_ids=true, to_apply=%region_0.1 | all-reduce | flops 3072 | bytes 24576 | tf_op jit(solution)/shard_map/psum | solution.py:293
  29.3 0.0 copy-done.16
  29.3 0.0 copy-done
  29.3 0.0 copy-done.6
  29.3 3.4 %shard_map.154 = (bf16[128,1024]{1,0:T(8,128)(2,1)S(1)}, f32[16,64,128]{2,1,0:T(8,128)S(1)}, f32[8,1024]{1,0:T(8,128)S(1)}, f32[16,128]{1,0:T(8,128)S(1)}) custom-call(s32[3]{0:T(128)S(1)} %pad_add_fusion.meta, f32[8]{0:T(128)S(1)} %copy-done.14, s32[1,16]{1,0:T(1,128)S(1)} %copy-done.15, f32[24,128]{1,0:T(8,128)S(1)} %psum.28.small, ...), custom_call_target="tpu_custom_call" | custom-call | flops 100000000 | bytes 2000000 | tf_op jit(solution)/shard_map/pallas_call | solution.py:294
  32.7 0.0 all-to-all-done.later
  32.7 17.5 %all_to_all.35.earlier = f32[16,64,128]{2,1,0:T(8,128)S(1)} all-to-all(f32[16,64,128]{2,1,0:T(8,128)S(1)} %get-tuple-element.33), channel_id=1, replica_groups=mesh['zh'=4,'zl'=4,'y'=4,'head'=4,'dp'=2] {'zl','y'}, dimensions={0} | all-to-all | bytes 1048576 | tf_op jit(solution)/shard_map/all_to_all | solution.py:277
  50.2 0.7 shard_map.155
  50.9 24.8 %all_to_all.36.others = f32[4,64,128]{2,1,0:T(8,128)S(1)} all-to-all(f32[4,64,128]{2,1,0:T(8,128)S(1)} %shard_map.155), channel_id=1, replica_groups=mesh['zh'=4,'zl'=4,'y'=4,'head'=4,'dp'=2] {'zh'}, dimensions={0} | all-to-all | bytes 262144 | tf_op jit(solution)/shard_map/all_to_all | solution.py:277
  75.7 1.7 %shard_map.156 = (f32[16,64,128]{2,1,0:T(8,128)}, f32[16,64,128]{2,1,0:T(8,128)}) custom-call(s32[3]{0:T(128)S(1)} %pad_add_fusion.meta, f32[8]{0:T(128)S(1)} %copy-done.14, f32[16,64,128]{2,1,0:T(8,128)S(1)} %all-to-all-done.later, f32[16,64,128]{2,1,0:T(8,128)S(1)} %all_to_all.35.earlier, f32[4,64,128]{2,1,0:T(8,128)S(1)} %all_to_all.36.others), custom_call_target="tpu_custom_call" | custom-call | flops 100000000 | bytes 2000000 | tf_op jit(solution)/shard_map/pallas_call | solution.py:305
  77.3 3.9 %all-to-all-start.4 = ((f32[16,64,128]{2,1,0:T(8,128)}), f32[16,64,128]{2,1,0:T(8,128)S(1)}, u32[]{:S(2)}, u32[]{:S(2)}) async-start(f32[16,64,128]{2,1,0:T(8,128)} %get-tuple-element.40), calls=%async_computation.4 | async-start | bytes 1048576 | tf_op jit(solution)/shard_map/all_to_all | solution.py:277
  81.3 2.5 %shard_map.157 = (f32[128,1024]{1,0:T(8,128)S(1)}, f32[128,1024]{1,0:T(8,128)S(1)}, f32[128,1024]{1,0:T(8,128)S(1)}, f32[128,1024]{1,0:T(8,128)S(1)}) custom-call(f32[8]{0:T(128)S(1)} %copy-done.14, bf16[128,1024]{1,0:T(8,128)(2,1)S(1)} %bitcast.18, bf16[128,1024]{1,0:T(8,128)(2,1)S(1)} %bitcast.15, bf16[128,1024]{1,0:T(8,128)(2,1)S(1)} %get-tuple-element.35.moved, ...), custom_call_target="tpu_custom_call" | custom-call | flops 100000000 | bytes 2000000 | tf_op jit(solution)/shard_map/pallas_call | solution.py:300
  83.8 0.8 copy-done.7
  84.6 0.8 copy-done.9
  85.4 7.0 %all-to-all-done.4.state = f32[16,64,128]{2,1,0:T(8,128)S(1)} async-done(((f32[16,64,128]{2,1,0:T(8,128)}), f32[16,64,128]{2,1,0:T(8,128)S(1)}, u32[]{:S(2)}, u32[]{:S(2)}) %all-to-all-start.4) | async-done | bytes 524320 | tf_op jit(solution)/shard_map/all_to_all | solution.py:277
  92.4 1.0 copy-done.8
  93.5 1.0 copy-done.10
  94.5 2.5 %shard_map.159 = (bf16[128,1024]{1,0:T(8,128)(2,1)}, f32[128,1024]{1,0:T(8,128)S(1)}, f32[16,1024]{1,0:T(8,128)S(1)}, f32[16,128]{1,0:T(8,128)S(1)}) custom-call(s32[3]{0:T(128)S(1)} %pad_add_fusion.meta, f32[8]{0:T(128)S(1)} %copy-done.14, s32[1,16]{1,0:T(1,128)S(1)} %copy-done.15, bf16[128,1024]{1,0:T(8,128)(2,1)S(1)} %bitcast.16, ...), custom_call_target="tpu_custom_call" | custom-call | flops 100000000 | bytes 2000000 | tf_op jit(solution)/shard_map/pallas_call | solution.py:309
  97.0 7.5 %psum.29.small_grad = f32[16,128]{1,0:T(8,128)S(1)} all-reduce(f32[16,128]{1,0:T(8,128)S(1)} %get-tuple-element.45), channel_id=1, replica_groups=mesh['zh'=4,'zl'=4,'y'=4,'head'=4,'dp'=2] {'head'}, use_global_device_ids=true, to_apply=%region_1.2 | all-reduce | flops 2048 | bytes 16384 | tf_op jit(solution)/shard_map/psum | solution.py:315
  104.5 2.6 %shard_map.160 = (bf16[128,1024]{1,0:T(8,128)(2,1)}, f32[16,8,128]{2,1,0:T(8,128)S(1)}) custom-call(s32[3]{0:T(128)S(1)} %pad_add_fusion.meta, s32[1,16]{1,0:T(1,128)S(1)} %copy-done.15, f32[16,128]{1,0:T(8,128)S(1)} %psum.29.small_grad, f32[24,128]{1,0:T(8,128)S(1)} %psum.28.small, f32[16,128]{1,0:T(8,128)S(1)} %get-tuple-element.46.code, ...), custom_call_target="tpu_custom_call" | custom-call | flops 100000000 | bytes 2000000 | tf_op jit(solution)/shard_map/pallas_call | solution.py:316
  107.1 10.2 %all_to_all.37 = f32[16,8,128]{2,1,0:T(8,128)S(1)} all-to-all(f32[16,8,128]{2,1,0:T(8,128)S(1)} %get-tuple-element.51), channel_id=1, replica_groups=mesh['zh'=4,'zl'=4,'y'=4,'head'=4,'dp'=2] {'zl','y'}, dimensions={0} | all-to-all | bytes 131072 | tf_op jit(solution)/shard_map/all_to_all | solution.py:277
  117.3 3.6 %all-to-all-start.3 = ((f32[16,64,128]{2,1,0:T(8,128)}), f32[16,64,128]{2,1,0:T(8,128)S(1)}, u32[]{:S(2)}, u32[]{:S(2)}) async-start(f32[16,64,128]{2,1,0:T(8,128)} %get-tuple-element.34), calls=%async_computation.3 | async-start | bytes 1048576 | tf_op jit(solution)/shard_map/all_to_all | solution.py:277
  120.9 9.8 %psum.30 = f32[8,128]{1,0:T(8,128)S(1)} all-reduce(f32[8,128]{1,0:T(8,128)S(1)} %reduce_sum.9), channel_id=1, replica_groups=mesh['zh'=4,'zl'=4,'y'=4,'head'=4,'dp'=2] {'zh'}, use_global_device_ids=true, to_apply=%region_3.4 | all-reduce | flops 1024 | bytes 8192 | tf_op jit(solution)/shard_map/psum | solution.py:323
  130.7 14.9 %psum.31 = f32[8,128]{1,0:T(8,128)S(1)} all-reduce(f32[8,128]{1,0:T(8,128)S(1)} %psum.30), channel_id=1, replica_groups=mesh['zh'=4,'zl'=4,'y'=4,'head'=4,'dp'=2] {'dp'}, use_global_device_ids=true, to_apply=%region_4.5 | all-reduce | flops 1024 | bytes 8192 | tf_op jit(solution)/shard_map/psum | solution.py:323
  145.5 0.0 all-to-all-done.3.state
  145.6 0.6 broadcast_in_dim.26
  146.2 9.2 %all-to-all-start.6 = ((f32[16,8,128]{2,1,0:T(8,128)}), f32[16,8,128]{2,1,0:T(8,128)S(1)}, u32[]{:S(2)}, u32[]{:S(2)}) async-start(f32[16,8,128]{2,1,0:T(8,128)} %broadcast_in_dim.26), calls=%async_computation.6 | async-start | bytes 131072 | tf_op jit(solution)/shard_map/all_to_all | solution.py:277
  155.4 2.0 %shard_map.158 = (bf16[128,1024]{1,0:T(8,128)(2,1)}, bf16[128,1024]{1,0:T(8,128)(2,1)}) custom-call(f32[8]{0:T(128)S(1)} %copy-done.14, bf16[128,1024]{1,0:T(8,128)(2,1)S(1)} %bitcast.19, bf16[128,1024]{1,0:T(8,128)(2,1)S(1)} %bitcast.22, f32[16,64,128]{2,1,0:T(8,128)S(1)} %all-to-all-done.3.state, f32[128,1024]{1,0:T(8,128)S(1)} %get-tuple-element.36.attended_in, ...), custom_call_target="tpu_custom_call" | custom-call | flops 100000000 | bytes 2000000 | tf_op jit(solution)/shard_map/pallas_call | solution.py:320
  157.3 5.3 %all-to-all-done.6.parts = f32[16,8,128]{2,1,0:T(8,128)S(1)} async-done(((f32[16,8,128]{2,1,0:T(8,128)}), f32[16,8,128]{2,1,0:T(8,128)S(1)}, u32[]{:S(2)}, u32[]{:S(2)}) %all-to-all-start.6) | async-done | bytes 65568 | tf_op jit(solution)/shard_map/all_to_all | solution.py:277
  162.6 1.0 shard_map.161
  163.6 0.6 slice_reduce_fusion
  (15 shorter events, 0.0 us)
Async XLA Ops:
  0.6 0.7 copy-start.13
  0.6 0.7 copy-start.14
  0.7 0.7 copy-start.15
  0.7 0.7 copy-start.11
  0.7 0.7 copy-start.12
  1.4 0.9 copy-start.1
  2.4 0.9 copy-start.3
  3.3 0.9 copy-start.5
  6.0 23.3 %copy-start = (bf16[1,128,1024]{2,1,0:T(8,128)(2,1)S(1)}, bf16[1,128,1024]{2,1,0:T(8,128)(2,1)}, u32[]{:S(2)}) copy-start(bf16[1,128,1024]{2,1,0:T(8,128)(2,1)} %param.11) | copy-start | bytes 786436
  6.0 23.3 %copy-start.6 = (bf16[1,128,1024]{2,1,0:T(8,128)(2,1)S(1)}, bf16[1,128,1024]{2,1,0:T(8,128)(2,1)}, u32[]{:S(2)}) copy-start(bf16[1,128,1024]{2,1,0:T(8,128)(2,1)} %param.12) | copy-start | bytes 786436
  6.0 26.7 %all-to-all-start = ((f32[16,64,128]{2,1,0:T(8,128)}), f32[16,64,128]{2,1,0:T(8,128)S(1)}, u32[]{:S(2)}, u32[]{:S(2)}) async-start(f32[16,64,128]{2,1,0:T(8,128)} %get-tuple-element.31), calls=%async_computation | async-start | bytes 1048576 | tf_op jit(solution)/shard_map/all_to_all | solution.py:277
  15.3 14.0 %copy-start.16 = (f32[4]{0:T(128)S(1)}, f32[4]{0:T(128)}, u32[]{:S(2)}) copy-start(f32[4]{0:T(128)} %param.18) | copy-start | bytes 52
  77.3 3.9 %copy-start.2 = (bf16[1,128,1024]{2,1,0:T(8,128)(2,1)S(1)}, bf16[1,128,1024]{2,1,0:T(8,128)(2,1)}, u32[]{:S(2)}) copy-start(bf16[1,128,1024]{2,1,0:T(8,128)(2,1)} %param.10) | copy-start | bytes 786436
  77.3 4.0 %copy-start.4 = (bf16[1,128,1024]{2,1,0:T(8,128)(2,1)S(1)}, bf16[1,128,1024]{2,1,0:T(8,128)(2,1)}, u32[]{:S(2)}) copy-start(bf16[1,128,1024]{2,1,0:T(8,128)(2,1)} %param.13) | copy-start | bytes 786436
  77.3 15.1 %all-to-all-start.4 = ((f32[16,64,128]{2,1,0:T(8,128)}), f32[16,64,128]{2,1,0:T(8,128)S(1)}, u32[]{:S(2)}, u32[]{:S(2)}) async-start(f32[16,64,128]{2,1,0:T(8,128)} %get-tuple-element.40), calls=%async_computation.4 | async-start | bytes 1048576 | tf_op jit(solution)/shard_map/all_to_all | solution.py:277
  83.8 0.8 copy-start.7
  84.6 0.8 copy-start.9
  92.4 1.0 copy-start.8
  93.4 1.0 copy-start.10
  117.3 28.3 %all-to-all-start.3 = ((f32[16,64,128]{2,1,0:T(8,128)}), f32[16,64,128]{2,1,0:T(8,128)S(1)}, u32[]{:S(2)}, u32[]{:S(2)}) async-start(f32[16,64,128]{2,1,0:T(8,128)} %get-tuple-element.34), calls=%async_computation.3 | async-start | bytes 1048576 | tf_op jit(solution)/shard_map/all_to_all | solution.py:277
  146.2 16.5 %all-to-all-start.6 = ((f32[16,8,128]{2,1,0:T(8,128)}), f32[16,8,128]{2,1,0:T(8,128)S(1)}, u32[]{:S(2)}, u32[]{:S(2)}) async-start(f32[16,8,128]{2,1,0:T(8,128)} %broadcast_in_dim.26), calls=%async_computation.6 | async-start | bytes 131072 | tf_op jit(solution)/shard_map/all_to_all | solution.py:277

commit v2 on v1

v2 whole, which is shorter than its diff:
```python
import functools
import jax
import jax.numpy as jnp
from jax import lax
from jax.experimental import pallas as pl
from jax.experimental.pallas import tpu as pltpu
from jax.sharding import Mesh, PartitionSpec as P

highest = lax.Precision.HIGHEST
f32, bf16 = jnp.float32, jnp.bfloat16
BLOCK = 128
HEADS = 8
SIZE = 128
WIDE = HEADS * SIZE
NPOS = 16
NEAR = ("zl", "y")
SMEM = pl.BlockSpec(memory_space=pltpu.SMEM)
VMEM = pl.BlockSpec(memory_space=pltpu.VMEM)


def nn(a, b):
    return lax.dot_general(a, b, (((1,), (0,)), ((), ())), preferred_element_type=f32)


def nt(a, b):
    return lax.dot_general(a, b, (((1,), (1,)), ((), ())), preferred_element_type=f32)


def tn(a, b):
    return lax.dot_general(a, b, (((0,), (0,)), ((), ())), preferred_element_type=f32)


def full_nt(a, b):
    return lax.dot_general(
        a, b, (((1,), (1,)), ((), ())), preferred_element_type=f32, precision=highest
    )


def full_tn(a, b):
    return lax.dot_general(
        a, b, (((0,), (0,)), ((), ())), preferred_element_type=f32, precision=highest
    )


def split(x):
    high = x.astype(bf16)
    return high, (x - high.astype(f32)).astype(bf16)


def log_keep(rate):
    total = jnp.float32(1.0 / 8.0)
    for n in range(7, 0, -1):
        total = total * rate + jnp.float32(1.0 / n)
    return -rate * total


def powers(rate, exponents):
    return jnp.exp(exponents * log_keep(rate))


def rows_iota(shape=(BLOCK, SIZE)):
    return lax.broadcasted_iota(jnp.int32, shape, 0)


def cols_iota(shape=(BLOCK, SIZE)):
    return lax.broadcasted_iota(jnp.int32, shape, 1)


def local_places(positions, start):
    row = rows_iota((NPOS, BLOCK))
    wanted = jnp.full((NPOS, BLOCK), -1, jnp.int32)
    for j in range(NPOS):
        wanted = jnp.where(row == j, positions[0, j], wanted)
    return wanted - start


def selector(positions, start):
    return (local_places(positions, start) == cols_iota((NPOS, BLOCK))).astype(f32)


def head_cols(h):
    return slice(h * SIZE, (h + 1) * SIZE)


def decayed_state(weighted, other):
    high, low = split(weighted)
    return tn(other, high) + tn(other, low)


def halves(left, right, odd):
    lane = cols_iota(left.shape)
    if odd:
        return jnp.where(lane < 64, pltpu.roll(left, 64, 1), right)
    return jnp.where(lane < 64, left, pltpu.roll(right, 64, 1))


def query_state(meta, rate, positions, q, k, grad, v, rot, ref, proj, out, small):
    offset = rows_iota().astype(f32)
    places = local_places(positions, meta[0])
    lane = cols_iota((NPOS, BLOCK))
    select = (places == lane).astype(bf16)
    after = lane - places
    reached = after >= 0
    distance = jnp.maximum(after, 0).astype(f32)
    leave = jnp.clip(BLOCK - places, 0, BLOCK).astype(f32)
    chosen = nn(select, v[...])
    for h in range(HEADS):
        c = head_cols(h)
        weighted = q[:, c].astype(f32) * powers(rate[h], offset)
        state = decayed_state(weighted, grad[:, c])
        key = nn(select, k[:, c])
        table = jnp.where(reached, powers(rate[h], distance), 0.0)
        mixing = (nt(key.astype(bf16), q[:, c]) * table).astype(bf16)
        local = nn(mixing, grad[:, c])
        key = key * powers(rate[h], leave)
        for odd in range(2):
            i = 2 * h + odd
            out[i, 0:64] = state[64 * odd : 64 * odd + 64]
            out[i, 64:80] = key
            out[i, 80:96] = halves(local, chosen[:, c], odd)
    left = jnp.concatenate([chosen, ref[...], rot[...], jnp.zeros((2, WIDE), f32)], axis=0)
    right = jnp.concatenate(
        [proj[...] - rot[...], ref[...], rot[...], jnp.zeros((6, WIDE), f32)], axis=0
    )
    small[...] = jnp.zeros((24, 128), f32)
    small[:, 0:16] = full_nt(left, right)


def inverse_of(small):
    g00, g01 = small[16:17, 4:5], small[16:17, 5:6]
    g10, g11 = small[17:18, 4:5], small[17:18, 5:6]
    det = g00 * g11 - g01 * g10
    return g11 / det, -g01 / det, -g10 / det, g00 / det


def key_state(meta, rate, positions, small, v, k, rot, ref, proj, bias, moved, state, basis):
    i00, i01, i10, i11 = inverse_of(small)
    c0, c1 = small[18:22, 4:5], small[18:22, 5:6]
    rotated = (
        rot[...]
        - (c0 * i00 + c1 * i10) * ref[0:1, :]
        - (c0 * i01 + c1 * i11) * ref[1:2, :]
    )
    lift = proj[...] - rotated
    rows = jnp.concatenate(
        [rotated, ref[...], lift, ref[...], jnp.zeros((4, WIDE), f32)], axis=0
    )
    turned = pltpu.roll(small[16:24, :], 122, 1)
    t0, t1 = turned[0:1], turned[1:2]
    full = (
        small[0:16, :]
        + bias[...]
        + small[0:16, 4:5] * (t0 * i00 + t1 * i10)
        + small[0:16, 5:6] * (t0 * i01 + t1 * i11)
    )
    full = jnp.where(cols_iota((NPOS, 128)) < 4, full, 0.0)
    shift = jnp.zeros((NPOS, WIDE), f32)
    for r in range(4):
        shift = shift + full[:, r : r + 1] * rotated[r : r + 1, :]
    select = selector(positions, meta[0])
    offset = rows_iota().astype(f32)
    for h in range(HEADS):
        c = head_cols(h)
        basis[h] = rows[:, c]
        new = (v[:, c].astype(f32) + full_tn(select, shift[:, c])).astype(bf16)
        moved[:, c] = new
        weighted = k[:, c].astype(f32) * powers(rate[h], BLOCK - 1.0 - offset)
        out = decayed_state(weighted, new)
        state[2 * h] = out[:64]
        state[2 * h + 1] = out[64:]


def inside(rate, q, k, moved, grad, attended, grad_q, mixings, grad_mixings):
    between = rows_iota() - cols_iota()
    lower = between >= 0
    distance = jnp.maximum(between, 0).astype(f32)
    for h in range(HEADS):
        c = head_cols(h)
        table = jnp.where(lower, powers(rate[h], distance), 0.0)
        qh, kh, mh, gh = q[:, c], k[:, c], moved[:, c], grad[:, c]
        mixing = (nt(qh, kh) * table).astype(bf16)
        grad_mixing = (nt(gh, mh) * table).astype(bf16)
        mixings[h] = mixing
        grad_mixings[h] = grad_mixing
        attended[:, c] = nn(mixing, mh)
        grad_q[:, c] = nn(grad_mixing, kh)


def dot3(a, b):
    ah, al = split(a)
    bh, bl = split(b)
    return nt(ah, bh) + (nt(al, bh) + nt(ah, bl))


def backward_totals(meta, rate, later, out, gathered):
    keep = powers(rate[meta[2] // 2], jnp.full((64, 128), float(BLOCK), f32))
    keep_key = keep[0:NPOS]
    state = later[15, 0:64]
    key = later[0, 64:80]
    rows = later[15, 80:96]
    gathered[...] = jnp.zeros((NPOS, 128), f32)
    for b in range(14, -1, -1):
        gathered[:, 0:64] += dot3(later[b, 64:80], state)
        rows = rows + later[b, 80:96]
        state = state * keep + later[b, 0:64]
    for b in range(1, 16):
        key = key * keep_key + later[b, 64:80]
    out[0:64] = state
    out[64:80] = key
    out[80:96] = rows + gathered[...]


def backward_carried(
    meta, rate, later, own, one, two, three, basis, out, pairs, groups, gathered
):
    far, near = meta[1], meta[2]
    exponent = jnp.full((64, 128), float(BLOCK), f32)
    keep = powers(rate[near // 2], exponent)
    keep_group = powers(rate[near // 2], exponent * 16.0)
    for d, part in enumerate((own, one, two, three)):
        groups[(far + 4 - d) % 4] = part[...]
    rows = groups[3, 80:96]
    gathered[...] = jnp.zeros((NPOS, 128), f32)
    carry = jnp.zeros((64, 128), f32)
    state = carry
    for z in (2, 1, 0):
        carry = carry * keep_group + groups[z + 1, 0:64]
        gathered[:, 0:64] += dot3(groups[z, 64:80], carry)
        rows = rows + groups[z, 80:96]
        state = jnp.where(far == z, carry, state)
    rows = rows + gathered[...]
    both = basis[near // 2]
    turned = pltpu.roll(both, 64, 1)
    odd = near % 2 == 1
    lane, row = cols_iota((16, 128)), rows_iota((16, 128))
    for_grad = jnp.where(odd, turned, both)
    for_value = jnp.where(odd, both, turned)
    right = jnp.where(
        row < 6,
        jnp.where(lane < 64, for_grad, 0.0),
        jnp.where(lane < 64, 0.0, for_value),
    )
    gathered[...] = jnp.zeros((NPOS, 128), f32)
    gathered[:, 0:16] = full_nt(rows, right)
    for b in range(15, -1, -1):
        out[b, 0:64] = state
        out[b, 64:80] = gathered[...]
        state = state * keep + later[b, 0:64]
    pairs[...] = rows


def forward_totals(meta, rate, earlier, out):
    keep = powers(rate[meta[2] // 2], jnp.full((64, 128), float(BLOCK), f32))
    state = earlier[0]
    for b in range(1, 16):
        state = state * keep + earlier[b]
    out[...] = state


def forward_carried(meta, rate, earlier, one, two, three, parts, out):
    exponent = jnp.full((64, 128), float(BLOCK), f32)
    keep = powers(rate[meta[2] // 2], exponent)
    keep_group = powers(rate[meta[2] // 2], exponent * 16.0)
    state = (three[...] * keep_group + two[...]) * keep_group + one[...]
    for b in range(16):
        out[b, 0:64] = state
        out[b, 64:72] = parts[...]
        state = state * keep + earlier[b]


def sum_slices(x, out):
    total = x[0, 64:80]
    for i in range(1, 16):
        total = total + x[i, 64:80]
    out[...] = total


def products(head_sums, bias, pairs, parts):
    lane = cols_iota((NPOS, 128))
    sums = head_sums[...]
    code_grad = jnp.where(lane < 4, sums, 0.0)
    code = jnp.where(lane < 4, pltpu.roll(sums, 122, 1) + bias[...], 0.0)
    values_along = pltpu.roll(sums, 122, 1)
    turn = full_tn(code, pairs[...])[0:4]
    weight = full_tn(code_grad, pairs[...])[0:4]
    along = (full_tn(code, sums) - full_tn(code_grad, values_along))[0:4]
    total = full_tn(code_grad, jnp.ones((NPOS, 128), f32))[0:4]
    lane = cols_iota((4, 128))
    parts[...] = jnp.concatenate(
        [jnp.where(lane < 64, turn, weight), jnp.where(lane < 4, total, along)], axis=0
    )


def backward_rest(
    meta, rate, positions, q, k, moved, grad, state, mixings, grad_mixings, basis, head_sums,
    grad_k, grad_v,
):
    offset = rows_iota().astype(f32)
    select = selector(positions, meta[0])
    code_grad = head_sums[...]
    for h in range(HEADS):
        c = head_cols(h)
        leave = powers(rate[h], BLOCK - offset)
        high, low = split(jnp.concatenate([state[2 * h, 0:64], state[2 * h + 1, 0:64]], axis=0))
        qh, mh, kh, gh = q[:, c], moved[:, c], k[:, c], grad[:, c]
        inner = tn(grad_mixings[h], qh)
        grad_k[:, c] = (inner + leave * (nn(mh, high) + nn(mh, low))).astype(bf16)
        inner = tn(mixings[h], gh)
        lift = basis[h][6:10]
        fix = jnp.zeros((NPOS, SIZE), f32)
        for r in range(4):
            fix = fix + code_grad[:, r : r + 1] * lift[r : r + 1]
        out = inner + leave * (nt(kh, high) + nt(kh, low))
        grad_v[:, c] = (out + full_tn(select, fix)).astype(bf16)


def forward_rest(
    rate, q, grad, state, attended_in, grad_q_in, small, ref, parts,
    attended, grad_q, grad_rotation, grad_weight, grad_bias,
):
    offset = rows_iota().astype(f32)
    i00, i01, i10, i11 = inverse_of(small)
    a0, a1 = parts[4:8, 4:5], parts[4:8, 5:6]
    b0 = a0 * i00 + a1 * i10
    b1 = a0 * i01 + a1 * i11
    lane = cols_iota((8, 128))
    for h in range(HEADS):
        c = head_cols(h)
        enter = powers(rate[h], offset + 1.0)
        high, low = split(jnp.concatenate([state[2 * h, 0:64], state[2 * h + 1, 0:64]], axis=0))
        qh, gh = q[:, c], grad[:, c]
        attended[:, c] = (attended_in[:, c] + enter * (nt(qh, high) + nt(qh, low))).astype(bf16)
        grad_q[:, c] = (grad_q_in[:, c] + enter * (nn(gh, high) + nn(gh, low))).astype(bf16)
        even, odd = state[2 * h, 64:72], state[2 * h + 1, 64:72]
        turn = jnp.where(lane < 64, even, pltpu.roll(odd, 64, 1))[0:4]
        weight = jnp.where(lane < 64, pltpu.roll(even, 64, 1), odd)[0:4]
        grad_weight[:, c] = weight
        grad_rotation[:, c] = turn - weight - b0 * ref[0:1, c] - b1 * ref[1:2, c]
    grad_bias[...] = parts[4:8, :]


def call(kernel, specs, outs, scratch=(), flops=1e8, bytes_accessed=2e6):
    return pl.pallas_call(
        kernel,
        in_specs=[SMEM if s == "s" else VMEM for s in specs],
        out_specs=[VMEM] * len(outs),
        out_shape=[jax.ShapeDtypeStruct(s, d) for s, d in outs],
        scratch_shapes=[pltpu.VMEM(s, f32) for s in scratch],
        compiler_params=pltpu.CompilerParams(vmem_limit_bytes=40 * 1024 * 1024),
        cost_estimate=pl.CostEstimate(
            flops=int(flops), bytes_accessed=int(bytes_accessed), transcendentals=0
        ),
    )


def swap(x, axes):
    return lax.all_to_all(x, axes, 0, 0, tiled=False)


def ahead(x, d):
    return lax.ppermute(x, "zh", [(i, i + d) for i in range(4 - d)])


def round_by(x, d):
    return lax.ppermute(x, "zh", [(i, (i + d) % 4) for i in range(4)])


def shards(queries, key_rows, values, out_grad, rate, rotation, refusal, proj_weight, proj_bias, positions):
    q, k, v, grad = queries[0], key_rows[0], values[0], out_grad[0]
    ref = refusal.T
    far, near = lax.axis_index("zh"), lax.axis_index(NEAR)
    meta = jnp.stack([(far * 16 + near) * BLOCK, far, near]).astype(jnp.int32)
    bias = jnp.pad(proj_bias, (0, 124))[None, :]
    rows = (BLOCK, WIDE)
    tile = (NPOS, 128)
    square = (HEADS, BLOCK, BLOCK)

    grad_state, small = call(
        query_state, "sssvvvvvvv", [((16, 96, 128), f32), ((24, 128), f32)]
    )(meta, rate, positions, q, k, grad, v, rotation, ref, proj_weight)
    later = swap(grad_state, NEAR)
    small = lax.psum(small, "head")
    moved, state, basis = call(
        key_state,
        "sssvvvvvvv",
        [(rows, bf16), ((16, 64, 128), f32), ((HEADS, 16, 128), f32)],
    )(meta, rate, positions, small, v, k, rotation, ref, proj_weight, bias)
    (own,) = call(backward_totals, "ssv", [((96, 128), f32)], [tile])(meta, rate, later)
    around = [round_by(own, d) for d in (1, 2, 3)]
    state, own = lax.optimization_barrier((state, own))
    earlier = swap(state, NEAR)
    leaving, pairs = call(
        backward_carried,
        "ssvvvvvv",
        [((16, 80, 128), f32), (tile, f32)],
        [(4, 96, 128), tile],
    )(meta, rate, later, own, *around, basis)
    (total,) = call(forward_totals, "ssv", [((64, 128), f32)])(meta, rate, earlier)
    passed = [ahead(total, d) for d in (1, 2, 3)]
    leaving, total = lax.optimization_barrier((leaving, total))
    leaving = swap(leaving, NEAR)
    attended_in, grad_q_in, mixings, grad_mixings = call(
        inside, "svvvv", [(rows, f32)] * 2 + [(square, bf16)] * 2
    )(rate, q, k, moved, grad)
    (head_sums,) = call(sum_slices, "v", [(tile, f32)])(leaving)
    head_sums = lax.psum(head_sums, "head")
    (parts,) = call(products, "vvv", [((8, 128), f32)])(head_sums, bias, pairs)
    parts = lax.psum(parts, "dp")
    (entering,) = call(forward_carried, "ssvvvvv", [((16, 72, 128), f32)])(
        meta, rate, earlier, *passed, parts
    )
    entering = swap(entering, NEAR)
    grad_k, grad_v = call(backward_rest, "sssvvvvvvvvv", [(rows, bf16)] * 2)(
        meta, rate, positions, q, k, moved, grad, leaving, mixings, grad_mixings, basis, head_sums
    )
    attended, grad_q, grad_rotation, grad_weight, grad_bias = call(
        forward_rest,
        "svvvvvvvv",
        [(rows, bf16)] * 2 + [((4, WIDE), f32)] * 2 + [((4, 128), f32)],
    )(rate, q, grad, entering, attended_in, grad_q_in, small, ref, parts)
    return (
        attended[None],
        grad_q[None],
        grad_k[None],
        grad_v[None],
        grad_rotation,
        grad_weight,
        grad_bias[:, 0],
    )


def solution(mesh):
    own = Mesh(mesh.devices.reshape(4, 4, 4, 4, 2), ("zh", "zl", "y", "head", "dp"))
    seq = ("zh", "zl", "y")
    stream = P("dp", seq, "head")
    return jax.shard_map(
        shards,
        mesh=own,
        in_specs=(
            stream,
            stream,
            stream,
            stream,
            P("head"),
            P(None, "head"),
            P("head", None),
            P(None, "head"),
            P(),
            P("dp", None),
        ),
        out_specs=(stream, stream, stream, stream, P(None, "head"), P(None, "head"), P()),
        check_vma=False,
    )
```

time: 165 us -> 141 us (0.85); the launches traced: 164 us -> 138 us
  blocking collectives: 98.6 us -> 32.1 us
  starting transfers between devices: 26 us -> 65 us
  waiting for transfers between devices: 12.3 us -> 14.3 us
    all_to_all x3 -> x0, blocking collectives: 52.4 us -> none  [swap(): return lax.all_to_all(x, axes, 0, 0, tiled=False)]
    ppermute x0 -> x6, starting transfers between devices: none -> 35.8 us  [the longest x3 21.8 us: round_by(): return lax.ppermute(x, 'zh', [(i, (i + d) % 4) for i in range(4)])]
    psum x3 -> x2, blocking collectives: 32.2 us -> 18.1 us  [the longest x1 10.7 us: shards(): parts = lax.psum(parts, 'dp')]
    ppermute x0 -> x6, waiting for transfers between devices: none -> 4.35 us  [the longest x3 4.34 us: round_by(): return lax.ppermute(x, 'zh', [(i, (i + d) % 4) for i in range(4)])]
    all_to_all x4, starting transfers between devices: 26 us -> 29.1 us  [swap(): return lax.all_to_all(x, axes, 0, 0, tiled=False)]
    all_to_all x4, waiting for transfers between devices: 12.3 us -> 9.98 us  [swap(): return lax.all_to_all(x, axes, 0, 0, tiled=False)]
    pallas_call x9 -> x11, Pallas kernels: 17.9 us -> 19.1 us  [the longest x1 4.23 us: shards(): call(key_state, 'sssvvvvvvv', [(rows, bf16), ((16, 64, 128), f32), ((HEAD...]
    unnamed x34 -> x44, local copies, waits for them, and re-layouts: 7.25 us -> 6.36 us
  transfers between devices with their start and end apart: 4 -> 10, of which waited for: 2 -> 3; matrix products, arithmetic and copies ran while one was open for 0% -> 0% of each run, Pallas kernels for 5% -> 8%
where the time goes in v2:
time: 141 us; the launch traced here: 138 us
  starting transfers between devices  65 us (46%)
  blocking collectives  32.1 us (23%)
  Pallas kernels  19.1 us (14%)
  waiting for transfers between devices  14.3 us (10%)
  local copies, waits for them, and re-layouts  6.99 us (5%)
    all_to_all x4, starting transfers between devices, swap(): return lax.all_to_all(x, axes, 0, 0, tiled=False)  29.1 us
    ppermute x3, starting transfers between devices, round_by(): return lax.ppermute(x, 'zh', [(i, (i + d) % 4) for i in range(4)])  21.8 us
    ppermute x3, starting transfers between devices, ahead(): return lax.ppermute(x, 'zh', [(i, i + d) for i in range(4 - d)])  14 us
    psum x1, blocking collectives, shards(): small = lax.psum(small, 'head')  14 us
    psum x1, blocking collectives, shards(): parts = lax.psum(parts, 'dp')  10.7 us
    all_to_all x4, waiting for transfers between devices, swap(): return lax.all_to_all(x, axes, 0, 0, tiled=False)  9.98 us
    psum x1, blocking collectives, shards(): head_sums = lax.psum(head_sums, 'head')  7.37 us
    unnamed x44, local copies, waits for them, and re-layouts  6.36 us
  transfers between devices with their start and end apart: 10, of which 3 were waited for; matrix products, arithmetic and copies ran while one was open for 0% of the time, Pallas kernels for 8%

profile of v2, /device:TPU:1, one launch (start us, length us, event | category | flops | bytes accessed | tf_op | source)
XLA Modules:
  0.0 138.4 jit_solution(7327761684088272339)
XLA Ops:
  0.7 0.0 copy-start.8
  0.7 0.1 pad_add_fusion.meta
  0.8 0.6 copy-done.11
  1.4 0.0 copy-done.10
  1.4 0.0 copy-done.12
  1.4 0.0 copy-done.19
  1.4 0.9 copy-done
  2.4 0.9 copy-done.2
  3.3 0.9 copy-done.4
  4.3 0.9 copy-done.6
  5.2 3.0 %shard_map.153 = (f32[16,96,128]{2,1,0:T(8,128)}, f32[24,128]{1,0:T(8,128)S(1)}) custom-call(s32[3]{0:T(128)S(1)} %pad_add_fusion.meta, f32[8]{0:T(128)S(1)} %copy-done.12, s32[1,16]{1,0:T(1,128)S(1)} %copy-done.19, bf16[128,1024]{1,0:T(8,128)(2,1)S(1)} %bitcast.14, bf16[128,1024]{1,0:T(8,128)(2,1)S(1)} %bitcast.22, bf16[128,1024]{1,0:T(8,128)(2,1)S(1)} %bitcast.18, ...), custom_call_target="tpu_custom_call" | custom-call | flops 100000000 | bytes 2000000 | tf_op jit(solution)/shard_map/pallas_call | solution.py:378
  8.2 9.3 %all-to-all-start = ((f32[16,96,128]{2,1,0:T(8,128)}), f32[16,96,128]{2,1,0:T(8,128)S(1)}, u32[]{:S(2)}, u32[]{:S(2)}) async-start(f32[16,96,128]{2,1,0:T(8,128)} %get-tuple-element.30), calls=%async_computation | async-start | bytes 1572864 | tf_op jit(solution)/shard_map/all_to_all | solution.py:357
  17.5 0.0 copy-start.21
  17.5 14.0 %psum.21.small = f32[24,128]{1,0:T(8,128)S(1)} all-reduce(f32[24,128]{1,0:T(8,128)S(1)} %get-tuple-element.28), channel_id=1, replica_groups=mesh['zh'=4,'zl'=4,'y'=4,'head'=4,'dp'=2] {'head'}, use_global_device_ids=true, to_apply=%region_0.1 | all-reduce | flops 3072 | bytes 24576 | tf_op jit(solution)/shard_map/psum | solution.py:382
  31.5 4.2 %shard_map.154 = (bf16[128,1024]{1,0:T(8,128)(2,1)S(1)}, f32[16,64,128]{2,1,0:T(8,128)}, f32[8,16,128]{2,1,0:T(8,128)S(1)}) custom-call(s32[3]{0:T(128)S(1)} %pad_add_fusion.meta, f32[8]{0:T(128)S(1)} %copy-done.12, s32[1,16]{1,0:T(1,128)S(1)} %copy-done.19, f32[24,128]{1,0:T(8,128)S(1)} %psum.21.small, bf16[128,1024]{1,0:T(8,128)(2,1)S(1)} %bitcast.27, ...), custom_call_target="tpu_custom_call" | custom-call | flops 100000000 | bytes 2000000 | tf_op jit(solution)/shard_map/pallas_call | solution.py:383
  35.8 0.0 all-to-all-done.later
  35.8 1.1 shard_map.155.own
  36.8 7.1 %all-to-all-start.1 = ((f32[16,64,128]{2,1,0:T(8,128)}), f32[16,64,128]{2,1,0:T(8,128)S(1)}, u32[]{:S(2)}, u32[]{:S(2)}) async-start(f32[16,64,128]{2,1,0:T(8,128)} %get-tuple-element.31), calls=%async_computation.1 | async-start | bytes 1048576 | tf_op jit(solution)/shard_map/all_to_all | solution.py:357
  43.9 8.7 %collective-permute-start.3 = (f32[96,128]{1,0:T(8,128)S(1)}, f32[96,128]{1,0:T(8,128)S(1)}, u32[]{:S(2)}, u32[]{:S(2)}) collective-permute-start(f32[96,128]{1,0:T(8,128)S(1)} %shard_map.155.own), channel_id=1, source_target_pairs={{0,128},{128,256},{256,384},{384,0},{1,129},{129,257},{257,385},{3... | collective-permute-start | bytes 147464 | tf_op jit(solution)/shard_map/ppermute | solution.py:365
  52.7 8.0 %collective-permute-start.4 = (f32[96,128]{1,0:T(8,128)S(1)}, f32[96,128]{1,0:T(8,128)S(1)}, u32[]{:S(2)}, u32[]{:S(2)}) collective-permute-start(f32[96,128]{1,0:T(8,128)S(1)} %shard_map.155.own), channel_id=1, source_target_pairs={{0,256},{128,384},{256,0},{384,128},{1,257},{129,385},{257,1},{385... | collective-permute-start | bytes 147464 | tf_op jit(solution)/shard_map/ppermute | solution.py:365
  60.6 5.2 %collective-permute-start.5 = (f32[96,128]{1,0:T(8,128)S(1)}, f32[96,128]{1,0:T(8,128)S(1)}, u32[]{:S(2)}, u32[]{:S(2)}) collective-permute-start(f32[96,128]{1,0:T(8,128)S(1)} %shard_map.155.own), channel_id=1, source_target_pairs={{0,384},{128,0},{256,128},{384,256},{1,385},{129,1},{257,129},{385... | collective-permute-start | bytes 147464 | tf_op jit(solution)/shard_map/ppermute | solution.py:365
  65.8 0.0 collective-permute-done.3.one
  65.8 1.4 %collective-permute-done.4.two = f32[96,128]{1,0:T(8,128)S(1)} collective-permute-done((f32[96,128]{1,0:T(8,128)S(1)}, f32[96,128]{1,0:T(8,128)S(1)}, u32[]{:S(2)}, u32[]{:S(2)}) %collective-permute-start.4) | collective-permute-done | bytes 49184 | tf_op jit(solution)/shard_map/ppermute | solution.py:365
  67.2 2.9 %collective-permute-done.5.three = f32[96,128]{1,0:T(8,128)S(1)} collective-permute-done((f32[96,128]{1,0:T(8,128)S(1)}, f32[96,128]{1,0:T(8,128)S(1)}, u32[]{:S(2)}, u32[]{:S(2)}) %collective-permute-start.5) | collective-permute-done | bytes 49184 | tf_op jit(solution)/shard_map/ppermute | solution.py:365
  70.1 1.8 %shard_map.157 = (f32[16,80,128]{2,1,0:T(8,128)}, f32[16,128]{1,0:T(8,128)S(1)}) custom-call(s32[3]{0:T(128)S(1)} %pad_add_fusion.meta, f32[8]{0:T(128)S(1)} %copy-done.12, f32[16,96,128]{2,1,0:T(8,128)S(1)} %all-to-all-done.later, f32[96,128]{1,0:T(8,128)S(1)} %shard_map.155.own, f32[96,128]{1,0:T(8,128)S(1)} %collective-permute-done.3.one, ...), custom_call_target="tpu_custom_call" | custom-call | flops 100000000 | bytes 2000000 | tf_op jit(solution)/shard_map/pallas_call | solution.py:392
  71.9 0.6 shard_map.156
  72.5 7.3 %all-to-all-start.2 = ((f32[16,80,128]{2,1,0:T(8,128)}), f32[16,80,128]{2,1,0:T(8,128)S(1)}, u32[]{:S(2)}, u32[]{:S(2)}) async-start(f32[16,80,128]{2,1,0:T(8,128)} %get-tuple-element.35), calls=%async_computation.2 | async-start | bytes 1310720 | tf_op jit(solution)/shard_map/all_to_all | solution.py:357
  79.9 2.7 %collective-permute-start = (f32[64,128]{1,0:T(8,128)S(1)}, f32[64,128]{1,0:T(8,128)S(1)}, u32[]{:S(2)}, u32[]{:S(2)}) collective-permute-start(f32[64,128]{1,0:T(8,128)S(1)} %shard_map.156), channel_id=1, source_target_pairs={{0,128},{128,256},{256,384},{1,129},{129,257},{257,385},{2,130},{1... | collective-permute-start | bytes 98312 | tf_op jit(solution)/shard_map/ppermute | solution.py:361
  82.6 10.0 %collective-permute-start.1 = (f32[64,128]{1,0:T(8,128)S(1)}, f32[64,128]{1,0:T(8,128)S(1)}, u32[]{:S(2)}, u32[]{:S(2)}) collective-permute-start(f32[64,128]{1,0:T(8,128)S(1)} %shard_map.156), channel_id=1, source_target_pairs={{0,256},{128,384},{1,257},{129,385},{2,258},{130,386},{3,259},{131... | collective-permute-start | bytes 98312 | tf_op jit(solution)/shard_map/ppermute | solution.py:361
  92.6 1.3 collective-permute-start.2
  94.0 7.4 %psum.22.head_sums = f32[16,128]{1,0:T(8,128)S(1)} all-reduce(f32[16,128]{1,0:T(8,128)S(1)} %shard_map.158), channel_id=1, replica_groups=mesh['zh'=4,'zl'=4,'y'=4,'head'=4,'dp'=2] {'head'}, use_global_device_ids=true, to_apply=%region_1.2 | all-reduce | flops 2048 | bytes 16384 | tf_op jit(solution)/shard_map/psum | solution.py:406
  101.3 0.5 shard_map.159
  101.9 0.0 copy-start.17
  101.9 0.6 copy-done.17
  102.5 10.7 %psum.23.parts = f32[8,128]{1,0:T(8,128)S(1)} all-reduce(f32[8,128]{1,0:T(8,128)S(1)} %shard_map.159), channel_id=1, replica_groups=mesh['zh'=4,'zl'=4,'y'=4,'head'=4,'dp'=2] {'dp'}, use_global_device_ids=true, to_apply=%region_2.3 | all-reduce | flops 1024 | bytes 8192 | tf_op jit(solution)/shard_map/psum | solution.py:408
  113.2 1.4 %shard_map.160 = f32[16,72,128]{2,1,0:T(8,128)} custom-call(s32[3]{0:T(128)S(1)} %pad_add_fusion.meta, f32[8]{0:T(128)S(1)} %copy-done.12, f32[16,64,128]{2,1,0:T(8,128)S(1)} %all-to-all-done.1.earlier, f32[64,128]{1,0:T(8,128)S(1)} %collective-permute-done.one, f32[64,128]{1,0:T(8,128)S(1)} %collective-permute-done.1.two, ...), custom_call_target="tpu_custom_call" | custom-call | flops 100000000 | bytes 2000000 | tf_op jit(solution)/shard_map/pallas_call | solution.py:409
  114.7 0.6 copy-done.13
  115.3 5.4 %all-to-all-start.3 = ((f32[16,72,128]{2,1,0:T(8,128)}), f32[16,72,128]{2,1,0:T(8,128)S(1)}, u32[]{:S(2)}, u32[]{:S(2)}) async-start(f32[16,72,128]{2,1,0:T(8,128)} %shard_map.160), calls=%async_computation.3 | async-start | bytes 1179648 | tf_op jit(solution)/shard_map/all_to_all | solution.py:357
  120.6 0.0 copy-start.18
  120.7 2.0 %shard_map.161 = (f32[128,1024]{1,0:T(8,128)S(1)}, f32[128,1024]{1,0:T(8,128)S(1)}, bf16[8,128,128]{2,1,0:T(8,128)(2,1)S(1)}, bf16[8,128,128]{2,1,0:T(8,128)(2,1)S(1)}) custom-call(f32[8]{0:T(128)S(1)} %copy-done.12, bf16[128,1024]{1,0:T(8,128)(2,1)S(1)} %bitcast.15, bf16[128,1024]{1,0:T(8,128)(2,1)S(1)} %bitcast.24, ...), custom_call_target="tpu_custom_call" | custom-call | flops 100000000 | bytes 2000000 | tf_op jit(solution)/shard_map/pallas_call | solution.py:402
  122.6 0.0 copy-start.16
  122.6 0.0 copy-start.20
  122.7 0.6 copy-done.16
  123.3 0.0 copy-done.20
  123.3 2.5 %shard_map.163 = (bf16[128,1024]{1,0:T(8,128)(2,1)}, bf16[128,1024]{1,0:T(8,128)(2,1)}) custom-call(s32[3]{0:T(128)S(1)} %copy-done.16, f32[8]{0:T(128)S(1)} %copy-done.12, s32[1,16]{1,0:T(1,128)S(1)} %copy-done.20, bf16[128,1024]{1,0:T(8,128)(2,1)S(1)} %bitcast.16, bf16[128,1024]{1,0:T(8,128)(2,1)S(1)} %bitcast.25, ...), custom_call_target="tpu_custom_call" | custom-call | flops 100000000 | bytes 2000000 | tf_op jit(solution)/shard_map/pallas_call | solution.py:413
  125.8 10.0 %all-to-all-done.3.state = f32[16,72,128]{2,1,0:T(8,128)S(1)} async-done(((f32[16,72,128]{2,1,0:T(8,128)}), f32[16,72,128]{2,1,0:T(8,128)S(1)}, u32[]{:S(2)}, u32[]{:S(2)}) %all-to-all-start.3) | async-done | bytes 589856 | tf_op jit(solution)/shard_map/all_to_all | solution.py:357
  135.8 2.0 %shard_map.162 = (bf16[128,1024]{1,0:T(8,128)(2,1)}, bf16[128,1024]{1,0:T(8,128)(2,1)}, f32[4,1024]{1,0:T(4,128)}, f32[4,1024]{1,0:T(4,128)}, f32[4,128]{1,0:T(4,128)S(1)}) custom-call(f32[8]{0:T(128)S(1)} %copy-done.12, bf16[128,1024]{1,0:T(8,128)(2,1)S(1)} %bitcast.17, bf16[128,1024]{1,0:T(8,128)(2,1)S(1)} %bitcast.21, ...), custom_call_target="tpu_custom_call" | custom-call | flops 100000000 | bytes 2000000 | tf_op jit(solution)/shard_map/pallas_call | solution.py:416
  137.8 0.6 slice_reduce_fusion
  (33 shorter events, 0.1 us)
Async XLA Ops:
  0.6 0.7 copy-start.11
  0.6 0.7 copy-start.10
  0.7 0.7 copy-start.8
  0.7 112.4 %copy-start.15 = (s32[3]{0:T(128)}, s32[3]{0:T(128)S(1)}, u32[]{:S(2)}) copy-start(s32[3]{0:T(128)S(1)} %pad_add_fusion.meta) | copy-start | bytes 40
  0.8 0.7 copy-start.12
  0.8 0.7 copy-start.19
  1.4 0.9 copy-start
  2.4 0.9 copy-start.2
  3.3 0.9 copy-start.4
  4.3 0.9 copy-start.6
  8.2 23.3 %copy-start.5 = (bf16[1,128,1024]{2,1,0:T(8,128)(2,1)S(1)}, bf16[1,128,1024]{2,1,0:T(8,128)(2,1)}, u32[]{:S(2)}) copy-start(bf16[1,128,1024]{2,1,0:T(8,128)(2,1)} %param.11) | copy-start | bytes 786436
  8.2 23.3 %copy-start.7 = (bf16[1,128,1024]{2,1,0:T(8,128)(2,1)S(1)}, bf16[1,128,1024]{2,1,0:T(8,128)(2,1)}, u32[]{:S(2)}) copy-start(bf16[1,128,1024]{2,1,0:T(8,128)(2,1)} %param.12) | copy-start | bytes 786436
  8.2 27.6 %all-to-all-start = ((f32[16,96,128]{2,1,0:T(8,128)}), f32[16,96,128]{2,1,0:T(8,128)S(1)}, u32[]{:S(2)}, u32[]{:S(2)}) async-start(f32[16,96,128]{2,1,0:T(8,128)} %get-tuple-element.30), calls=%async_computation | async-start | bytes 1572864 | tf_op jit(solution)/shard_map/all_to_all | solution.py:357
  17.5 14.0 %copy-start.21 = (f32[4]{0:T(128)S(1)}, f32[4]{0:T(128)}, u32[]{:S(2)}) copy-start(f32[4]{0:T(128)} %param.18) | copy-start | bytes 52
  36.8 35.1 %all-to-all-start.1 = ((f32[16,64,128]{2,1,0:T(8,128)}), f32[16,64,128]{2,1,0:T(8,128)S(1)}, u32[]{:S(2)}, u32[]{:S(2)}) async-start(f32[16,64,128]{2,1,0:T(8,128)} %get-tuple-element.31), calls=%async_computation.1 | async-start | bytes 1048576 | tf_op jit(solution)/shard_map/all_to_all | solution.py:357
  43.9 21.9 %collective-permute-start.3 = (f32[96,128]{1,0:T(8,128)S(1)}, f32[96,128]{1,0:T(8,128)S(1)}, u32[]{:S(2)}, u32[]{:S(2)}) collective-permute-start(f32[96,128]{1,0:T(8,128)S(1)} %shard_map.155.own), channel_id=1, source_target_pairs={{0,128},{128,256},{256,384},{384,0},{1,129},{129,257},{257,385},{3... | collective-permute-start | bytes 147464 | tf_op jit(solution)/shard_map/ppermute | solution.py:365
  52.7 14.6 %collective-permute-start.4 = (f32[96,128]{1,0:T(8,128)S(1)}, f32[96,128]{1,0:T(8,128)S(1)}, u32[]{:S(2)}, u32[]{:S(2)}) collective-permute-start(f32[96,128]{1,0:T(8,128)S(1)} %shard_map.155.own), channel_id=1, source_target_pairs={{0,256},{128,384},{256,0},{384,128},{1,257},{129,385},{257,1},{385... | collective-permute-start | bytes 147464 | tf_op jit(solution)/shard_map/ppermute | solution.py:365
  60.6 9.5 %collective-permute-start.5 = (f32[96,128]{1,0:T(8,128)S(1)}, f32[96,128]{1,0:T(8,128)S(1)}, u32[]{:S(2)}, u32[]{:S(2)}) collective-permute-start(f32[96,128]{1,0:T(8,128)S(1)} %shard_map.155.own), channel_id=1, source_target_pairs={{0,384},{128,0},{256,128},{384,256},{1,385},{129,1},{257,129},{385... | collective-permute-start | bytes 147464 | tf_op jit(solution)/shard_map/ppermute | solution.py:365
  72.5 21.4 %all-to-all-start.2 = ((f32[16,80,128]{2,1,0:T(8,128)}), f32[16,80,128]{2,1,0:T(8,128)S(1)}, u32[]{:S(2)}, u32[]{:S(2)}) async-start(f32[16,80,128]{2,1,0:T(8,128)} %get-tuple-element.35), calls=%async_computation.2 | async-start | bytes 1310720 | tf_op jit(solution)/shard_map/all_to_all | solution.py:357
  79.9 33.3 %collective-permute-start = (f32[64,128]{1,0:T(8,128)S(1)}, f32[64,128]{1,0:T(8,128)S(1)}, u32[]{:S(2)}, u32[]{:S(2)}) collective-permute-start(f32[64,128]{1,0:T(8,128)S(1)} %shard_map.156), channel_id=1, source_target_pairs={{0,128},{128,256},{256,384},{1,129},{129,257},{257,385},{2,130},{1... | collective-permute-start | bytes 98312 | tf_op jit(solution)/shard_map/ppermute | solution.py:361
  82.6 30.6 %collective-permute-start.1 = (f32[64,128]{1,0:T(8,128)S(1)}, f32[64,128]{1,0:T(8,128)S(1)}, u32[]{:S(2)}, u32[]{:S(2)}) collective-permute-start(f32[64,128]{1,0:T(8,128)S(1)} %shard_map.156), channel_id=1, source_target_pairs={{0,256},{128,384},{1,257},{129,385},{2,258},{130,386},{3,259},{131... | collective-permute-start | bytes 98312 | tf_op jit(solution)/shard_map/ppermute | solution.py:361
  92.6 20.6 %collective-permute-start.2 = (f32[64,128]{1,0:T(8,128)S(1)}, f32[64,128]{1,0:T(8,128)S(1)}, u32[]{:S(2)}, u32[]{:S(2)}) collective-permute-start(f32[64,128]{1,0:T(8,128)S(1)} %shard_map.156), channel_id=1, source_target_pairs={{0,384},{1,385},{2,386},{3,387},{4,388},{5,389},{6,390},{7,391},{8... | collective-permute-start | bytes 98312 | tf_op jit(solution)/shard_map/ppermute | solution.py:361
  101.9 0.6 copy-start.17
  114.7 0.6 copy-start.13
  115.2 5.4 %copy-start.1 = (bf16[1,128,1024]{2,1,0:T(8,128)(2,1)S(1)}, bf16[1,128,1024]{2,1,0:T(8,128)(2,1)}, u32[]{:S(2)}) copy-start(bf16[1,128,1024]{2,1,0:T(8,128)(2,1)} %param.10) | copy-start | bytes 786436
  115.3 5.4 %copy-start.3 = (bf16[1,128,1024]{2,1,0:T(8,128)(2,1)S(1)}, bf16[1,128,1024]{2,1,0:T(8,128)(2,1)}, u32[]{:S(2)}) copy-start(bf16[1,128,1024]{2,1,0:T(8,128)(2,1)} %param.13) | copy-start | bytes 786436
  115.3 20.6 %all-to-all-start.3 = ((f32[16,72,128]{2,1,0:T(8,128)}), f32[16,72,128]{2,1,0:T(8,128)S(1)}, u32[]{:S(2)}, u32[]{:S(2)}) async-start(f32[16,72,128]{2,1,0:T(8,128)} %shard_map.160), calls=%async_computation.3 | async-start | bytes 1179648 | tf_op jit(solution)/shard_map/all_to_all | solution.py:357
  120.6 2.0 %copy-start.18 = (f32[16,128]{1,0:T(8,128)S(1)}, f32[16,128]{1,0:T(8,128)}, u32[]{:S(2)}) copy-start(f32[16,128]{1,0:T(8,128)} %copy-done.17) | copy-start | bytes 24580
  122.6 0.7 copy-start.16
  122.6 0.7 copy-start.20
  123.3 12.5 %copy-start.9 = (f32[1024,2]{0,1:T(2,128)S(1)}, f32[1024,2]{0,1:T(2,128)}, u32[]{:S(2)}) copy-start(f32[1024,2]{0,1:T(2,128)} %param.16) | copy-start | bytes 24580
  123.3 12.5 %copy-start.14 = (f32[8,128]{1,0:T(8,128)S(1)}, f32[8,128]{1,0:T(8,128)}, u32[]{:S(2)}) copy-start(f32[8,128]{1,0:T(8,128)} %copy-done.13) | copy-start | bytes 12292

commit v3 on v2

v3 whole, which is shorter than its diff:
```python
import functools
import jax
import jax.numpy as jnp
from jax import lax
from jax.experimental import pallas as pl
from jax.experimental.pallas import tpu as pltpu
from jax.sharding import Mesh, PartitionSpec as P

highest = lax.Precision.HIGHEST
f32, bf16 = jnp.float32, jnp.bfloat16
BLOCK = 128
HEADS = 8
SIZE = 128
WIDE = HEADS * SIZE
NPOS = 16
NEAR = ("zl", "y")
ANY = pl.BlockSpec(memory_space=pltpu.HBM)
SMEM = pl.BlockSpec(memory_space=pltpu.SMEM)
VMEM = pl.BlockSpec(memory_space=pltpu.VMEM)


def nn(a, b):
    return lax.dot_general(a, b, (((1,), (0,)), ((), ())), preferred_element_type=f32)


def nt(a, b):
    return lax.dot_general(a, b, (((1,), (1,)), ((), ())), preferred_element_type=f32)


def tn(a, b):
    return lax.dot_general(a, b, (((0,), (0,)), ((), ())), preferred_element_type=f32)


def full_nt(a, b):
    return lax.dot_general(
        a, b, (((1,), (1,)), ((), ())), preferred_element_type=f32, precision=highest
    )


def full_tn(a, b):
    return lax.dot_general(
        a, b, (((0,), (0,)), ((), ())), preferred_element_type=f32, precision=highest
    )


def split(x):
    high = x.astype(bf16)
    return high, (x - high.astype(f32)).astype(bf16)


def log_keep(rate):
    total = jnp.float32(1.0 / 8.0)
    for n in range(7, 0, -1):
        total = total * rate + jnp.float32(1.0 / n)
    return -rate * total


def powers(rate, exponents):
    return jnp.exp(exponents * log_keep(rate))


def rows_iota(shape=(BLOCK, SIZE)):
    return lax.broadcasted_iota(jnp.int32, shape, 0)


def cols_iota(shape=(BLOCK, SIZE)):
    return lax.broadcasted_iota(jnp.int32, shape, 1)


def far_place():
    return lax.axis_index("zh")


def near_place():
    return lax.axis_index("zl") * 4 + lax.axis_index("y")


def block_start():
    return (far_place() * 16 + near_place()) * BLOCK


def local_places(positions, start):
    row = rows_iota((NPOS, BLOCK))
    wanted = jnp.full((NPOS, BLOCK), -1, jnp.int32)
    for j in range(NPOS):
        wanted = jnp.where(row == j, positions[0, j], wanted)
    return wanted - start


def selector(positions, start):
    return (local_places(positions, start) == cols_iota((NPOS, BLOCK))).astype(f32)


def head_cols(h):
    return slice(h * SIZE, (h + 1) * SIZE)


def decayed_state(weighted, other):
    high, low = split(weighted)
    return tn(other, high) + tn(other, low)


def halves(left, right, odd):
    lane = cols_iota(left.shape)
    if odd:
        return jnp.where(lane < 64, pltpu.roll(left, 64, 1), right)
    return jnp.where(lane < 64, left, pltpu.roll(right, 64, 1))


def query_state(
    rate, positions, q_far, k_far, grad_far, v_far, rot, ref, proj, out_far, small,
    q, k, grad, v, out, chosen, arrived, sent,
):
    fetches = []
    for part in range(4):
        c = slice(part * 2 * SIZE, (part + 1) * 2 * SIZE)
        pairs = ((q_far, q), (grad_far, grad), (k_far, k), (v_far, v))
        for n, (src, dst) in enumerate(pairs):
            fetch = pltpu.make_async_copy(src.at[:, c], dst.at[:, c], arrived.at[part, n])
            fetch.start()
            fetches.append(fetch)
    sends = []
    offset = rows_iota().astype(f32)
    places = local_places(positions, block_start())
    lane = cols_iota((NPOS, BLOCK))
    select = (places == lane).astype(bf16)
    after = lane - places
    reached = after >= 0
    distance = jnp.maximum(after, 0).astype(f32)
    leave = jnp.clip(BLOCK - places, 0, BLOCK).astype(f32)
    for h in range(HEADS):
        c = head_cols(h)
        if h % 2 == 0:
            for fetch in fetches[2 * h : 2 * h + 4]:
                fetch.wait()
        chosen[:, c] = nn(select, v[:, c])
        weighted = q[:, c].astype(f32) * powers(rate[h], offset)
        state = decayed_state(weighted, grad[:, c])
        key = nn(select, k[:, c])
        table = jnp.where(reached, powers(rate[h], distance), 0.0)
        mixing = (nt(key.astype(bf16), q[:, c]) * table).astype(bf16)
        local = nn(mixing, grad[:, c])
        key = key * powers(rate[h], leave)
        for odd in range(2):
            i = 2 * h + odd
            out[i, 0:64] = state[64 * odd : 64 * odd + 64]
            out[i, 64:80] = key
            out[i, 80:96] = halves(local, chosen[:, c], odd)
        part = pl.ds(2 * h, 2)
        send = pltpu.make_async_copy(out.at[part], out_far.at[part], sent.at[h])
        send.start()
        sends.append(send)
    left = jnp.concatenate([chosen[...], ref[...], rot[...], jnp.zeros((2, WIDE), f32)], axis=0)
    right = jnp.concatenate(
        [proj[...] - rot[...], ref[...], rot[...], jnp.zeros((6, WIDE), f32)], axis=0
    )
    small[...] = jnp.zeros((24, 128), f32)
    small[:, 0:16] = full_nt(left, right)
    for send in sends:
        send.wait()


def inverse_of(small):
    g00, g01 = small[16:17, 4:5], small[16:17, 5:6]
    g10, g11 = small[17:18, 4:5], small[17:18, 5:6]
    det = g00 * g11 - g01 * g10
    return g11 / det, -g01 / det, -g10 / det, g00 / det


def third_terms(x):
    high = x.astype(bf16)
    rest = x - high.astype(f32)
    middle = rest.astype(bf16)
    low = (rest - middle.astype(f32)).astype(bf16)
    return jnp.concatenate([high, middle, low], axis=0)


def key_state(
    rate, positions, small, v, k, rot, ref, proj, bias, moved, state_far, basis, state, sent
):
    i00, i01, i10, i11 = inverse_of(small)
    c0, c1 = small[18:22, 4:5], small[18:22, 5:6]
    rotated = (
        rot[...]
        - (c0 * i00 + c1 * i10) * ref[0:1, :]
        - (c0 * i01 + c1 * i11) * ref[1:2, :]
    )
    lift = proj[...] - rotated
    rows = jnp.concatenate(
        [rotated, ref[...], lift, ref[...], jnp.zeros((4, WIDE), f32)], axis=0
    )
    turned = pltpu.roll(small[16:24, :], 122, 1)
    t0, t1 = turned[0:1], turned[1:2]
    full = (
        small[0:16, :]
        + bias[...]
        + small[0:16, 4:5] * (t0 * i00 + t1 * i10)
        + small[0:16, 5:6] * (t0 * i01 + t1 * i11)
    )
    full = jnp.where(cols_iota((NPOS, 128)) < 4, full, 0.0)
    shift = jnp.zeros((NPOS, WIDE), f32)
    for r in range(4):
        shift = shift + full[:, r : r + 1] * rotated[r : r + 1, :]
    select = selector(positions, block_start()).astype(bf16)
    select = jnp.concatenate([select, select, select], axis=0)
    shift = third_terms(shift)
    offset = rows_iota().astype(f32)
    sends = []
    for h in range(HEADS):
        c = head_cols(h)
        basis[h] = rows[:, c]
        new = (v[:, c].astype(f32) + tn(select, shift[:, c])).astype(bf16)
        moved[:, c] = new
        weighted = k[:, c].astype(f32) * powers(rate[h], BLOCK - 1.0 - offset)
        out = decayed_state(weighted, new)
        state[2 * h] = out[:64]
        state[2 * h + 1] = out[64:]
        part = pl.ds(2 * h, 2)
        send = pltpu.make_async_copy(state.at[part], state_far.at[part], sent.at[h])
        send.start()
        sends.append(send)
    for send in sends:
        send.wait()


def dot3(a, b):
    ah, al = split(a)
    bh, bl = split(b)
    return nt(ah, bh) + (nt(al, bh) + nt(ah, bl))


def backward_totals(rate, later, out, gathered):
    keep = powers(rate[near_place() // 2], jnp.full((64, 128), float(BLOCK), f32))
    keep_key = keep[0:NPOS]
    state = later[15, 0:64]
    key = later[0, 64:80]
    rows = later[15, 80:96]
    gathered[...] = jnp.zeros((NPOS, 128), f32)
    for b in range(14, -1, -1):
        gathered[:, 0:64] += dot3(later[b, 64:80], state)
        rows = rows + later[b, 80:96]
        state = state * keep + later[b, 0:64]
    for b in range(1, 16):
        key = key * keep_key + later[b, 64:80]
    out[0:64] = state
    out[64:80] = key
    out[80:96] = rows + gathered[...]


def backward_carried(
    rate, later, groups, basis, out_far, out, gathered, sent
):
    far, near = far_place(), near_place()
    exponent = jnp.full((64, 128), float(BLOCK), f32)
    keep = powers(rate[near // 2], exponent)
    keep_group = powers(rate[near // 2], exponent * 16.0)
    rows = groups[3, 80:96]
    gathered[...] = jnp.zeros((NPOS, 128), f32)
    carry = jnp.zeros((64, 128), f32)
    state = carry
    for z in (2, 1, 0):
        carry = carry * keep_group + groups[z + 1, 0:64]
        gathered[:, 0:64] += dot3(groups[z, 64:80], carry)
        rows = rows + groups[z, 80:96]
        state = jnp.where(far == z, carry, state)
    rows = rows + gathered[...]
    both = basis[near // 2]
    turned = pltpu.roll(both, 64, 1)
    odd = near % 2 == 1
    lane, row = cols_iota((16, 128)), rows_iota((16, 128))
    for_grad = jnp.where(odd, turned, both)
    for_value = jnp.where(odd, both, turned)
    right = jnp.where(
        row < 6,
        jnp.where(lane < 64, for_grad, 0.0),
        jnp.where(lane < 64, 0.0, for_value),
    )
    gathered[...] = jnp.zeros((NPOS, 128), f32)
    gathered[:, 0:16] = full_nt(rows, right)
    packed = gathered[0:8] + pltpu.roll(gathered[8:16], 16, 1)
    sends = []
    for b in range(15, -1, -1):
        out[b, 0:64] = state
        out[b, 64:72] = packed
        out[b, 72:88] = rows
        state = state * keep + later[b, 0:64]
        if b % 4 == 0:
            part = pl.ds(b, 4)
            send = pltpu.make_async_copy(out.at[part], out_far.at[part], sent.at[b // 4])
            send.start()
            sends.append(send)
    for send in sends:
        send.wait()


def forward_totals(rate, earlier, out):
    keep = powers(rate[near_place() // 2], jnp.full((64, 128), float(BLOCK), f32))
    state = earlier[0]
    for b in range(1, 16):
        state = state * keep + earlier[b]
    out[...] = state


def forward_carried(rate, earlier, one, two, three, out_far, out, sent):
    exponent = jnp.full((64, 128), float(BLOCK), f32)
    keep = powers(rate[near_place() // 2], exponent)
    keep_group = powers(rate[near_place() // 2], exponent * 16.0)
    state = (three[...] * keep_group + two[...]) * keep_group + one[...]
    sends = []
    for b in range(16):
        out[b] = state
        state = state * keep + earlier[b]
        if b % 4 == 3:
            part = pl.ds(b - 3, 4)
            send = pltpu.make_async_copy(out.at[part], out_far.at[part], sent.at[b // 4])
            send.start()
            sends.append(send)
    for send in sends:
        send.wait()


def sum_slices(x, out):
    total = x[0, 64:72]
    for i in range(1, 16):
        total = total + x[i, 64:72]
    lane = cols_iota((8, 128))
    out[0:8] = jnp.where(lane < 16, total, 0.0)
    out[8:16] = jnp.where(lane < 16, pltpu.roll(total, 112, 1), 0.0)


def products(head_sums, bias, x, parts):
    lane = cols_iota((NPOS, 128))
    sums = head_sums[...]
    turned = pltpu.roll(sums, 122, 1)
    code_grad = jnp.where(lane < 4, sums, 0.0)
    code = jnp.where(lane < 4, turned + bias[...], 0.0)
    both = code_grad + pltpu.roll(code, 4, 1)
    lane = cols_iota((4, 128))
    for i in range(16):
        got = full_tn(both, x[i, 72:88])
        parts[4 * i : 4 * i + 4] = jnp.where(lane < 64, got[4:8], got[0:4])
    along = (full_tn(code, sums) - full_tn(code_grad, turned))[0:4]
    total = jnp.broadcast_to(jnp.sum(code_grad, axis=0, keepdims=True), (4, 128))
    parts[64:68] = along
    parts[68:72] = total


def backward_rest(
    rate, positions, q, k, moved, grad, state, basis, head_sums, attended, grad_q, grad_k, grad_v
):
    between = rows_iota() - cols_iota()
    lower = between >= 0
    distance = jnp.maximum(between, 0).astype(f32)
    offset = rows_iota().astype(f32)
    select = selector(positions, block_start()).astype(bf16)
    select = jnp.concatenate([select, select, select], axis=0)
    code_grad = head_sums[...]
    for h in range(HEADS):
        c = head_cols(h)
        table = jnp.where(lower, powers(rate[h], distance), 0.0)
        leave = powers(rate[h], BLOCK - offset)
        high, low = split(jnp.concatenate([state[2 * h, 0:64], state[2 * h + 1, 0:64]], axis=0))
        qh, mh, kh, gh = q[:, c], moved[:, c], k[:, c], grad[:, c]
        mixing = (nt(qh, kh) * table).astype(bf16)
        grad_mixing = (nt(gh, mh) * table).astype(bf16)
        attended[:, c] = nn(mixing, mh)
        grad_q[:, c] = nn(grad_mixing, kh)
        inner = tn(grad_mixing, qh)
        grad_k[:, c] = (inner + leave * (nn(mh, high) + nn(mh, low))).astype(bf16)
        inner = tn(mixing, gh)
        lift = basis[h][6:10]
        fix = jnp.zeros((NPOS, SIZE), f32)
        for r in range(4):
            fix = fix + code_grad[:, r : r + 1] * lift[r : r + 1]
        out = inner + leave * (nt(kh, high) + nt(kh, low))
        grad_v[:, c] = (out + tn(select, third_terms(fix))).astype(bf16)


def forward_rest(
    rate, q, grad, state, attended_in, grad_q_in, small, ref, parts, others,
    attended, grad_q, grad_rotation, grad_weight, grad_bias,
):
    offset = rows_iota().astype(f32)
    i00, i01, i10, i11 = inverse_of(small)
    extra = parts[64:72] + others[64:72]
    a0, a1 = extra[0:4, 4:5], extra[0:4, 5:6]
    b0 = a0 * i00 + a1 * i10
    b1 = a0 * i01 + a1 * i11
    lane = cols_iota((4, 128))
    for h in range(HEADS):
        c = head_cols(h)
        enter = powers(rate[h], offset + 1.0)
        high, low = split(jnp.concatenate([state[2 * h], state[2 * h + 1]], axis=0))
        qh, gh = q[:, c], grad[:, c]
        attended[:, c] = (attended_in[:, c] + enter * (nt(qh, high) + nt(qh, low))).astype(bf16)
        grad_q[:, c] = (grad_q_in[:, c] + enter * (nn(gh, high) + nn(gh, low))).astype(bf16)
        both = parts[8 * h : 8 * h + 8] + others[8 * h : 8 * h + 8]
        turned = pltpu.roll(both, 64, 1)
        turn = jnp.where(lane < 64, both[0:4], turned[4:8])
        weight = jnp.where(lane < 64, turned[0:4], both[4:8])
        grad_weight[:, c] = weight
        grad_rotation[:, c] = turn - weight - b0 * ref[0:1, c] - b1 * ref[1:2, c]
    grad_bias[...] = extra[4, 0:4]


def call(kernel, specs, outs, scratch=(), far_outs=(), mib=8, flops=1e8, bytes_accessed=2e6):
    return pl.pallas_call(
        kernel,
        in_specs=[{"s": SMEM, "v": VMEM, "a": ANY}[s] for s in specs],
        out_specs=[ANY if n in far_outs else VMEM for n in range(len(outs))],
        out_shape=[jax.ShapeDtypeStruct(s, d) for s, d in outs],
        scratch_shapes=scratch,
        compiler_params=pltpu.CompilerParams(vmem_limit_bytes=mib * 1024 * 1024),
        cost_estimate=pl.CostEstimate(
            flops=int(flops), bytes_accessed=int(bytes_accessed), transcendentals=0
        ),
    )


def swap(x, axes):
    return lax.all_to_all(x, axes, 0, 0, tiled=False)


def ahead(x, d):
    return lax.ppermute(x, "zh", [(i, i + d) for i in range(4 - d)])


def shards(queries, key_rows, values, out_grad, rate, rotation, refusal, proj_weight, proj_bias, positions):
    q, k, v, grad = queries[0], key_rows[0], values[0], out_grad[0]
    ref = refusal.T
    bias = jnp.pad(proj_bias, (0, 124))[None, :]
    rows = (BLOCK, WIDE)
    tile = (NPOS, 128)

    def space(shape, dtype=f32):
        return pltpu.VMEM(shape, dtype)

    def marks(*shape):
        return pltpu.SemaphoreType.DMA(shape)

    grad_state, small = call(
        query_state,
        "ssaaaavvv",
        [((16, 96, 128), f32), ((24, 128), f32)],
        [space(rows, bf16)] * 4
        + [space((16, 96, 128)), space((NPOS, WIDE)), marks(4, 4), marks(HEADS)],
        (0,),
        mib=60,
    )(rate, positions, q, k, grad, v, rotation, ref, proj_weight)
    later = swap(grad_state, NEAR)
    small = lax.psum(small, "head")
    moved, state, basis = call(
        key_state,
        "ssvvvvvvv",
        [(rows, bf16), ((16, 64, 128), f32), ((HEADS, 16, 128), f32)],
        [space((16, 64, 128)), marks(HEADS)],
        (1,),
    )(rate, positions, small, v, k, rotation, ref, proj_weight, bias)
    state, later = lax.optimization_barrier((state, later))
    earlier = swap(state, NEAR)
    (own,) = call(backward_totals, "sv", [((96, 128), f32)], [space(tile)])(rate, later)
    groups = lax.all_gather(own, "zh")
    groups, earlier = lax.optimization_barrier((groups, earlier))
    (total,) = call(forward_totals, "sv", [((64, 128), f32)])(rate, earlier)
    passed = [ahead(total, d) for d in (2, 1, 3)]
    one, two, three = passed[1], passed[0], passed[2]
    (leaving,) = call(
        backward_carried,
        "svvv",
        [((16, 88, 128), f32)],
        [space((16, 88, 128)), space(tile), marks(4)],
        (0,),
    )(rate, later, groups, basis)
    leaving, total = lax.optimization_barrier((leaving, total))
    leaving = swap(leaving, NEAR)
    (entering,) = call(
        forward_carried,
        "svvvv",
        [((16, 64, 128), f32)],
        [space((16, 64, 128)), marks(4)],
        (0,),
    )(rate, earlier, one, two, three)
    (head_sums,) = call(sum_slices, "v", [(tile, f32)])(leaving)
    head_sums = lax.psum(head_sums, "head")
    entering, head_sums = lax.optimization_barrier((entering, head_sums))
    entering = swap(entering, NEAR)
    (parts,) = call(products, "vvv", [((72, 128), f32)])(head_sums, bias, leaving)
    others = lax.ppermute(parts, "dp", [(0, 1), (1, 0)])
    attended_in, grad_q_in, grad_k, grad_v = call(
        backward_rest, "ssvvvvvvv", [(rows, f32)] * 2 + [(rows, bf16)] * 2
    )(rate, positions, q, k, moved, grad, leaving, basis, head_sums)
    attended, grad_q, grad_rotation, grad_weight, grad_bias = call(
        forward_rest,
        "svvvvvvvvv",
        [(rows, bf16)] * 2 + [((4, WIDE), f32)] * 2 + [((4,), f32)],
    )(rate, q, grad, entering, attended_in, grad_q_in, small, ref, parts, others)
    return (
        attended[None],
        grad_q[None],
        grad_k[None],
        grad_v[None],
        grad_rotation,
        grad_weight,
        grad_bias,
    )


def solution(mesh):
    own = Mesh(mesh.devices.reshape(4, 4, 4, 4, 2), ("zh", "zl", "y", "head", "dp"))
    seq = ("zh", "zl", "y")
    stream = P("dp", seq, "head")
    return jax.shard_map(
        shards,
        mesh=own,
        in_specs=(
            stream,
            stream,
            stream,
            stream,
            P("head"),
            P(None, "head"),
            P("head", None),
            P(None, "head"),
            P(),
            P("dp", None),
        ),
        out_specs=(stream, stream, stream, stream, P(None, "head"), P(None, "head"), P()),
        check_vma=False,
    )
```

time: 141 us -> 130 us (0.922)
  the two profiles are of different devices: /device:TPU:1 before, /device:TPU:8 now
where the time goes in v3:
time: 130 us; the launch traced here: 129 us
  starting transfers between devices  50.9 us (39%)
  blocking collectives  50.4 us (39%)
  Pallas kernels  20.9 us (16%)
  waiting for transfers between devices  5.54 us (4%)
    all_to_all x4, starting transfers between devices, swap(): return lax.all_to_all(x, axes, 0, 0, tiled=False)  34.7 us
    all_gather x1, blocking collectives, shards(): groups = lax.all_gather(own, 'zh')  23.8 us
    psum x1, blocking collectives, shards(): small = lax.psum(small, 'head')  16.6 us
    ppermute x3, starting transfers between devices, ahead(): return lax.ppermute(x, 'zh', [(i, i + d) for i in range(4 - d)])  14.2 us
    psum x1, blocking collectives, shards(): head_sums = lax.psum(head_sums, 'head')  10 us
    pallas_call x1, Pallas kernels, shards(): call(query_state, 'ssaaaavvv', [((16, 96, 128), f32), ((24, 128), f32)],...  6.12 us
    all_to_all x4, waiting for transfers between devices, swap(): return lax.all_to_all(x, axes, 0, 0, tiled=False)  3.97 us
    pallas_call x1, Pallas kernels, shards(): call(backward_rest, 'ssvvvvvvv', [(rows, f32)] * 2 + [(rows, bf16)] * 2)  3.73 us
  transfers between devices with their start and end apart: 8, of which 3 were waited for; matrix products, arithmetic and copies ran while one was open for 0% of the time, Pallas kernels for 8%

profile of v3, /device:TPU:8, one launch (start us, length us, event | category | flops | bytes accessed | tf_op | source)
XLA Modules:
  0.0 129.3 jit_solution(935233288653344429)
XLA Ops:
  0.6 6.1 %shard_map.153 = (f32[16,96,128]{2,1,0:T(8,128)}, f32[24,128]{1,0:T(8,128)}) custom-call(f32[8]{0:T(128)} %rate.15, s32[1,16]{1,0:T(1,128)} %positions.5, bf16[128,1024]{1,0:T(8,128)(2,1)} %bitcast.12, bf16[128,1024]{1,0:T(8,128)(2,1)} %bitcast.18, bf16[128,1024]{1,0:T(8,128)(2,1)} %bitcast.15, bf16[128,1024]{1,0:T(8,128)(2,1)} %bitcast.21, f32[4,1024]{1,0:T(4,128)} %rot.3, ...), custom_call_target="tpu_custom_call" | custom-call | flops 100000000 | bytes 2000000 | tf_op jit(solution)/shard_map/pallas_call | solution.py:441
  6.8 0.0 copy-start.9
  6.8 0.0 copy-start.2
  6.8 0.0 copy-start.3
  6.8 0.0 copy-start.6
  6.8 9.4 %all-to-all-start = ((f32[16,96,128]{2,1,0:T(8,128)}), f32[16,96,128]{2,1,0:T(8,128)S(1)}, u32[]{:S(2)}, u32[]{:S(2)}) async-start(f32[16,96,128]{2,1,0:T(8,128)} %get-tuple-element.30), calls=%async_computation | async-start | bytes 1572864 | tf_op jit(solution)/shard_map/all_to_all | solution.py:421
  16.2 0.0 copy-start.5
  16.2 0.0 copy-done.9
  16.2 0.0 copy-start.10
  16.2 0.0 copy-start.4
  16.2 16.6 %psum.14.small = f32[24,128]{1,0:T(8,128)S(1)} all-reduce(f32[24,128]{1,0:T(8,128)S(1)} %copy-done.9), channel_id=1, replica_groups=mesh['zh'=4,'zl'=4,'y'=4,'head'=4,'dp'=2] {'head'}, use_global_device_ids=true, to_apply=%region_0.1 | all-reduce | flops 3072 | bytes 24576 | tf_op jit(solution)/shard_map/psum | solution.py:451
  32.8 0.0 copy-done.10
  32.9 0.0 copy-done.2
  32.9 0.0 copy-done.3
  32.9 0.0 copy-done.6
  32.9 0.0 copy-done.5
  32.9 0.0 copy-done.4
  32.9 0.6 copy-done.7
  33.5 0.0 copy-done.8
  33.5 2.7 %shard_map.154 = (bf16[128,1024]{1,0:T(8,128)(2,1)S(1)}, f32[16,64,128]{2,1,0:T(8,128)}, f32[8,16,128]{2,1,0:T(8,128)S(1)}) custom-call(f32[8]{0:T(128)S(1)} %copy-done.7, s32[1,16]{1,0:T(1,128)S(1)} %copy-done.8, f32[24,128]{1,0:T(8,128)S(1)} %psum.14.small, bf16[128,1024]{1,0:T(8,128)(2,1)S(1)} %bitcast.22, bf16[128,1024]{1,0:T(8,128)(2,1)S(1)} %bitcast.19, ...), custom_call_target="tpu_custom_call" | custom-call | flops 100000000 | bytes 2000000 | tf_op jit(solution)/shard_map/pallas_call | solution.py:452
  36.2 0.0 all-to-all-done.later
  36.2 7.5 %all-to-all-start.1 = ((f32[16,64,128]{2,1,0:T(8,128)}), f32[16,64,128]{2,1,0:T(8,128)S(1)}, u32[]{:S(2)}, u32[]{:S(2)}) async-start(f32[16,64,128]{2,1,0:T(8,128)} %get-tuple-element.32), calls=%async_computation.1 | async-start | bytes 1048576 | tf_op jit(solution)/shard_map/all_to_all | solution.py:421
  43.7 1.1 shard_map.155
  44.8 23.8 %all-gather = f32[384,128]{1,0:T(8,128)S(1)} all-gather(f32[96,128]{1,0:T(8,128)S(1)} %shard_map.155), channel_id=2, replica_groups=mesh['zh'=4,'zl'=4,'y'=4,'head'=4,'dp'=2] {'zh'}, dimensions={0}, use_global_device_ids=true | all-gather | bytes 245760 | tf_op jit(solution)/shard_map/all_gather | solution.py:462
  68.6 0.0 all-to-all-done.1.earlier
  68.6 0.6 shard_map.156
  69.2 1.9 %shard_map.158 = f32[16,88,128]{2,1,0:T(8,128)} custom-call(f32[8]{0:T(128)S(1)} %copy-done.7, f32[16,96,128]{2,1,0:T(8,128)S(1)} %all-to-all-done.later, f32[4,96,128]{2,1,0:T(8,128)S(1)} %bitcast.23, f32[8,16,128]{2,1,0:T(8,128)S(1)} %get-tuple-element.35.basis), custom_call_target="tpu_custom_call" | custom-call | flops 100000000 | bytes 2000000 | tf_op jit(solution)/shard_map/pallas_call | solution.py:467
  71.1 10.7 %all-to-all-start.2 = ((f32[16,88,128]{2,1,0:T(8,128)}), f32[16,88,128]{2,1,0:T(8,128)S(1)}, u32[]{:S(2)}, u32[]{:S(2)}) async-start(f32[16,88,128]{2,1,0:T(8,128)} %shard_map.158), calls=%async_computation.2 | async-start | bytes 1441792 | tf_op jit(solution)/shard_map/all_to_all | solution.py:421
  81.8 5.7 %collective-permute-start = (f32[64,128]{1,0:T(8,128)S(1)}, f32[64,128]{1,0:T(8,128)S(1)}, u32[]{:S(2)}, u32[]{:S(2)}) collective-permute-start(f32[64,128]{1,0:T(8,128)S(1)} %shard_map.156), channel_id=1, source_target_pairs={{0,128},{128,256},{256,384},{1,129},{129,257},{257,385},{2,130},{1... | collective-permute-start | bytes 98312 | tf_op jit(solution)/shard_map/ppermute | solution.py:425
  87.6 7.2 %collective-permute-start.1 = (f32[64,128]{1,0:T(8,128)S(1)}, f32[64,128]{1,0:T(8,128)S(1)}, u32[]{:S(2)}, u32[]{:S(2)}) collective-permute-start(f32[64,128]{1,0:T(8,128)S(1)} %shard_map.156), channel_id=1, source_target_pairs={{0,256},{128,384},{1,257},{129,385},{2,258},{130,386},{3,259},{131... | collective-permute-start | bytes 98312 | tf_op jit(solution)/shard_map/ppermute | solution.py:425
  94.8 1.3 collective-permute-start.2
  96.1 0.0 collective-permute-done.one
  96.1 0.3 collective-permute-done.1.two
  96.4 1.3 %collective-permute-done.2.three = f32[64,128]{1,0:T(8,128)S(1)} collective-permute-done((f32[64,128]{1,0:T(8,128)S(1)}, f32[64,128]{1,0:T(8,128)S(1)}, u32[]{:S(2)}, u32[]{:S(2)}) %collective-permute-start.2) | collective-permute-done | bytes 32800 | tf_op jit(solution)/shard_map/ppermute | solution.py:425
  97.7 1.4 %shard_map.157 = f32[16,64,128]{2,1,0:T(8,128)} custom-call(f32[8]{0:T(128)S(1)} %copy-done.7, f32[16,64,128]{2,1,0:T(8,128)S(1)} %all-to-all-done.1.earlier, f32[64,128]{1,0:T(8,128)S(1)} %collective-permute-done.one, f32[64,128]{1,0:T(8,128)S(1)} %collective-permute-done.1.two, f32[64,128]{1,0:T(8,128)S(1)} %collective-permute-done.2.three), custom_call_target="tpu_custom_call" | custom-call | flops 100000000 | bytes 2000000 | tf_op jit(solution)/shard_map/pallas_call | solution.py:476
  99.1 0.0 all-to-all-done.2.x.state
  99.1 0.1 shard_map.159
  99.2 10.0 %psum.15.head_sums = f32[16,128]{1,0:T(8,128)S(1)} all-reduce(f32[16,128]{1,0:T(8,128)S(1)} %shard_map.159), channel_id=1, replica_groups=mesh['zh'=4,'zl'=4,'y'=4,'head'=4,'dp'=2] {'head'}, use_global_device_ids=true, to_apply=%region_1.2 | all-reduce | flops 2048 | bytes 16384 | tf_op jit(solution)/shard_map/psum | solution.py:484
  109.2 7.1 %all-to-all-start.3 = ((f32[16,64,128]{2,1,0:T(8,128)}), f32[16,64,128]{2,1,0:T(8,128)S(1)}, u32[]{:S(2)}, u32[]{:S(2)}) async-start(f32[16,64,128]{2,1,0:T(8,128)} %shard_map.157), calls=%async_computation.3 | async-start | bytes 1048576 | tf_op jit(solution)/shard_map/all_to_all | solution.py:421
  116.4 0.0 copy-start.1
  116.4 1.3 shard_map.161.parts
  117.7 1.9 %collective-permute-start.3 = (f32[72,128]{1,0:T(8,128)S(1)}, f32[72,128]{1,0:T(8,128)S(1)}, u32[]{:S(2)}, u32[]{:S(2)}) collective-permute-start(f32[72,128]{1,0:T(8,128)S(1)} %shard_map.161.parts), channel_id=1, source_target_pairs={{0,1},{1,0},{2,3},{3,2},{4,5},{5,4},{6,7},{7,6},{8,9},{9,8},{10,11... | collective-permute-start | bytes 110600 | tf_op jit(solution)/shard_map/ppermute | solution.py:488
  119.6 0.0 copy-done
  119.6 0.0 copy-done.1
  119.6 3.7 %shard_map.160 = (f32[128,1024]{1,0:T(8,128)S(1)}, f32[128,1024]{1,0:T(8,128)S(1)}, bf16[128,1024]{1,0:T(8,128)(2,1)}, bf16[128,1024]{1,0:T(8,128)(2,1)}) custom-call(f32[8]{0:T(128)S(1)} %copy-done.7, s32[1,16]{1,0:T(1,128)S(1)} %copy-done.8, bf16[128,1024]{1,0:T(8,128)(2,1)S(1)} %bitcast.13, bf16[128,1024]{1,0:T(8,128)(2,1)S(1)} %bitcast.20, ...), custom_call_target="tpu_custom_call" | custom-call | flops 100000000 | bytes 2000000 | tf_op jit(solution)/shard_map/pallas_call | solution.py:489
  123.3 0.0 collective-permute-done.3.others
  123.3 4.0 %all-to-all-done.3.state = f32[16,64,128]{2,1,0:T(8,128)S(1)} async-done(((f32[16,64,128]{2,1,0:T(8,128)}), f32[16,64,128]{2,1,0:T(8,128)S(1)}, u32[]{:S(2)}, u32[]{:S(2)}) %all-to-all-start.3) | async-done | bytes 524320 | tf_op jit(solution)/shard_map/all_to_all | solution.py:421
  127.3 2.0 %shard_map.162 = (bf16[128,1024]{1,0:T(8,128)(2,1)}, bf16[128,1024]{1,0:T(8,128)(2,1)}, f32[4,1024]{1,0:T(4,128)}, f32[4,1024]{1,0:T(4,128)}, f32[4]{0:T(128)}) custom-call(f32[8]{0:T(128)S(1)} %copy-done.7, bf16[128,1024]{1,0:T(8,128)(2,1)S(1)} %bitcast.14, bf16[128,1024]{1,0:T(8,128)(2,1)S(1)} %bitcast.17, f32[16,64,128]{2,1,0:T(8,128)S(1)} %all-to-all-done.3.state, ...), custom_call_target="tpu_custom_call" | custom-call | flops 100000000 | bytes 2000000 | tf_op jit(solution)/shard_map/pallas_call | solution.py:492
  (4 shorter events, 0.0 us)
Async XLA Ops:
  6.8 9.4 %copy-start.9 = (f32[24,128]{1,0:T(8,128)S(1)}, f32[24,128]{1,0:T(8,128)}, u32[]{:S(2)}) copy-start(f32[24,128]{1,0:T(8,128)} %get-tuple-element.28) | copy-start | bytes 36868
  6.8 26.1 %copy-start.2 = (bf16[1,128,1024]{2,1,0:T(8,128)(2,1)S(1)}, bf16[1,128,1024]{2,1,0:T(8,128)(2,1)}, u32[]{:S(2)}) copy-start(bf16[1,128,1024]{2,1,0:T(8,128)(2,1)} %param.11) | copy-start | bytes 786436
  6.8 26.1 %copy-start.3 = (bf16[1,128,1024]{2,1,0:T(8,128)(2,1)S(1)}, bf16[1,128,1024]{2,1,0:T(8,128)(2,1)}, u32[]{:S(2)}) copy-start(bf16[1,128,1024]{2,1,0:T(8,128)(2,1)} %param.12) | copy-start | bytes 786436
  6.8 26.1 %copy-start.6 = (f32[4,1024]{1,0:T(4,128)S(1)}, f32[4,1024]{1,0:T(4,128)}, u32[]{:S(2)}) copy-start(f32[4,1024]{1,0:T(4,128)} %proj.3) | copy-start | bytes 49156
  6.8 29.4 %all-to-all-start = ((f32[16,96,128]{2,1,0:T(8,128)}), f32[16,96,128]{2,1,0:T(8,128)S(1)}, u32[]{:S(2)}, u32[]{:S(2)}) async-start(f32[16,96,128]{2,1,0:T(8,128)} %get-tuple-element.30), calls=%async_computation | async-start | bytes 1572864 | tf_op jit(solution)/shard_map/all_to_all | solution.py:421
  16.2 16.7 %copy-start.5 = (f32[4,1024]{1,0:T(4,128)S(1)}, f32[4,1024]{1,0:T(4,128)}, u32[]{:S(2)}) copy-start(f32[4,1024]{1,0:T(4,128)} %rot.3) | copy-start | bytes 49156
  16.2 16.6 %copy-start.10 = (f32[4]{0:T(128)S(1)}, f32[4]{0:T(128)}, u32[]{:S(2)}) copy-start(f32[4]{0:T(128)} %param.18) | copy-start | bytes 52
  16.2 16.7 %copy-start.4 = (f32[1024,2]{0,1:T(2,128)S(1)}, f32[1024,2]{0,1:T(2,128)}, u32[]{:S(2)}) copy-start(f32[1024,2]{0,1:T(2,128)} %param.16) | copy-start | bytes 24580
  32.8 0.7 copy-start.7
  32.8 0.7 copy-start.8
  36.2 32.4 %all-to-all-start.1 = ((f32[16,64,128]{2,1,0:T(8,128)}), f32[16,64,128]{2,1,0:T(8,128)S(1)}, u32[]{:S(2)}, u32[]{:S(2)}) async-start(f32[16,64,128]{2,1,0:T(8,128)} %get-tuple-element.32), calls=%async_computation.1 | async-start | bytes 1048576 | tf_op jit(solution)/shard_map/all_to_all | solution.py:421
  71.1 28.0 %all-to-all-start.2 = ((f32[16,88,128]{2,1,0:T(8,128)}), f32[16,88,128]{2,1,0:T(8,128)S(1)}, u32[]{:S(2)}, u32[]{:S(2)}) async-start(f32[16,88,128]{2,1,0:T(8,128)} %shard_map.158), calls=%async_computation.2 | async-start | bytes 1441792 | tf_op jit(solution)/shard_map/all_to_all | solution.py:421
  81.8 14.3 %collective-permute-start = (f32[64,128]{1,0:T(8,128)S(1)}, f32[64,128]{1,0:T(8,128)S(1)}, u32[]{:S(2)}, u32[]{:S(2)}) collective-permute-start(f32[64,128]{1,0:T(8,128)S(1)} %shard_map.156), channel_id=1, source_target_pairs={{0,128},{128,256},{256,384},{1,129},{129,257},{257,385},{2,130},{1... | collective-permute-start | bytes 98312 | tf_op jit(solution)/shard_map/ppermute | solution.py:425
  87.6 8.8 %collective-permute-start.1 = (f32[64,128]{1,0:T(8,128)S(1)}, f32[64,128]{1,0:T(8,128)S(1)}, u32[]{:S(2)}, u32[]{:S(2)}) collective-permute-start(f32[64,128]{1,0:T(8,128)S(1)} %shard_map.156), channel_id=1, source_target_pairs={{0,256},{128,384},{1,257},{129,385},{2,258},{130,386},{3,259},{131... | collective-permute-start | bytes 98312 | tf_op jit(solution)/shard_map/ppermute | solution.py:425
  94.8 2.9 %collective-permute-start.2 = (f32[64,128]{1,0:T(8,128)S(1)}, f32[64,128]{1,0:T(8,128)S(1)}, u32[]{:S(2)}, u32[]{:S(2)}) collective-permute-start(f32[64,128]{1,0:T(8,128)S(1)} %shard_map.156), channel_id=1, source_target_pairs={{0,384},{1,385},{2,386},{3,387},{4,388},{5,389},{6,390},{7,391},{8... | collective-permute-start | bytes 98312 | tf_op jit(solution)/shard_map/ppermute | solution.py:425
  109.2 18.1 %all-to-all-start.3 = ((f32[16,64,128]{2,1,0:T(8,128)}), f32[16,64,128]{2,1,0:T(8,128)S(1)}, u32[]{:S(2)}, u32[]{:S(2)}) async-start(f32[16,64,128]{2,1,0:T(8,128)} %shard_map.157), calls=%async_computation.3 | async-start | bytes 1048576 | tf_op jit(solution)/shard_map/all_to_all | solution.py:421
  116.4 3.2 %copy-start = (bf16[1,128,1024]{2,1,0:T(8,128)(2,1)S(1)}, bf16[1,128,1024]{2,1,0:T(8,128)(2,1)}, u32[]{:S(2)}) copy-start(bf16[1,128,1024]{2,1,0:T(8,128)(2,1)} %param.10) | copy-start | bytes 786436
  116.4 3.2 %copy-start.1 = (bf16[1,128,1024]{2,1,0:T(8,128)(2,1)S(1)}, bf16[1,128,1024]{2,1,0:T(8,128)(2,1)}, u32[]{:S(2)}) copy-start(bf16[1,128,1024]{2,1,0:T(8,128)(2,1)} %param.13) | copy-start | bytes 786436
  117.7 5.7 %collective-permute-start.3 = (f32[72,128]{1,0:T(8,128)S(1)}, f32[72,128]{1,0:T(8,128)S(1)}, u32[]{:S(2)}, u32[]{:S(2)}) collective-permute-start(f32[72,128]{1,0:T(8,128)S(1)} %shard_map.161.parts), channel_id=1, source_target_pairs={{0,1},{1,0},{2,3},{3,2},{4,5},{5,4},{6,7},{7,6},{8,9},{9,8},{10,11... | collective-permute-start | bytes 110600 | tf_op jit(solution)/shard_map/ppermute | solution.py:488

commit v4 on v3

--- a/solution.py
+++ b/solution.py
@@ -55,8 +55,8 @@
     return -rate * total
 
 
-def powers(rate, exponents):
-    return jnp.exp(exponents * log_keep(rate))
+def powers(logs, head, exponents):
+    return jnp.exp(exponents * logs[pl.ds(head, 1), :])
 
 
 def rows_iota(shape=(BLOCK, SIZE)):
@@ -87,8 +87,8 @@
     return wanted - start
 
 
-def selector(positions, start):
-    return (local_places(positions, start) == cols_iota((NPOS, BLOCK))).astype(f32)
+def selector(places):
+    return (places[...] == cols_iota((NPOS, BLOCK))).astype(bf16)
 
 
 def head_cols(h):
@@ -108,56 +108,67 @@
 
 
 def query_state(
-    rate, positions, q_far, k_far, grad_far, v_far, rot, ref, proj, out_far, small,
-    q, k, grad, v, out, chosen, arrived, sent,
+    rate, positions, q_far, k_far, grad_far, v_far, rot, ref, proj,
+    out_far, small, logs, places_out, q, k, grad, v, out, arrived, sent,
 ):
     fetches = []
-    for part in range(4):
-        c = slice(part * 2 * SIZE, (part + 1) * 2 * SIZE)
-        pairs = ((q_far, q), (grad_far, grad), (k_far, k), (v_far, v))
-        for n, (src, dst) in enumerate(pairs):
-            fetch = pltpu.make_async_copy(src.at[:, c], dst.at[:, c], arrived.at[part, n])
-            fetch.start()
-            fetches.append(fetch)
+    for n, (src, dst) in enumerate(((q_far, q), (grad_far, grad), (k_far, k), (v_far, v))):
+        fetch = pltpu.make_async_copy(src, dst, arrived.at[n])
+        fetch.start()
+        fetches.append(fetch)
     sends = []
-    offset = rows_iota().astype(f32)
+
+    def send(h, start, rows):
+        here = (pl.ds(2 * h, 2), pl.ds(start, rows))
+        copy = pltpu.make_async_copy(out.at[here], out_far.at[here], sent.at[len(sends)])
+        copy.start()
+        sends.append(copy)
+
+    for h in range(HEADS):
+        logs[h : h + 1, :] = jnp.full((1, 128), log_keep(rate[h]), f32)
     places = local_places(positions, block_start())
+    places_out[...] = places
     lane = cols_iota((NPOS, BLOCK))
     select = (places == lane).astype(bf16)
     after = lane - places
     reached = after >= 0
     distance = jnp.maximum(after, 0).astype(f32)
     leave = jnp.clip(BLOCK - places, 0, BLOCK).astype(f32)
+    tables = [jnp.where(reached, powers(logs, h, distance), 0.0) for h in range(HEADS)]
+    offset = rows_iota().astype(f32)
+    for fetch in fetches[:2]:
+        fetch.wait()
     for h in range(HEADS):
         c = head_cols(h)
-        if h % 2 == 0:
-            for fetch in fetches[2 * h : 2 * h + 4]:
-                fetch.wait()
-        chosen[:, c] = nn(select, v[:, c])
-        weighted = q[:, c].astype(f32) * powers(rate[h], offset)
+        weighted = q[:, c].astype(f32) * powers(logs, h, offset)
         state = decayed_state(weighted, grad[:, c])
-        key = nn(select, k[:, c])
-        table = jnp.where(reached, powers(rate[h], distance), 0.0)
-        mixing = (nt(key.astype(bf16), q[:, c]) * table).astype(bf16)
-        local = nn(mixing, grad[:, c])
-        key = key * powers(rate[h], leave)
+        out[2 * h, 0:64] = state[:64]
+        out[2 * h + 1, 0:64] = state[64:]
+        send(h, 0, 64)
+    for fetch in fetches[2:]:
+        fetch.wait()
+    keys = nn(select, k[...])
+    chosen = nn(select, v[...])
+    low = keys.astype(bf16)
+    scores = [nt(low[:, head_cols(h)], q[:, head_cols(h)]) for h in range(HEADS)]
+    mixing = [(scores[h] * tables[h]).astype(bf16) for h in range(HEADS)]
+    local = [nn(mixing[h], grad[:, head_cols(h)]) for h in range(HEADS)]
+    for h in range(HEADS):
+        c = head_cols(h)
+        key = keys[:, c] * powers(logs, h, leave)
         for odd in range(2):
             i = 2 * h + odd
-            out[i, 0:64] = state[64 * odd : 64 * odd + 64]
             out[i, 64:80] = key
-            out[i, 80:96] = halves(local, chosen[:, c], odd)
-        part = pl.ds(2 * h, 2)
-        send = pltpu.make_async_copy(out.at[part], out_far.at[part], sent.at[h])
-        send.start()
-        sends.append(send)
-    left = jnp.concatenate([chosen[...], ref[...], rot[...], jnp.zeros((2, WIDE), f32)], axis=0)
+            out[i, 80:96] = halves(local[h], chosen[:, c], odd)
+        send(h, 64, 32)
+    left = jnp.concatenate([chosen, ref[...], rot[...], jnp.zeros((2, WIDE), f32)], axis=0)
     right = jnp.concatenate(
         [proj[...] - rot[...], ref[...], rot[...], jnp.zeros((6, WIDE), f32)], axis=0
     )
     small[...] = jnp.zeros((24, 128), f32)
     small[:, 0:16] = full_nt(left, right)
-    for send in sends:
-        send.wait()
+    for copy in sends:
+        copy.wait()
 
 
 def inverse_of(small):
@@ -176,7 +187,7 @@
 
 
 def key_state(
-    rate, positions, small, v, k, rot, ref, proj, bias, moved, state_far, basis, state, sent
+    logs, places, small, v, k, rot, ref, proj, bias, moved, state_far, basis, state, sent
 ):
     i00, i01, i10, i11 = inverse_of(small)
     c0, c1 = small[18:22, 4:5], small[18:22, 5:6]
@@ -201,7 +212,7 @@
     shift = jnp.zeros((NPOS, WIDE), f32)
     for r in range(4):
         shift = shift + full[:, r : r + 1] * rotated[r : r + 1, :]
-    select = selector(positions, block_start()).astype(bf16)
+    select = selector(places)
     select = jnp.concatenate([select, select, select], axis=0)
     shift = third_terms(shift)
     offset = rows_iota().astype(f32)
@@ -211,7 +222,7 @@
         basis[h] = rows[:, c]
         new = (v[:, c].astype(f32) + tn(select, shift[:, c])).astype(bf16)
         moved[:, c] = new
-        weighted = k[:, c].astype(f32) * powers(rate[h], BLOCK - 1.0 - offset)
+        weighted = k[:, c].astype(f32) * powers(logs, h, BLOCK - 1.0 - offset)
         out = decayed_state(weighted, new)
         state[2 * h] = out[:64]
         state[2 * h + 1] = out[64:]
@@ -229,8 +240,8 @@
     return nt(ah, bh) + (nt(al, bh) + nt(ah, bl))
 
 
-def backward_totals(rate, later, out, gathered):
-    keep = powers(rate[near_place() // 2], jnp.full((64, 128), float(BLOCK), f32))
+def backward_totals(logs, later, out, gathered):
+    keep = powers(logs, near_place() // 2, jnp.full((64, 128), float(BLOCK), f32))
     keep_key = keep[0:NPOS]
     state = later[15, 0:64]
     key = later[0, 64:80]
@@ -248,12 +259,12 @@
 
 
 def backward_carried(
-    rate, later, groups, basis, out_far, out, gathered, sent
+    logs, later, groups, basis, out_far, out, gathered, sent
 ):
     far, near = far_place(), near_place()
     exponent = jnp.full((64, 128), float(BLOCK), f32)
-    keep = powers(rate[near // 2], exponent)
-    keep_group = powers(rate[near // 2], exponent * 16.0)
+    keep = powers(logs, near // 2, exponent)
+    keep_group = powers(logs, near // 2, exponent * 16.0)
     rows = groups[3, 80:96]
     gathered[...] = jnp.zeros((NPOS, 128), f32)
     carry = jnp.zeros((64, 128), f32)
@@ -293,18 +304,18 @@
         send.wait()
 
 
-def forward_totals(rate, earlier, out):
-    keep = powers(rate[near_place() // 2], jnp.full((64, 128), float(BLOCK), f32))
+def forward_totals(logs, earlier, out):
+    keep = powers(logs, near_place() // 2, jnp.full((64, 128), float(BLOCK), f32))
     state = earlier[0]
     for b in range(1, 16):
         state = state * keep + earlier[b]
     out[...] = state
 
 
-def forward_carried(rate, earlier, one, two, three, out_far, out, sent):
+def forward_carried(logs, earlier, one, two, three, out_far, out, sent):
     exponent = jnp.full((64, 128), float(BLOCK), f32)
-    keep = powers(rate[near_place() // 2], exponent)
-    keep_group = powers(rate[near_place() // 2], exponent * 16.0)
+    keep = powers(logs, near_place() // 2, exponent)
+    keep_group = powers(logs, near_place() // 2, exponent * 16.0)
     state = (three[...] * keep_group + two[...]) * keep_group + one[...]
     sends = []
     for b in range(16):
@@ -346,19 +357,19 @@
 
 
 def backward_rest(
-    rate, positions, q, k, moved, grad, state, basis, head_sums, attended, grad_q, grad_k, grad_v
+    logs, places, q, k, moved, grad, state, basis, head_sums, attended, grad_q, grad_k, grad_v
 ):
     between = rows_iota() - cols_iota()
     lower = between >= 0
     distance = jnp.maximum(between, 0).astype(f32)
     offset = rows_iota().astype(f32)
-    select = selector(positions, block_start()).astype(bf16)
+    select = selector(places)
     select = jnp.concatenate([select, select, select], axis=0)
     code_grad = head_sums[...]
     for h in range(HEADS):
         c = head_cols(h)
-        table = jnp.where(lower, powers(rate[h], distance), 0.0)
-        leave = powers(rate[h], BLOCK - offset)
+        table = jnp.where(lower, powers(logs, h, distance), 0.0)
+        leave = powers(logs, h, BLOCK - offset)
         high, low = split(jnp.concatenate([state[2 * h, 0:64], state[2 * h + 1, 0:64]], axis=0))
         qh, mh, kh, gh = q[:, c], moved[:, c], k[:, c], grad[:, c]
         mixing = (nt(qh, kh) * table).astype(bf16)
@@ -377,9 +388,10 @@
 
 
 def forward_rest(
-    rate, q, grad, state, attended_in, grad_q_in, small, ref, parts, others,
-    attended, grad_q, grad_rotation, grad_weight, grad_bias,
+    logs, q, grad, state, attended_in, grad_q_in, small, ref, parts, others,
+    attended_far, grad_q_far, grad_rotation, grad_weight, grad_bias, attended, grad_q, sent,
 ):
+    sends = []
     offset = rows_iota().astype(f32)
     i00, i01, i10, i11 = inverse_of(small)
     extra = parts[64:72] + others[64:72]
@@ -389,11 +401,18 @@
     lane = cols_iota((4, 128))
     for h in range(HEADS):
         c = head_cols(h)
-        enter = powers(rate[h], offset + 1.0)
+        enter = powers(logs, h, offset + 1.0)
         high, low = split(jnp.concatenate([state[2 * h], state[2 * h + 1]], axis=0))
         qh, gh = q[:, c], grad[:, c]
         attended[:, c] = (attended_in[:, c] + enter * (nt(qh, high) + nt(qh, low))).astype(bf16)
         grad_q[:, c] = (grad_q_in[:, c] + enter * (nn(gh, high) + nn(gh, low))).astype(bf16)
+        if h % 2 == 1:
+            wide = slice((h - 1) * SIZE, (h + 1) * SIZE)
+            pairs = ((attended, attended_far), (grad_q, grad_q_far))
+            for n, (src, dst) in enumerate(pairs):
+                copy = pltpu.make_async_copy(src.at[:, wide], dst.at[:, wide], sent.at[h // 2, n])
+                copy.start()
+                sends.append(copy)
         both = parts[8 * h : 8 * h + 8] + others[8 * h : 8 * h + 8]
         turned = pltpu.roll(both, 64, 1)
         turn = jnp.where(lane < 64, both[0:4], turned[4:8])
@@ -401,6 +420,8 @@
         grad_weight[:, c] = weight
         grad_rotation[:, c] = turn - weight - b0 * ref[0:1, c] - b1 * ref[1:2, c]
     grad_bias[...] = extra[4, 0:4]
+    for copy in sends:
+        copy.wait()
 
 
 def call(kernel, specs, outs, scratch=(), far_outs=(), mib=8, flops=1e8, bytes_accessed=2e6):
@@ -438,12 +459,11 @@
     def marks(*shape):
         return pltpu.SemaphoreType.DMA(shape)
 
-    grad_state, small = call(
+    grad_state, small, logs, places = call(
         query_state,
         "ssaaaavvv",
-        [((16, 96, 128), f32), ((24, 128), f32)],
-        [space(rows, bf16)] * 4
-        + [space((16, 96, 128)), space((NPOS, WIDE)), marks(4, 4), marks(HEADS)],
+        [((16, 96, 128), f32), ((24, 128), f32), ((8, 128), f32), (tile, jnp.int32)],
+        [space(rows, bf16)] * 4 + [space((16, 96, 128)), marks(4), marks(2 * HEADS)],
         (0,),
         mib=60,
     )(rate, positions, q, k, grad, v, rotation, ref, proj_weight)
@@ -451,35 +471,35 @@
     small = lax.psum(small, "head")
     moved, state, basis = call(
         key_state,
-        "ssvvvvvvv",
+        "vvvvvvvvv",
         [(rows, bf16), ((16, 64, 128), f32), ((HEADS, 16, 128), f32)],
         [space((16, 64, 128)), marks(HEADS)],
         (1,),
-    )(rate, positions, small, v, k, rotation, ref, proj_weight, bias)
+    )(logs, places, small, v, k, rotation, ref, proj_weight, bias)
     state, later = lax.optimization_barrier((state, later))
     earlier = swap(state, NEAR)
-    (own,) = call(backward_totals, "sv", [((96, 128), f32)], [space(tile)])(rate, later)
+    (own,) = call(backward_totals, "vv", [((96, 128), f32)], [space(tile)])(logs, later)
     groups = lax.all_gather(own, "zh")
     groups, earlier = lax.optimization_barrier((groups, earlier))
-    (total,) = call(forward_totals, "sv", [((64, 128), f32)])(rate, earlier)
+    (total,) = call(forward_totals, "vv", [((64, 128), f32)])(logs, earlier)
     passed = [ahead(total, d) for d in (2, 1, 3)]
     one, two, three = passed[1], passed[0], passed[2]
     (leaving,) = call(
         backward_carried,
-        "svvv",
+        "vvvv",
         [((16, 88, 128), f32)],
         [space((16, 88, 128)), space(tile), marks(4)],
         (0,),
-    )(rate, later, groups, basis)
+    )(logs, later, groups, basis)
     leaving, total = lax.optimization_barrier((leaving, total))
     leaving = swap(leaving, NEAR)
     (entering,) = call(
         forward_carried,
-        "svvvv",
+        "vvvvv",
         [((16, 64, 128), f32)],
         [space((16, 64, 128)), marks(4)],
         (0,),
-    )(rate, earlier, one, two, three)
+    )(logs, earlier, one, two, three)
     (head_sums,) = call(sum_slices, "v", [(tile, f32)])(leaving)
     head_sums = lax.psum(head_sums, "head")
     entering, head_sums = lax.optimization_barrier((entering, head_sums))
@@ -487,13 +507,15 @@
     (parts,) = call(products, "vvv", [((72, 128), f32)])(head_sums, bias, leaving)
     others = lax.ppermute(parts, "dp", [(0, 1), (1, 0)])
     attended_in, grad_q_in, grad_k, grad_v = call(
-        backward_rest, "ssvvvvvvv", [(rows, f32)] * 2 + [(rows, bf16)] * 2
-    )(rate, positions, q, k, moved, grad, leaving, basis, head_sums)
+        backward_rest, "vvvvvvvvv", [(rows, f32)] * 2 + [(rows, bf16)] * 2
+    )(logs, places, q, k, moved, grad, leaving, basis, head_sums)
     attended, grad_q, grad_rotation, grad_weight, grad_bias = call(
         forward_rest,
-        "svvvvvvvvv",
+        "vvvvvvvvvv",
         [(rows, bf16)] * 2 + [((4, WIDE), f32)] * 2 + [((4,), f32)],
-    )(rate, q, grad, entering, attended_in, grad_q_in, small, ref, parts, others)
+        [space(rows, bf16)] * 2 + [marks(4, 2)],
+        (0, 1),
+    )(logs, q, grad, entering, attended_in, grad_q_in, small, ref, parts, others)
     return (
         attended[None],
         grad_q[None],

time: 130 us -> 127 us (0.977)
  Pallas kernels: 20.9 us -> 15.7 us
    pallas_call x8, Pallas kernels: 19.5 us -> 14.3 us  [the longest x1 4.25 us: shards(): call(query_state, 'ssaaaavvv', [((16, 96, 128), f32), ((24, 128), f32), (...]
  transfers between devices with their start and end apart: 8 -> 8, of which waited for: 3 -> 3; matrix products, arithmetic and copies ran while one was open for 0% -> 0% of each run, Pallas kernels for 8% -> 6%
where the time goes in v4:
time: 127 us; the launch traced here: 126 us
  blocking collectives  51.5 us (41%)
  starting transfers between devices  50.9 us (40%)
  Pallas kernels  15.7 us (12%)
  waiting for transfers between devices  6.07 us (5%)
    all_to_all x4, starting transfers between devices, swap(): return lax.all_to_all(x, axes, 0, 0, tiled=False)  35.4 us
    all_gather x1, blocking collectives, shards(): groups = lax.all_gather(own, 'zh')  24.3 us
    psum x1, blocking collectives, shards(): small = lax.psum(small, 'head')  16.6 us
    ppermute x3, starting transfers between devices, ahead(): return lax.ppermute(x, 'zh', [(i, i + d) for i in range(4 - d)])  13.6 us
    psum x1, blocking collectives, shards(): head_sums = lax.psum(head_sums, 'head')  10.5 us
    all_to_all x4, waiting for transfers between devices, swap(): return lax.all_to_all(x, axes, 0, 0, tiled=False)  4.49 us
    pallas_call x1, Pallas kernels, shards(): call(query_state, 'ssaaaavvv', [((16, 96, 128), f32), ((24, 128), f32), (...  4.25 us
    pallas_call x1, Pallas kernels, shards(): call(backward_rest, 'vvvvvvvvv', [(rows, f32)] * 2 + [(rows, bf16)] * 2)  3.2 us
  transfers between devices with their start and end apart: 8, of which 3 were waited for; matrix products, arithmetic and copies ran while one was open for 0% of the time, Pallas kernels for 6%

profile of v4, /device:TPU:8, one launch (start us, length us, event | category | flops | bytes accessed | tf_op | source)
XLA Modules:
  0.0 125.8 jit_solution(2183805904950177781)
XLA Ops:
  0.6 4.2 %shard_map.153 = (f32[16,96,128]{2,1,0:T(8,128)}, f32[24,128]{1,0:T(8,128)}, f32[8,128]{1,0:T(8,128)}, s32[16,128]{1,0:T(8,128)}) custom-call(f32[8]{0:T(128)} %rate.1, s32[1,16]{1,0:T(1,128)} %positions.1, bf16[128,1024]{1,0:T(8,128)(2,1)} %bitcast.12, bf16[128,1024]{1,0:T(8,128)(2,1)} %bitcast.18, bf16[128,1024]{1,0:T(8,128)(2,1)} %bitcast.15, ...), custom_call_target="tpu_custom_call" | custom-call | flops 100000000 | bytes 2000000 | tf_op jit(solution)/shard_map/pallas_call | solution.py:462
  4.9 0.0 copy-start.9
  4.9 0.0 copy-start.2
  4.9 0.0 copy-start.3
  4.9 0.0 copy-start.7
  4.9 0.0 copy-start.8
  4.9 9.4 %all-to-all-start = ((f32[16,96,128]{2,1,0:T(8,128)}), f32[16,96,128]{2,1,0:T(8,128)S(1)}, u32[]{:S(2)}, u32[]{:S(2)}) async-start(f32[16,96,128]{2,1,0:T(8,128)} %get-tuple-element.34), calls=%async_computation | async-start | bytes 1572864 | tf_op jit(solution)/shard_map/all_to_all | solution.py:442
  14.3 0.0 copy-done.9
  14.3 0.0 copy-start.10
  14.3 0.0 copy-start.5
  14.4 16.6 %psum.14.small = f32[24,128]{1,0:T(8,128)S(1)} all-reduce(f32[24,128]{1,0:T(8,128)S(1)} %copy-done.9), channel_id=1, replica_groups=mesh['zh'=4,'zl'=4,'y'=4,'head'=4,'dp'=2] {'head'}, use_global_device_ids=true, to_apply=%region_0.1 | all-reduce | flops 3072 | bytes 24576 | tf_op jit(solution)/shard_map/psum | solution.py:471
  31.0 0.0 copy-done.10
  31.0 0.0 copy-done.2
  31.0 0.0 copy-done.3
  31.0 0.0 copy-done.7
  31.0 0.0 copy-done.8
  31.0 0.0 copy-done.6
  31.0 0.0 copy-done.5
  31.0 0.6 copy-done.4
  31.7 2.1 %shard_map.154 = (bf16[128,1024]{1,0:T(8,128)(2,1)S(1)}, f32[16,64,128]{2,1,0:T(8,128)}, f32[8,16,128]{2,1,0:T(8,128)S(1)}) custom-call(f32[8,128]{1,0:T(8,128)S(1)} %copy-done.4, s32[16,128]{1,0:T(8,128)S(1)} %copy-done.8, f32[24,128]{1,0:T(8,128)S(1)} %psum.14.small, bf16[128,1024]{1,0:T(8,128)(2,1)S(1)} %bitcast.22, bf16[128,1024]{1,0:T(8,128)(2,1)S(1)} %bitcast.19, ...), custom_call_target="tpu_custom_call" | custom-call | flops 100000000 | bytes 2000000 | tf_op jit(solution)/shard_map/pallas_call | solution.py:472
  33.8 0.0 all-to-all-done.later
  33.8 7.5 %all-to-all-start.1 = ((f32[16,64,128]{2,1,0:T(8,128)}), f32[16,64,128]{2,1,0:T(8,128)S(1)}, u32[]{:S(2)}, u32[]{:S(2)}) async-start(f32[16,64,128]{2,1,0:T(8,128)} %get-tuple-element.36), calls=%async_computation.1 | async-start | bytes 1048576 | tf_op jit(solution)/shard_map/all_to_all | solution.py:442
  41.3 0.5 shard_map.155
  41.8 24.3 %all-gather = f32[384,128]{1,0:T(8,128)S(1)} all-gather(f32[96,128]{1,0:T(8,128)S(1)} %shard_map.155), channel_id=2, replica_groups=mesh['zh'=4,'zl'=4,'y'=4,'head'=4,'dp'=2] {'zh'}, dimensions={0}, use_global_device_ids=true | all-gather | bytes 245760 | tf_op jit(solution)/shard_map/all_gather | solution.py:482
  66.2 0.0 all-to-all-done.1.earlier
  66.2 0.1 shard_map.156
  66.3 1.4 %shard_map.158 = f32[16,88,128]{2,1,0:T(8,128)} custom-call(f32[8,128]{1,0:T(8,128)S(1)} %copy-done.4, f32[16,96,128]{2,1,0:T(8,128)S(1)} %all-to-all-done.later, f32[4,96,128]{2,1,0:T(8,128)S(1)} %bitcast.23, f32[8,16,128]{2,1,0:T(8,128)S(1)} %get-tuple-element.39.basis), custom_call_target="tpu_custom_call" | custom-call | flops 100000000 | bytes 2000000 | tf_op jit(solution)/shard_map/pallas_call | solution.py:487
  67.6 11.5 %all-to-all-start.2 = ((f32[16,88,128]{2,1,0:T(8,128)}), f32[16,88,128]{2,1,0:T(8,128)S(1)}, u32[]{:S(2)}, u32[]{:S(2)}) async-start(f32[16,88,128]{2,1,0:T(8,128)} %shard_map.158), calls=%async_computation.2 | async-start | bytes 1441792 | tf_op jit(solution)/shard_map/all_to_all | solution.py:442
  79.2 5.0 %collective-permute-start = (f32[64,128]{1,0:T(8,128)S(1)}, f32[64,128]{1,0:T(8,128)S(1)}, u32[]{:S(2)}, u32[]{:S(2)}) collective-permute-start(f32[64,128]{1,0:T(8,128)S(1)} %shard_map.156), channel_id=1, source_target_pairs={{0,128},{128,256},{256,384},{1,129},{129,257},{257,385},{2,130},{1... | collective-permute-start | bytes 98312 | tf_op jit(solution)/shard_map/ppermute | solution.py:446
  84.2 7.3 %collective-permute-start.1 = (f32[64,128]{1,0:T(8,128)S(1)}, f32[64,128]{1,0:T(8,128)S(1)}, u32[]{:S(2)}, u32[]{:S(2)}) collective-permute-start(f32[64,128]{1,0:T(8,128)S(1)} %shard_map.156), channel_id=1, source_target_pairs={{0,256},{128,384},{1,257},{129,385},{2,258},{130,386},{3,259},{131... | collective-permute-start | bytes 98312 | tf_op jit(solution)/shard_map/ppermute | solution.py:446
  91.5 1.3 %collective-permute-start.2 = (f32[64,128]{1,0:T(8,128)S(1)}, f32[64,128]{1,0:T(8,128)S(1)}, u32[]{:S(2)}, u32[]{:S(2)}) collective-permute-start(f32[64,128]{1,0:T(8,128)S(1)} %shard_map.156), channel_id=1, source_target_pairs={{0,384},{1,385},{2,386},{3,387},{4,388},{5,389},{6,390},{7,391},{8... | collective-permute-start | bytes 98312 | tf_op jit(solution)/shard_map/ppermute | solution.py:446
  92.8 0.0 collective-permute-done.one
  92.8 0.3 collective-permute-done.1.two
  93.1 1.3 %collective-permute-done.2.three = f32[64,128]{1,0:T(8,128)S(1)} collective-permute-done((f32[64,128]{1,0:T(8,128)S(1)}, f32[64,128]{1,0:T(8,128)S(1)}, u32[]{:S(2)}, u32[]{:S(2)}) %collective-permute-start.2) | collective-permute-done | bytes 32800 | tf_op jit(solution)/shard_map/ppermute | solution.py:446
  94.4 0.9 shard_map.157
  95.2 0.0 all-to-all-done.2.x.state
  95.2 0.1 shard_map.159
  95.3 10.5 %psum.15.head_sums = f32[16,128]{1,0:T(8,128)S(1)} all-reduce(f32[16,128]{1,0:T(8,128)S(1)} %shard_map.159), channel_id=1, replica_groups=mesh['zh'=4,'zl'=4,'y'=4,'head'=4,'dp'=2] {'head'}, use_global_device_ids=true, to_apply=%region_1.2 | all-reduce | flops 2048 | bytes 16384 | tf_op jit(solution)/shard_map/psum | solution.py:504
  105.9 7.0 %all-to-all-start.3 = ((f32[16,64,128]{2,1,0:T(8,128)}), f32[16,64,128]{2,1,0:T(8,128)S(1)}, u32[]{:S(2)}, u32[]{:S(2)}) async-start(f32[16,64,128]{2,1,0:T(8,128)} %shard_map.157), calls=%async_computation.3 | async-start | bytes 1048576 | tf_op jit(solution)/shard_map/all_to_all | solution.py:442
  112.9 0.0 copy-start.1
  112.9 1.3 shard_map.161.parts
  114.2 1.9 %collective-permute-start.3 = (f32[72,128]{1,0:T(8,128)S(1)}, f32[72,128]{1,0:T(8,128)S(1)}, u32[]{:S(2)}, u32[]{:S(2)}) collective-permute-start(f32[72,128]{1,0:T(8,128)S(1)} %shard_map.161.parts), channel_id=1, source_target_pairs={{0,1},{1,0},{2,3},{3,2},{4,5},{5,4},{6,7},{7,6},{8,9},{9,8},{10,11... | collective-permute-start | bytes 110600 | tf_op jit(solution)/shard_map/ppermute | solution.py:508
  116.1 0.0 copy-done
  116.1 0.0 copy-done.1
  116.1 3.2 %shard_map.160 = (f32[128,1024]{1,0:T(8,128)S(1)}, f32[128,1024]{1,0:T(8,128)S(1)}, bf16[128,1024]{1,0:T(8,128)(2,1)}, bf16[128,1024]{1,0:T(8,128)(2,1)}) custom-call(f32[8,128]{1,0:T(8,128)S(1)} %copy-done.4, s32[16,128]{1,0:T(8,128)S(1)} %copy-done.8, bf16[128,1024]{1,0:T(8,128)(2,1)S(1)} %bitcast.13, bf16[128,1024]{1,0:T(8,128)(2,1)S(1)} %bitcast.20, ...), custom_call_target="tpu_custom_call" | custom-call | flops 100000000 | bytes 2000000 | tf_op jit(solution)/shard_map/pallas_call | solution.py:509
  119.3 0.0 collective-permute-done.3.others
  119.3 4.5 %all-to-all-done.3.state = f32[16,64,128]{2,1,0:T(8,128)S(1)} async-done(((f32[16,64,128]{2,1,0:T(8,128)}), f32[16,64,128]{2,1,0:T(8,128)S(1)}, u32[]{:S(2)}, u32[]{:S(2)}) %all-to-all-start.3) | async-done | bytes 524320 | tf_op jit(solution)/shard_map/all_to_all | solution.py:442
  123.8 2.0 %shard_map.162 = (bf16[128,1024]{1,0:T(8,128)(2,1)}, bf16[128,1024]{1,0:T(8,128)(2,1)}, f32[4,1024]{1,0:T(4,128)}, f32[4,1024]{1,0:T(4,128)}, f32[4]{0:T(128)}) custom-call(f32[8,128]{1,0:T(8,128)S(1)} %copy-done.4, bf16[128,1024]{1,0:T(8,128)(2,1)S(1)} %bitcast.14, bf16[128,1024]{1,0:T(8,128)(2,1)S(1)} %bitcast.17, ...), custom_call_target="tpu_custom_call" | custom-call | flops 100000000 | bytes 2000000 | tf_op jit(solution)/shard_map/pallas_call | solution.py:512
  (4 shorter events, 0.0 us)
Async XLA Ops:
  4.9 9.4 %copy-start.9 = (f32[24,128]{1,0:T(8,128)S(1)}, f32[24,128]{1,0:T(8,128)}, u32[]{:S(2)}) copy-start(f32[24,128]{1,0:T(8,128)} %get-tuple-element.32) | copy-start | bytes 36868
  4.9 26.1 %copy-start.2 = (bf16[1,128,1024]{2,1,0:T(8,128)(2,1)S(1)}, bf16[1,128,1024]{2,1,0:T(8,128)(2,1)}, u32[]{:S(2)}) copy-start(bf16[1,128,1024]{2,1,0:T(8,128)(2,1)} %param.11) | copy-start | bytes 786436
  4.9 26.1 %copy-start.3 = (bf16[1,128,1024]{2,1,0:T(8,128)(2,1)S(1)}, bf16[1,128,1024]{2,1,0:T(8,128)(2,1)}, u32[]{:S(2)}) copy-start(bf16[1,128,1024]{2,1,0:T(8,128)(2,1)} %param.12) | copy-start | bytes 786436
  4.9 26.1 %copy-start.7 = (f32[4,1024]{1,0:T(4,128)S(1)}, f32[4,1024]{1,0:T(4,128)}, u32[]{:S(2)}) copy-start(f32[4,1024]{1,0:T(4,128)} %proj.3) | copy-start | bytes 49156
  4.9 26.1 %copy-start.8 = (s32[16,128]{1,0:T(8,128)S(1)}, s32[16,128]{1,0:T(8,128)}, u32[]{:S(2)}) copy-start(s32[16,128]{1,0:T(8,128)} %get-tuple-element.31.places) | copy-start | bytes 24580
  4.9 28.8 %all-to-all-start = ((f32[16,96,128]{2,1,0:T(8,128)}), f32[16,96,128]{2,1,0:T(8,128)S(1)}, u32[]{:S(2)}, u32[]{:S(2)}) async-start(f32[16,96,128]{2,1,0:T(8,128)} %get-tuple-element.34), calls=%async_computation | async-start | bytes 1572864 | tf_op jit(solution)/shard_map/all_to_all | solution.py:442
  14.3 16.7 %copy-start.6 = (f32[4,1024]{1,0:T(4,128)S(1)}, f32[4,1024]{1,0:T(4,128)}, u32[]{:S(2)}) copy-start(f32[4,1024]{1,0:T(4,128)} %rot.3) | copy-start | bytes 49156
  14.3 16.6 %copy-start.10 = (f32[4]{0:T(128)S(1)}, f32[4]{0:T(128)}, u32[]{:S(2)}) copy-start(f32[4]{0:T(128)} %param.18) | copy-start | bytes 52
  14.3 16.7 %copy-start.5 = (f32[1024,2]{0,1:T(2,128)S(1)}, f32[1024,2]{0,1:T(2,128)}, u32[]{:S(2)}) copy-start(f32[1024,2]{0,1:T(2,128)} %param.16) | copy-start | bytes 24580
  31.0 0.7 copy-start.4
  33.8 32.4 %all-to-all-start.1 = ((f32[16,64,128]{2,1,0:T(8,128)}), f32[16,64,128]{2,1,0:T(8,128)S(1)}, u32[]{:S(2)}, u32[]{:S(2)}) async-start(f32[16,64,128]{2,1,0:T(8,128)} %get-tuple-element.36), calls=%async_computation.1 | async-start | bytes 1048576 | tf_op jit(solution)/shard_map/all_to_all | solution.py:442
  67.6 27.6 %all-to-all-start.2 = ((f32[16,88,128]{2,1,0:T(8,128)}), f32[16,88,128]{2,1,0:T(8,128)S(1)}, u32[]{:S(2)}, u32[]{:S(2)}) async-start(f32[16,88,128]{2,1,0:T(8,128)} %shard_map.158), calls=%async_computation.2 | async-start | bytes 1441792 | tf_op jit(solution)/shard_map/all_to_all | solution.py:442
  79.2 13.6 %collective-permute-start = (f32[64,128]{1,0:T(8,128)S(1)}, f32[64,128]{1,0:T(8,128)S(1)}, u32[]{:S(2)}, u32[]{:S(2)}) collective-permute-start(f32[64,128]{1,0:T(8,128)S(1)} %shard_map.156), channel_id=1, source_target_pairs={{0,128},{128,256},{256,384},{1,129},{129,257},{257,385},{2,130},{1... | collective-permute-start | bytes 98312 | tf_op jit(solution)/shard_map/ppermute | solution.py:446
  84.2 8.9 %collective-permute-start.1 = (f32[64,128]{1,0:T(8,128)S(1)}, f32[64,128]{1,0:T(8,128)S(1)}, u32[]{:S(2)}, u32[]{:S(2)}) collective-permute-start(f32[64,128]{1,0:T(8,128)S(1)} %shard_map.156), channel_id=1, source_target_pairs={{0,256},{128,384},{1,257},{129,385},{2,258},{130,386},{3,259},{131... | collective-permute-start | bytes 98312 | tf_op jit(solution)/shard_map/ppermute | solution.py:446
  91.5 2.9 %collective-permute-start.2 = (f32[64,128]{1,0:T(8,128)S(1)}, f32[64,128]{1,0:T(8,128)S(1)}, u32[]{:S(2)}, u32[]{:S(2)}) collective-permute-start(f32[64,128]{1,0:T(8,128)S(1)} %shard_map.156), channel_id=1, source_target_pairs={{0,384},{1,385},{2,386},{3,387},{4,388},{5,389},{6,390},{7,391},{8... | collective-permute-start | bytes 98312 | tf_op jit(solution)/shard_map/ppermute | solution.py:446
  105.9 17.9 %all-to-all-start.3 = ((f32[16,64,128]{2,1,0:T(8,128)}), f32[16,64,128]{2,1,0:T(8,128)S(1)}, u32[]{:S(2)}, u32[]{:S(2)}) async-start(f32[16,64,128]{2,1,0:T(8,128)} %shard_map.157), calls=%async_computation.3 | async-start | bytes 1048576 | tf_op jit(solution)/shard_map/all_to_all | solution.py:442
  112.9 3.2 %copy-start = (bf16[1,128,1024]{2,1,0:T(8,128)(2,1)S(1)}, bf16[1,128,1024]{2,1,0:T(8,128)(2,1)}, u32[]{:S(2)}) copy-start(bf16[1,128,1024]{2,1,0:T(8,128)(2,1)} %param.10) | copy-start | bytes 786436
  112.9 3.2 %copy-start.1 = (bf16[1,128,1024]{2,1,0:T(8,128)(2,1)S(1)}, bf16[1,128,1024]{2,1,0:T(8,128)(2,1)}, u32[]{:S(2)}) copy-start(bf16[1,128,1024]{2,1,0:T(8,128)(2,1)} %param.13) | copy-start | bytes 786436
  114.2 5.1 %collective-permute-start.3 = (f32[72,128]{1,0:T(8,128)S(1)}, f32[72,128]{1,0:T(8,128)S(1)}, u32[]{:S(2)}, u32[]{:S(2)}) collective-permute-start(f32[72,128]{1,0:T(8,128)S(1)} %shard_map.161.parts), channel_id=1, source_target_pairs={{0,1},{1,0},{2,3},{3,2},{4,5},{5,4},{6,7},{7,6},{8,9},{9,8},{10,11... | collective-permute-start | bytes 110600 | tf_op jit(solution)/shard_map/ppermute | solution.py:508

commit v5 on v4

--- a/solution.py
+++ b/solution.py
@@ -502,7 +502,6 @@
     )(logs, earlier, one, two, three)
     (head_sums,) = call(sum_slices, "v", [(tile, f32)])(leaving)
     head_sums = lax.psum(head_sums, "head")
-    entering, head_sums = lax.optimization_barrier((entering, head_sums))
     entering = swap(entering, NEAR)
     (parts,) = call(products, "vvv", [((72, 128), f32)])(head_sums, bias, leaving)
     others = lax.ppermute(parts, "dp", [(0, 1), (1, 0)])

time: 127 us -> 123 us (0.969)
  the two profiles are of different devices: /device:TPU:8 before, /device:TPU:1 now
where the time goes in v5:
time: 123 us; the launch traced here: 122 us
  starting transfers between devices  57.4 us (47%)
  blocking collectives  45.5 us (37%)
  Pallas kernels  15.7 us (13%)
  waiting for transfers between devices  2.24 us (2%)
    all_to_all x4, starting transfers between devices, swap(): return lax.all_to_all(x, axes, 0, 0, tiled=False)  35.2 us
    all_gather x1, blocking collectives, shards(): groups = lax.all_gather(own, 'zh')  22 us
    psum x1, blocking collectives, shards(): small = lax.psum(small, 'head')  14 us
    ppermute x3, starting transfers between devices, ahead(): return lax.ppermute(x, 'zh', [(i, i + d) for i in range(4 - d)])  13.5 us
    psum x1, blocking collectives, shards(): head_sums = lax.psum(head_sums, 'head')  9.52 us
    ppermute x1, starting transfers between devices, shards(): others = lax.ppermute(parts, 'dp', [(0, 1), (1, 0)])  8.68 us
    pallas_call x1, Pallas kernels, shards(): call(query_state, 'ssaaaavvv', [((16, 96, 128), f32), ((24, 128), f32), (...  4.25 us
    pallas_call x1, Pallas kernels, shards(): call(backward_rest, 'vvvvvvvvv', [(rows, f32)] * 2 + [(rows, bf16)] * 2)  3.2 us
  transfers between devices with their start and end apart: 8, of which 2 were waited for; matrix products, arithmetic and copies ran while one was open for 0% of the time, Pallas kernels for 7%

profile of v5, /device:TPU:1, one launch (start us, length us, event | category | flops | bytes accessed | tf_op | source)
XLA Modules:
  0.0 122.5 jit_solution(6662205245884231883)
XLA Ops:
  0.6 4.2 %shard_map.153 = (f32[16,96,128]{2,1,0:T(8,128)}, f32[24,128]{1,0:T(8,128)}, f32[8,128]{1,0:T(8,128)}, s32[16,128]{1,0:T(8,128)}) custom-call(f32[8]{0:T(128)} %rate.1, s32[1,16]{1,0:T(1,128)} %positions.1, bf16[128,1024]{1,0:T(8,128)(2,1)} %bitcast.12, bf16[128,1024]{1,0:T(8,128)(2,1)} %bitcast.18, bf16[128,1024]{1,0:T(8,128)(2,1)} %bitcast.15, ...), custom_call_target="tpu_custom_call" | custom-call | flops 100000000 | bytes 2000000 | tf_op jit(solution)/shard_map/pallas_call | solution.py:462
  4.9 0.0 copy-start.9
  4.9 0.0 copy-start.2
  4.9 0.0 copy-start.3
  4.9 0.0 copy-start.7
  4.9 0.0 copy-start.8
  4.9 9.3 %all-to-all-start = ((f32[16,96,128]{2,1,0:T(8,128)}), f32[16,96,128]{2,1,0:T(8,128)S(1)}, u32[]{:S(2)}, u32[]{:S(2)}) async-start(f32[16,96,128]{2,1,0:T(8,128)} %get-tuple-element.32), calls=%async_computation | async-start | bytes 1572864 | tf_op jit(solution)/shard_map/all_to_all | solution.py:442
  14.3 0.0 copy-start.6
  14.3 0.0 copy-done.9
  14.3 0.0 copy-start.10
  14.3 0.0 copy-start.5
  14.3 14.0 %psum.14.small = f32[24,128]{1,0:T(8,128)S(1)} all-reduce(f32[24,128]{1,0:T(8,128)S(1)} %copy-done.9), channel_id=1, replica_groups=mesh['zh'=4,'zl'=4,'y'=4,'head'=4,'dp'=2] {'head'}, use_global_device_ids=true, to_apply=%region_0.1 | all-reduce | flops 3072 | bytes 24576 | tf_op jit(solution)/shard_map/psum | solution.py:471
  28.3 0.0 copy-done.10
  28.3 0.0 copy-done.2
  28.3 0.0 copy-done.3
  28.3 0.0 copy-done.7
  28.3 0.0 copy-done.8
  28.4 0.0 copy-done.6
  28.4 0.0 copy-done.5
  28.4 0.6 copy-done.4
  29.0 2.1 %shard_map.154 = (bf16[128,1024]{1,0:T(8,128)(2,1)S(1)}, f32[16,64,128]{2,1,0:T(8,128)}, f32[8,16,128]{2,1,0:T(8,128)S(1)}) custom-call(f32[8,128]{1,0:T(8,128)S(1)} %copy-done.4, s32[16,128]{1,0:T(8,128)S(1)} %copy-done.8, f32[24,128]{1,0:T(8,128)S(1)} %psum.14.small, bf16[128,1024]{1,0:T(8,128)(2,1)S(1)} %bitcast.22, bf16[128,1024]{1,0:T(8,128)(2,1)S(1)} %bitcast.19, ...), custom_call_target="tpu_custom_call" | custom-call | flops 100000000 | bytes 2000000 | tf_op jit(solution)/shard_map/pallas_call | solution.py:472
  31.1 0.9 all-to-all-done.later
  32.0 6.5 %all-to-all-start.1 = ((f32[16,64,128]{2,1,0:T(8,128)}), f32[16,64,128]{2,1,0:T(8,128)S(1)}, u32[]{:S(2)}, u32[]{:S(2)}) async-start(f32[16,64,128]{2,1,0:T(8,128)} %get-tuple-element.34), calls=%async_computation.1 | async-start | bytes 1048576 | tf_op jit(solution)/shard_map/all_to_all | solution.py:442
  38.5 0.5 shard_map.155
  39.0 22.0 %all-gather = f32[384,128]{1,0:T(8,128)S(1)} all-gather(f32[96,128]{1,0:T(8,128)S(1)} %shard_map.155), channel_id=2, replica_groups=mesh['zh'=4,'zl'=4,'y'=4,'head'=4,'dp'=2] {'zh'}, dimensions={0}, use_global_device_ids=true | all-gather | bytes 245760 | tf_op jit(solution)/shard_map/all_gather | solution.py:482
  61.1 0.0 all-to-all-done.1.earlier
  61.1 0.1 shard_map.156
  61.1 1.4 %shard_map.158 = f32[16,88,128]{2,1,0:T(8,128)} custom-call(f32[8,128]{1,0:T(8,128)S(1)} %copy-done.4, f32[16,96,128]{2,1,0:T(8,128)S(1)} %all-to-all-done.later, f32[4,96,128]{2,1,0:T(8,128)S(1)} %bitcast.23, f32[8,16,128]{2,1,0:T(8,128)S(1)} %get-tuple-element.38.basis), custom_call_target="tpu_custom_call" | custom-call | flops 100000000 | bytes 2000000 | tf_op jit(solution)/shard_map/pallas_call | solution.py:487
  62.5 12.1 %all-to-all-start.3 = ((f32[16,88,128]{2,1,0:T(8,128)}), f32[16,88,128]{2,1,0:T(8,128)S(1)}, u32[]{:S(2)}, u32[]{:S(2)}) async-start(f32[16,88,128]{2,1,0:T(8,128)} %shard_map.158), calls=%async_computation.3 | async-start | bytes 1441792 | tf_op jit(solution)/shard_map/all_to_all | solution.py:442
  74.6 5.2 %collective-permute-start = (f32[64,128]{1,0:T(8,128)S(1)}, f32[64,128]{1,0:T(8,128)S(1)}, u32[]{:S(2)}, u32[]{:S(2)}) collective-permute-start(f32[64,128]{1,0:T(8,128)S(1)} %shard_map.156), channel_id=1, source_target_pairs={{0,128},{128,256},{256,384},{1,129},{129,257},{257,385},{2,130},{1... | collective-permute-start | bytes 98312 | tf_op jit(solution)/shard_map/ppermute | solution.py:446
  79.8 7.0 %collective-permute-start.1 = (f32[64,128]{1,0:T(8,128)S(1)}, f32[64,128]{1,0:T(8,128)S(1)}, u32[]{:S(2)}, u32[]{:S(2)}) collective-permute-start(f32[64,128]{1,0:T(8,128)S(1)} %shard_map.156), channel_id=1, source_target_pairs={{0,256},{128,384},{1,257},{129,385},{2,258},{130,386},{3,259},{131... | collective-permute-start | bytes 98312 | tf_op jit(solution)/shard_map/ppermute | solution.py:446
  86.8 1.3 %collective-permute-start.2 = (f32[64,128]{1,0:T(8,128)S(1)}, f32[64,128]{1,0:T(8,128)S(1)}, u32[]{:S(2)}, u32[]{:S(2)}) collective-permute-start(f32[64,128]{1,0:T(8,128)S(1)} %shard_map.156), channel_id=1, source_target_pairs={{0,384},{1,385},{2,386},{3,387},{4,388},{5,389},{6,390},{7,391},{8... | collective-permute-start | bytes 98312 | tf_op jit(solution)/shard_map/ppermute | solution.py:446
  88.1 0.0 collective-permute-done.one
  88.1 0.0 collective-permute-done.1.two
  88.1 1.3 %collective-permute-done.2.three = f32[64,128]{1,0:T(8,128)S(1)} collective-permute-done((f32[64,128]{1,0:T(8,128)S(1)}, f32[64,128]{1,0:T(8,128)S(1)}, u32[]{:S(2)}, u32[]{:S(2)}) %collective-permute-start.2) | collective-permute-done | bytes 32800 | tf_op jit(solution)/shard_map/ppermute | solution.py:446
  89.4 0.9 shard_map.157
  90.3 0.0 all-to-all-done.3.x.state
  90.3 7.3 %all-to-all-start.2 = ((f32[16,64,128]{2,1,0:T(8,128)}), f32[16,64,128]{2,1,0:T(8,128)S(1)}, u32[]{:S(2)}, u32[]{:S(2)}) async-start(f32[16,64,128]{2,1,0:T(8,128)} %shard_map.157), calls=%async_computation.2 | async-start | bytes 1048576 | tf_op jit(solution)/shard_map/all_to_all | solution.py:442
  97.7 0.1 shard_map.159
  97.7 9.5 %psum.15.head_sums = f32[16,128]{1,0:T(8,128)S(1)} all-reduce(f32[16,128]{1,0:T(8,128)S(1)} %shard_map.159), channel_id=1, replica_groups=mesh['zh'=4,'zl'=4,'y'=4,'head'=4,'dp'=2] {'head'}, use_global_device_ids=true, to_apply=%region_1.2 | all-reduce | flops 2048 | bytes 16384 | tf_op jit(solution)/shard_map/psum | solution.py:504
  107.3 0.0 copy-start
  107.3 0.0 copy-start.1
  107.3 1.3 %shard_map.161.parts = f32[72,128]{1,0:T(8,128)S(1)} custom-call(f32[16,128]{1,0:T(8,128)S(1)} %psum.15.head_sums, f32[1,128]{1,0:T(1,128)S(1)} %pad_bitcast_fusion.bias, f32[16,88,128]{2,1,0:T(8,128)S(1)} %all-to-all-done.3.x.state), custom_call_target="tpu_custom_call" | custom-call | flops 100000000 | bytes 2000000 | tf_op jit(solution)/shard_map/pallas_call | solution.py:506
  108.6 8.7 %collective-permute-start.3 = (f32[72,128]{1,0:T(8,128)S(1)}, f32[72,128]{1,0:T(8,128)S(1)}, u32[]{:S(2)}, u32[]{:S(2)}) collective-permute-start(f32[72,128]{1,0:T(8,128)S(1)} %shard_map.161.parts), channel_id=1, source_target_pairs={{0,1},{1,0},{2,3},{3,2},{4,5},{5,4},{6,7},{7,6},{8,9},{9,8},{10,11... | collective-permute-start | bytes 110600 | tf_op jit(solution)/shard_map/ppermute | solution.py:507
  117.3 3.2 %shard_map.160 = (f32[128,1024]{1,0:T(8,128)S(1)}, f32[128,1024]{1,0:T(8,128)S(1)}, bf16[128,1024]{1,0:T(8,128)(2,1)}, bf16[128,1024]{1,0:T(8,128)(2,1)}) custom-call(f32[8,128]{1,0:T(8,128)S(1)} %copy-done.4, s32[16,128]{1,0:T(8,128)S(1)} %copy-done.8, bf16[128,1024]{1,0:T(8,128)(2,1)S(1)} %bitcast.13, bf16[128,1024]{1,0:T(8,128)(2,1)S(1)} %bitcast.20, ...), custom_call_target="tpu_custom_call" | custom-call | flops 100000000 | bytes 2000000 | tf_op jit(solution)/shard_map/pallas_call | solution.py:508
  120.5 0.0 all-to-all-done.2.state
  120.5 0.0 collective-permute-done.3.others
  120.5 2.0 %shard_map.162 = (bf16[128,1024]{1,0:T(8,128)(2,1)}, bf16[128,1024]{1,0:T(8,128)(2,1)}, f32[4,1024]{1,0:T(4,128)}, f32[4,1024]{1,0:T(4,128)}, f32[4]{0:T(128)}) custom-call(f32[8,128]{1,0:T(8,128)S(1)} %copy-done.4, bf16[128,1024]{1,0:T(8,128)(2,1)S(1)} %bitcast.14, bf16[128,1024]{1,0:T(8,128)(2,1)S(1)} %bitcast.17, ...), custom_call_target="tpu_custom_call" | custom-call | flops 100000000 | bytes 2000000 | tf_op jit(solution)/shard_map/pallas_call | solution.py:511
  (4 shorter events, 0.0 us)
Async XLA Ops:
  4.9 9.4 %copy-start.9 = (f32[24,128]{1,0:T(8,128)S(1)}, f32[24,128]{1,0:T(8,128)}, u32[]{:S(2)}) copy-start(f32[24,128]{1,0:T(8,128)} %get-tuple-element.30) | copy-start | bytes 36868
  4.9 23.4 %copy-start.2 = (bf16[1,128,1024]{2,1,0:T(8,128)(2,1)S(1)}, bf16[1,128,1024]{2,1,0:T(8,128)(2,1)}, u32[]{:S(2)}) copy-start(bf16[1,128,1024]{2,1,0:T(8,128)(2,1)} %param.11) | copy-start | bytes 786436
  4.9 23.4 %copy-start.3 = (bf16[1,128,1024]{2,1,0:T(8,128)(2,1)S(1)}, bf16[1,128,1024]{2,1,0:T(8,128)(2,1)}, u32[]{:S(2)}) copy-start(bf16[1,128,1024]{2,1,0:T(8,128)(2,1)} %param.12) | copy-start | bytes 786436
  4.9 23.4 %copy-start.7 = (f32[4,1024]{1,0:T(4,128)S(1)}, f32[4,1024]{1,0:T(4,128)}, u32[]{:S(2)}) copy-start(f32[4,1024]{1,0:T(4,128)} %proj.3) | copy-start | bytes 49156
  4.9 23.4 %copy-start.8 = (s32[16,128]{1,0:T(8,128)S(1)}, s32[16,128]{1,0:T(8,128)}, u32[]{:S(2)}) copy-start(s32[16,128]{1,0:T(8,128)} %get-tuple-element.29.places) | copy-start | bytes 24580
  4.9 27.1 %all-to-all-start = ((f32[16,96,128]{2,1,0:T(8,128)}), f32[16,96,128]{2,1,0:T(8,128)S(1)}, u32[]{:S(2)}, u32[]{:S(2)}) async-start(f32[16,96,128]{2,1,0:T(8,128)} %get-tuple-element.32), calls=%async_computation | async-start | bytes 1572864 | tf_op jit(solution)/shard_map/all_to_all | solution.py:442
  14.3 14.1 %copy-start.6 = (f32[4,1024]{1,0:T(4,128)S(1)}, f32[4,1024]{1,0:T(4,128)}, u32[]{:S(2)}) copy-start(f32[4,1024]{1,0:T(4,128)} %rot.3) | copy-start | bytes 49156
  14.3 14.0 %copy-start.10 = (f32[4]{0:T(128)S(1)}, f32[4]{0:T(128)}, u32[]{:S(2)}) copy-start(f32[4]{0:T(128)} %param.18) | copy-start | bytes 52
  14.3 14.1 %copy-start.5 = (f32[1024,2]{0,1:T(2,128)S(1)}, f32[1024,2]{0,1:T(2,128)}, u32[]{:S(2)}) copy-start(f32[1024,2]{0,1:T(2,128)} %param.16) | copy-start | bytes 24580
  28.3 0.7 copy-start.4
  32.0 29.0 %all-to-all-start.1 = ((f32[16,64,128]{2,1,0:T(8,128)}), f32[16,64,128]{2,1,0:T(8,128)S(1)}, u32[]{:S(2)}, u32[]{:S(2)}) async-start(f32[16,64,128]{2,1,0:T(8,128)} %get-tuple-element.34), calls=%async_computation.1 | async-start | bytes 1048576 | tf_op jit(solution)/shard_map/all_to_all | solution.py:442
  62.5 27.8 %all-to-all-start.3 = ((f32[16,88,128]{2,1,0:T(8,128)}), f32[16,88,128]{2,1,0:T(8,128)S(1)}, u32[]{:S(2)}, u32[]{:S(2)}) async-start(f32[16,88,128]{2,1,0:T(8,128)} %shard_map.158), calls=%async_computation.3 | async-start | bytes 1441792 | tf_op jit(solution)/shard_map/all_to_all | solution.py:442
  74.6 13.5 %collective-permute-start = (f32[64,128]{1,0:T(8,128)S(1)}, f32[64,128]{1,0:T(8,128)S(1)}, u32[]{:S(2)}, u32[]{:S(2)}) collective-permute-start(f32[64,128]{1,0:T(8,128)S(1)} %shard_map.156), channel_id=1, source_target_pairs={{0,128},{128,256},{256,384},{1,129},{129,257},{257,385},{2,130},{1... | collective-permute-start | bytes 98312 | tf_op jit(solution)/shard_map/ppermute | solution.py:446
  79.8 8.3 %collective-permute-start.1 = (f32[64,128]{1,0:T(8,128)S(1)}, f32[64,128]{1,0:T(8,128)S(1)}, u32[]{:S(2)}, u32[]{:S(2)}) collective-permute-start(f32[64,128]{1,0:T(8,128)S(1)} %shard_map.156), channel_id=1, source_target_pairs={{0,256},{128,384},{1,257},{129,385},{2,258},{130,386},{3,259},{131... | collective-permute-start | bytes 98312 | tf_op jit(solution)/shard_map/ppermute | solution.py:446
  86.8 2.6 %collective-permute-start.2 = (f32[64,128]{1,0:T(8,128)S(1)}, f32[64,128]{1,0:T(8,128)S(1)}, u32[]{:S(2)}, u32[]{:S(2)}) collective-permute-start(f32[64,128]{1,0:T(8,128)S(1)} %shard_map.156), channel_id=1, source_target_pairs={{0,384},{1,385},{2,386},{3,387},{4,388},{5,389},{6,390},{7,391},{8... | collective-permute-start | bytes 98312 | tf_op jit(solution)/shard_map/ppermute | solution.py:446
  90.3 30.1 %all-to-all-start.2 = ((f32[16,64,128]{2,1,0:T(8,128)}), f32[16,64,128]{2,1,0:T(8,128)S(1)}, u32[]{:S(2)}, u32[]{:S(2)}) async-start(f32[16,64,128]{2,1,0:T(8,128)} %shard_map.157), calls=%async_computation.2 | async-start | bytes 1048576 | tf_op jit(solution)/shard_map/all_to_all | solution.py:442
  107.3 10.0 %copy-start = (bf16[1,128,1024]{2,1,0:T(8,128)(2,1)S(1)}, bf16[1,128,1024]{2,1,0:T(8,128)(2,1)}, u32[]{:S(2)}) copy-start(bf16[1,128,1024]{2,1,0:T(8,128)(2,1)} %param.10) | copy-start | bytes 786436
  107.3 10.0 %copy-start.1 = (bf16[1,128,1024]{2,1,0:T(8,128)(2,1)S(1)}, bf16[1,128,1024]{2,1,0:T(8,128)(2,1)}, u32[]{:S(2)}) copy-start(bf16[1,128,1024]{2,1,0:T(8,128)(2,1)} %param.13) | copy-start | bytes 786436
  108.6 11.9 %collective-permute-start.3 = (f32[72,128]{1,0:T(8,128)S(1)}, f32[72,128]{1,0:T(8,128)S(1)}, u32[]{:S(2)}, u32[]{:S(2)}) collective-permute-start(f32[72,128]{1,0:T(8,128)S(1)} %shard_map.161.parts), channel_id=1, source_target_pairs={{0,1},{1,0},{2,3},{3,2},{4,5},{5,4},{6,7},{7,6},{8,9},{9,8},{10,11... | collective-permute-start | bytes 110600 | tf_op jit(solution)/shard_map/ppermute | solution.py:507

commit v6 on v5

--- a/solution.py
+++ b/solution.py
@@ -97,7 +97,16 @@
 
 def decayed_state(weighted, other):
     high, low = split(weighted)
-    return tn(other, high) + tn(other, low)
+    both = tn(other, jnp.concatenate([high, low], axis=1))
+    return both[:, 0:SIZE] + both[:, SIZE:]
+
+
+def nn_terms(a, terms):
+    return nn(jnp.concatenate([a, a], axis=1), jnp.concatenate(terms, axis=0))
+
+
+def nt_terms(a, terms):
+    return nt(jnp.concatenate([a, a], axis=1), jnp.concatenate(terms, axis=1))
 
 
 def halves(left, right, odd):
@@ -347,8 +356,16 @@
     code = jnp.where(lane < 4, turned + bias[...], 0.0)
     both = code_grad + pltpu.roll(code, 4, 1)
     lane = cols_iota((4, 128))
+    wide = jnp.concatenate([x[i, 72:88] for i in range(16)], axis=1)
+    every = lax.dot_general(
+        jnp.transpose(both)[0:8],
+        wide,
+        (((1,), (0,)), ((), ())),
+        preferred_element_type=f32,
+        precision=highest,
+    )
     for i in range(16):
-        got = full_tn(both, x[i, 72:88])
+        got = every[:, head_cols(i)]
         parts[4 * i : 4 * i + 4] = jnp.where(lane < 64, got[4:8], got[0:4])
     along = (full_tn(code, sums) - full_tn(code_grad, turned))[0:4]
     total = jnp.broadcast_to(jnp.sum(code_grad, axis=0, keepdims=True), (4, 128))
@@ -357,8 +374,10 @@
 
 
 def backward_rest(
-    logs, places, q, k, moved, grad, state, basis, head_sums, attended, grad_q, grad_k, grad_v
+    logs, places, q, k, moved, grad, state, basis, head_sums, attended, grad_q,
+    grad_k_far, grad_v_far, grad_k, grad_v, sent,
 ):
+    sends = []
     between = rows_iota() - cols_iota()
     lower = between >= 0
     distance = jnp.maximum(between, 0).astype(f32)
@@ -370,21 +389,29 @@
         c = head_cols(h)
         table = jnp.where(lower, powers(logs, h, distance), 0.0)
         leave = powers(logs, h, BLOCK - offset)
-        high, low = split(jnp.concatenate([state[2 * h, 0:64], state[2 * h + 1, 0:64]], axis=0))
+        terms = split(jnp.concatenate([state[2 * h, 0:64], state[2 * h + 1, 0:64]], axis=0))
         qh, mh, kh, gh = q[:, c], moved[:, c], k[:, c], grad[:, c]
         mixing = (nt(qh, kh) * table).astype(bf16)
         grad_mixing = (nt(gh, mh) * table).astype(bf16)
         attended[:, c] = nn(mixing, mh)
         grad_q[:, c] = nn(grad_mixing, kh)
         inner = tn(grad_mixing, qh)
-        grad_k[:, c] = (inner + leave * (nn(mh, high) + nn(mh, low))).astype(bf16)
+        grad_k[:, c] = (inner + leave * nn_terms(mh, terms)).astype(bf16)
         inner = tn(mixing, gh)
         lift = basis[h][6:10]
         fix = jnp.zeros((NPOS, SIZE), f32)
         for r in range(4):
             fix = fix + code_grad[:, r : r + 1] * lift[r : r + 1]
-        out = inner + leave * (nt(kh, high) + nt(kh, low))
+        out = inner + leave * nt_terms(kh, terms)
         grad_v[:, c] = (out + tn(select, third_terms(fix))).astype(bf16)
+        if h % 2 == 1:
+            wide = slice((h - 1) * SIZE, (h + 1) * SIZE)
+            for n, (src, dst) in enumerate(((grad_k, grad_k_far), (grad_v, grad_v_far))):
+                copy = pltpu.make_async_copy(src.at[:, wide], dst.at[:, wide], sent.at[h // 2, n])
+                copy.start()
+                sends.append(copy)
+    for copy in sends:
+        copy.wait()
 
 
 def forward_rest(
@@ -402,10 +429,10 @@
     for h in range(HEADS):
         c = head_cols(h)
         enter = powers(logs, h, offset + 1.0)
-        high, low = split(jnp.concatenate([state[2 * h], state[2 * h + 1]], axis=0))
+        terms = split(jnp.concatenate([state[2 * h], state[2 * h + 1]], axis=0))
         qh, gh = q[:, c], grad[:, c]
-        attended[:, c] = (attended_in[:, c] + enter * (nt(qh, high) + nt(qh, low))).astype(bf16)
-        grad_q[:, c] = (grad_q_in[:, c] + enter * (nn(gh, high) + nn(gh, low))).astype(bf16)
+        attended[:, c] = (attended_in[:, c] + enter * nt_terms(qh, terms)).astype(bf16)
+        grad_q[:, c] = (grad_q_in[:, c] + enter * nn_terms(gh, terms)).astype(bf16)
         if h % 2 == 1:
             wide = slice((h - 1) * SIZE, (h + 1) * SIZE)
             pairs = ((attended, attended_far), (grad_q, grad_q_far))
@@ -506,7 +533,11 @@
     (parts,) = call(products, "vvv", [((72, 128), f32)])(head_sums, bias, leaving)
     others = lax.ppermute(parts, "dp", [(0, 1), (1, 0)])
     attended_in, grad_q_in, grad_k, grad_v = call(
-        backward_rest, "vvvvvvvvv", [(rows, f32)] * 2 + [(rows, bf16)] * 2
+        backward_rest,
+        "v" * 9,
+        [(rows, f32)] * 2 + [(rows, bf16)] * 2,
+        [space(rows, bf16)] * 2 + [marks(4, 2)],
+        (2, 3),
     )(logs, places, q, k, moved, grad, leaving, basis, head_sums)
     attended, grad_q, grad_rotation, grad_weight, grad_bias = call(
         forward_rest,

time: 123 us -> 122 us (level)
  Pallas kernels: 15.7 us -> 14.4 us
  transfers between devices with their start and end apart: 8 -> 8, of which waited for: 2 -> 2; matrix products, arithmetic and copies ran while one was open for 0% -> 0% of each run, Pallas kernels for 7% -> 6%
where the time goes in v6:
time: 122 us; the launch traced here: 121 us
  starting transfers between devices  57.2 us (47%)
  blocking collectives  45.5 us (37%)
  Pallas kernels  14.4 us (12%)
  waiting for transfers between devices  2.45 us (2%)
    all_to_all x4, starting transfers between devices, swap(): return lax.all_to_all(x, axes, 0, 0, tiled=False)  35.2 us
    all_gather x1, blocking collectives, shards(): groups = lax.all_gather(own, 'zh')  22 us
    psum x1, blocking collectives, shards(): small = lax.psum(small, 'head')  14 us
    ppermute x3, starting transfers between devices, ahead(): return lax.ppermute(x, 'zh', [(i, i + d) for i in range(4 - d)])  13.3 us
    psum x1, blocking collectives, shards(): head_sums = lax.psum(head_sums, 'head')  9.51 us
    ppermute x1, starting transfers between devices, shards(): others = lax.ppermute(parts, 'dp', [(0, 1), (1, 0)])  8.69 us
    pallas_call x1, Pallas kernels, shards(): call(query_state, 'ssaaaavvv', [((16, 96, 128), f32), ((24, 128), f32), (...  4.24 us
    pallas_call x1, Pallas kernels, shards(): call(backward_rest, 'v' * 9, [(rows, f32)] * 2 + [(rows, bf16)] * 2, [spa...  2.87 us
  transfers between devices with their start and end apart: 8, of which 2 were waited for; matrix products, arithmetic and copies ran while one was open for 0% of the time, Pallas kernels for 6%

profile of v6, /device:TPU:1, one launch (start us, length us, event | category | flops | bytes accessed | tf_op | source)
XLA Modules:
  0.0 121.2 jit_solution(17636859081514134663)
XLA Ops:
  0.6 4.2 %shard_map.153 = (f32[16,96,128]{2,1,0:T(8,128)}, f32[24,128]{1,0:T(8,128)}, f32[8,128]{1,0:T(8,128)}, s32[16,128]{1,0:T(8,128)}) custom-call(f32[8]{0:T(128)} %rate.1, s32[1,16]{1,0:T(1,128)} %positions.1, bf16[128,1024]{1,0:T(8,128)(2,1)} %bitcast.12, bf16[128,1024]{1,0:T(8,128)(2,1)} %bitcast.18, bf16[128,1024]{1,0:T(8,128)(2,1)} %bitcast.15, ...), custom_call_target="tpu_custom_call" | custom-call | flops 100000000 | bytes 2000000 | tf_op jit(solution)/shard_map/pallas_call | solution.py:489
  4.9 0.0 copy-start.9
  4.9 0.0 copy-start.2
  4.9 0.0 copy-start.3
  4.9 0.0 copy-start.7
  4.9 0.0 copy-start.8
  4.9 9.3 %all-to-all-start = ((f32[16,96,128]{2,1,0:T(8,128)}), f32[16,96,128]{2,1,0:T(8,128)S(1)}, u32[]{:S(2)}, u32[]{:S(2)}) async-start(f32[16,96,128]{2,1,0:T(8,128)} %get-tuple-element.32), calls=%async_computation | async-start | bytes 1572864 | tf_op jit(solution)/shard_map/all_to_all | solution.py:469
  14.3 0.0 copy-start.6
  14.3 0.0 copy-done.9
  14.3 0.0 copy-start.10
  14.3 0.0 copy-start.5
  14.3 14.0 %psum.14.small = f32[24,128]{1,0:T(8,128)S(1)} all-reduce(f32[24,128]{1,0:T(8,128)S(1)} %copy-done.9), channel_id=1, replica_groups=mesh['zh'=4,'zl'=4,'y'=4,'head'=4,'dp'=2] {'head'}, use_global_device_ids=true, to_apply=%region_0.1 | all-reduce | flops 3072 | bytes 24576 | tf_op jit(solution)/shard_map/psum | solution.py:498
  28.3 0.0 copy-done.10
  28.3 0.0 copy-done.2
  28.3 0.0 copy-done.3
  28.3 0.0 copy-done.7
  28.3 0.0 copy-done.8
  28.4 0.6 copy-done.4
  29.0 2.1 %shard_map.154 = (bf16[128,1024]{1,0:T(8,128)(2,1)S(1)}, f32[16,64,128]{2,1,0:T(8,128)}, f32[8,16,128]{2,1,0:T(8,128)S(1)}) custom-call(f32[8,128]{1,0:T(8,128)S(1)} %copy-done.4, s32[16,128]{1,0:T(8,128)S(1)} %copy-done.8, f32[24,128]{1,0:T(8,128)S(1)} %psum.14.small, bf16[128,1024]{1,0:T(8,128)(2,1)S(1)} %bitcast.22, bf16[128,1024]{1,0:T(8,128)(2,1)S(1)} %bitcast.19, ...), custom_call_target="tpu_custom_call" | custom-call | flops 100000000 | bytes 2000000 | tf_op jit(solution)/shard_map/pallas_call | solution.py:499
  31.1 1.0 all-to-all-done.later
  32.1 6.4 %all-to-all-start.1 = ((f32[16,64,128]{2,1,0:T(8,128)}), f32[16,64,128]{2,1,0:T(8,128)S(1)}, u32[]{:S(2)}, u32[]{:S(2)}) async-start(f32[16,64,128]{2,1,0:T(8,128)} %get-tuple-element.34), calls=%async_computation.1 | async-start | bytes 1048576 | tf_op jit(solution)/shard_map/all_to_all | solution.py:469
  38.5 0.5 shard_map.155
  39.0 22.0 %all-gather = f32[384,128]{1,0:T(8,128)S(1)} all-gather(f32[96,128]{1,0:T(8,128)S(1)} %shard_map.155), channel_id=2, replica_groups=mesh['zh'=4,'zl'=4,'y'=4,'head'=4,'dp'=2] {'zh'}, dimensions={0}, use_global_device_ids=true | all-gather | bytes 245760 | tf_op jit(solution)/shard_map/all_gather | solution.py:509
  61.0 0.0 all-to-all-done.1.earlier
  61.0 0.1 shard_map.156
  61.1 1.4 %shard_map.158 = f32[16,88,128]{2,1,0:T(8,128)} custom-call(f32[8,128]{1,0:T(8,128)S(1)} %copy-done.4, f32[16,96,128]{2,1,0:T(8,128)S(1)} %all-to-all-done.later, f32[4,96,128]{2,1,0:T(8,128)S(1)} %bitcast.23, f32[8,16,128]{2,1,0:T(8,128)S(1)} %get-tuple-element.38.basis), custom_call_target="tpu_custom_call" | custom-call | flops 100000000 | bytes 2000000 | tf_op jit(solution)/shard_map/pallas_call | solution.py:514
  62.4 12.2 %all-to-all-start.3 = ((f32[16,88,128]{2,1,0:T(8,128)}), f32[16,88,128]{2,1,0:T(8,128)S(1)}, u32[]{:S(2)}, u32[]{:S(2)}) async-start(f32[16,88,128]{2,1,0:T(8,128)} %shard_map.158), calls=%async_computation.3 | async-start | bytes 1441792 | tf_op jit(solution)/shard_map/all_to_all | solution.py:469
  74.6 5.1 %collective-permute-start = (f32[64,128]{1,0:T(8,128)S(1)}, f32[64,128]{1,0:T(8,128)S(1)}, u32[]{:S(2)}, u32[]{:S(2)}) collective-permute-start(f32[64,128]{1,0:T(8,128)S(1)} %shard_map.156), channel_id=1, source_target_pairs={{0,128},{128,256},{256,384},{1,129},{129,257},{257,385},{2,130},{1... | collective-permute-start | bytes 98312 | tf_op jit(solution)/shard_map/ppermute | solution.py:473
  79.7 6.9 %collective-permute-start.1 = (f32[64,128]{1,0:T(8,128)S(1)}, f32[64,128]{1,0:T(8,128)S(1)}, u32[]{:S(2)}, u32[]{:S(2)}) collective-permute-start(f32[64,128]{1,0:T(8,128)S(1)} %shard_map.156), channel_id=1, source_target_pairs={{0,256},{128,384},{1,257},{129,385},{2,258},{130,386},{3,259},{131... | collective-permute-start | bytes 98312 | tf_op jit(solution)/shard_map/ppermute | solution.py:473
  86.7 1.3 %collective-permute-start.2 = (f32[64,128]{1,0:T(8,128)S(1)}, f32[64,128]{1,0:T(8,128)S(1)}, u32[]{:S(2)}, u32[]{:S(2)}) collective-permute-start(f32[64,128]{1,0:T(8,128)S(1)} %shard_map.156), channel_id=1, source_target_pairs={{0,384},{1,385},{2,386},{3,387},{4,388},{5,389},{6,390},{7,391},{8... | collective-permute-start | bytes 98312 | tf_op jit(solution)/shard_map/ppermute | solution.py:473
  88.0 0.0 collective-permute-done.one
  88.0 0.0 collective-permute-done.1.two
  88.0 1.5 %collective-permute-done.2.three = f32[64,128]{1,0:T(8,128)S(1)} collective-permute-done((f32[64,128]{1,0:T(8,128)S(1)}, f32[64,128]{1,0:T(8,128)S(1)}, u32[]{:S(2)}, u32[]{:S(2)}) %collective-permute-start.2) | collective-permute-done | bytes 32800 | tf_op jit(solution)/shard_map/ppermute | solution.py:473
  89.4 0.9 shard_map.157
  90.3 0.0 all-to-all-done.3.x.state
  90.3 7.3 %all-to-all-start.2 = ((f32[16,64,128]{2,1,0:T(8,128)}), f32[16,64,128]{2,1,0:T(8,128)S(1)}, u32[]{:S(2)}, u32[]{:S(2)}) async-start(f32[16,64,128]{2,1,0:T(8,128)} %shard_map.157), calls=%async_computation.2 | async-start | bytes 1048576 | tf_op jit(solution)/shard_map/all_to_all | solution.py:469
  97.6 0.1 shard_map.159
  97.7 9.5 %psum.15.head_sums = f32[16,128]{1,0:T(8,128)S(1)} all-reduce(f32[16,128]{1,0:T(8,128)S(1)} %shard_map.159), channel_id=1, replica_groups=mesh['zh'=4,'zl'=4,'y'=4,'head'=4,'dp'=2] {'head'}, use_global_device_ids=true, to_apply=%region_1.2 | all-reduce | flops 2048 | bytes 16384 | tf_op jit(solution)/shard_map/psum | solution.py:531
  107.2 0.0 copy-start
  107.3 0.0 copy-start.1
  107.3 0.5 shard_map.161.parts
  107.8 8.7 %collective-permute-start.3 = (f32[72,128]{1,0:T(8,128)S(1)}, f32[72,128]{1,0:T(8,128)S(1)}, u32[]{:S(2)}, u32[]{:S(2)}) collective-permute-start(f32[72,128]{1,0:T(8,128)S(1)} %shard_map.161.parts), channel_id=1, source_target_pairs={{0,1},{1,0},{2,3},{3,2},{4,5},{5,4},{6,7},{7,6},{8,9},{9,8},{10,11... | collective-permute-start | bytes 110600 | tf_op jit(solution)/shard_map/ppermute | solution.py:534
  116.5 0.0 copy-done
  116.5 0.0 copy-done.1
  116.5 2.9 %shard_map.160 = (f32[128,1024]{1,0:T(8,128)S(1)}, f32[128,1024]{1,0:T(8,128)S(1)}, bf16[128,1024]{1,0:T(8,128)(2,1)}, bf16[128,1024]{1,0:T(8,128)(2,1)}) custom-call(f32[8,128]{1,0:T(8,128)S(1)} %copy-done.4, s32[16,128]{1,0:T(8,128)S(1)} %copy-done.8, bf16[128,1024]{1,0:T(8,128)(2,1)S(1)} %bitcast.13, bf16[128,1024]{1,0:T(8,128)(2,1)S(1)} %bitcast.20, ...), custom_call_target="tpu_custom_call" | custom-call | flops 100000000 | bytes 2000000 | tf_op jit(solution)/shard_map/pallas_call | solution.py:535
  119.4 0.0 all-to-all-done.2.state
  119.4 0.0 collective-permute-done.3.others
  119.4 1.8 %shard_map.162 = (bf16[128,1024]{1,0:T(8,128)(2,1)}, bf16[128,1024]{1,0:T(8,128)(2,1)}, f32[4,1024]{1,0:T(4,128)}, f32[4,1024]{1,0:T(4,128)}, f32[4]{0:T(128)}) custom-call(f32[8,128]{1,0:T(8,128)S(1)} %copy-done.4, bf16[128,1024]{1,0:T(8,128)(2,1)S(1)} %bitcast.14, bf16[128,1024]{1,0:T(8,128)(2,1)S(1)} %bitcast.17, ...), custom_call_target="tpu_custom_call" | custom-call | flops 100000000 | bytes 2000000 | tf_op jit(solution)/shard_map/pallas_call | solution.py:542
  (4 shorter events, 0.0 us)
Async XLA Ops:
  4.9 9.4 %copy-start.9 = (f32[24,128]{1,0:T(8,128)S(1)}, f32[24,128]{1,0:T(8,128)}, u32[]{:S(2)}) copy-start(f32[24,128]{1,0:T(8,128)} %get-tuple-element.30) | copy-start | bytes 36868
  4.9 23.4 %copy-start.2 = (bf16[1,128,1024]{2,1,0:T(8,128)(2,1)S(1)}, bf16[1,128,1024]{2,1,0:T(8,128)(2,1)}, u32[]{:S(2)}) copy-start(bf16[1,128,1024]{2,1,0:T(8,128)(2,1)} %param.11) | copy-start | bytes 786436
  4.9 23.4 %copy-start.3 = (bf16[1,128,1024]{2,1,0:T(8,128)(2,1)S(1)}, bf16[1,128,1024]{2,1,0:T(8,128)(2,1)}, u32[]{:S(2)}) copy-start(bf16[1,128,1024]{2,1,0:T(8,128)(2,1)} %param.12) | copy-start | bytes 786436
  4.9 23.4 %copy-start.7 = (f32[4,1024]{1,0:T(4,128)S(1)}, f32[4,1024]{1,0:T(4,128)}, u32[]{:S(2)}) copy-start(f32[4,1024]{1,0:T(4,128)} %proj.3) | copy-start | bytes 49156
  4.9 23.4 %copy-start.8 = (s32[16,128]{1,0:T(8,128)S(1)}, s32[16,128]{1,0:T(8,128)}, u32[]{:S(2)}) copy-start(s32[16,128]{1,0:T(8,128)} %get-tuple-element.29.places) | copy-start | bytes 24580
  4.9 27.1 %all-to-all-start = ((f32[16,96,128]{2,1,0:T(8,128)}), f32[16,96,128]{2,1,0:T(8,128)S(1)}, u32[]{:S(2)}, u32[]{:S(2)}) async-start(f32[16,96,128]{2,1,0:T(8,128)} %get-tuple-element.32), calls=%async_computation | async-start | bytes 1572864 | tf_op jit(solution)/shard_map/all_to_all | solution.py:469
  14.3 14.1 %copy-start.6 = (f32[4,1024]{1,0:T(4,128)S(1)}, f32[4,1024]{1,0:T(4,128)}, u32[]{:S(2)}) copy-start(f32[4,1024]{1,0:T(4,128)} %rot.3) | copy-start | bytes 49156
  14.3 14.0 %copy-start.10 = (f32[4]{0:T(128)S(1)}, f32[4]{0:T(128)}, u32[]{:S(2)}) copy-start(f32[4]{0:T(128)} %param.18) | copy-start | bytes 52
  14.3 14.0 %copy-start.5 = (f32[1024,2]{0,1:T(2,128)S(1)}, f32[1024,2]{0,1:T(2,128)}, u32[]{:S(2)}) copy-start(f32[1024,2]{0,1:T(2,128)} %param.16) | copy-start | bytes 24580
  28.3 0.7 copy-start.4
  32.1 29.0 %all-to-all-start.1 = ((f32[16,64,128]{2,1,0:T(8,128)}), f32[16,64,128]{2,1,0:T(8,128)S(1)}, u32[]{:S(2)}, u32[]{:S(2)}) async-start(f32[16,64,128]{2,1,0:T(8,128)} %get-tuple-element.34), calls=%async_computation.1 | async-start | bytes 1048576 | tf_op jit(solution)/shard_map/all_to_all | solution.py:469
  62.4 27.9 %all-to-all-start.3 = ((f32[16,88,128]{2,1,0:T(8,128)}), f32[16,88,128]{2,1,0:T(8,128)S(1)}, u32[]{:S(2)}, u32[]{:S(2)}) async-start(f32[16,88,128]{2,1,0:T(8,128)} %shard_map.158), calls=%async_computation.3 | async-start | bytes 1441792 | tf_op jit(solution)/shard_map/all_to_all | solution.py:469
  74.6 13.3 %collective-permute-start = (f32[64,128]{1,0:T(8,128)S(1)}, f32[64,128]{1,0:T(8,128)S(1)}, u32[]{:S(2)}, u32[]{:S(2)}) collective-permute-start(f32[64,128]{1,0:T(8,128)S(1)} %shard_map.156), channel_id=1, source_target_pairs={{0,128},{128,256},{256,384},{1,129},{129,257},{257,385},{2,130},{1... | collective-permute-start | bytes 98312 | tf_op jit(solution)/shard_map/ppermute | solution.py:473
  79.7 8.3 %collective-permute-start.1 = (f32[64,128]{1,0:T(8,128)S(1)}, f32[64,128]{1,0:T(8,128)S(1)}, u32[]{:S(2)}, u32[]{:S(2)}) collective-permute-start(f32[64,128]{1,0:T(8,128)S(1)} %shard_map.156), channel_id=1, source_target_pairs={{0,256},{128,384},{1,257},{129,385},{2,258},{130,386},{3,259},{131... | collective-permute-start | bytes 98312 | tf_op jit(solution)/shard_map/ppermute | solution.py:473
  86.7 2.8 %collective-permute-start.2 = (f32[64,128]{1,0:T(8,128)S(1)}, f32[64,128]{1,0:T(8,128)S(1)}, u32[]{:S(2)}, u32[]{:S(2)}) collective-permute-start(f32[64,128]{1,0:T(8,128)S(1)} %shard_map.156), channel_id=1, source_target_pairs={{0,384},{1,385},{2,386},{3,387},{4,388},{5,389},{6,390},{7,391},{8... | collective-permute-start | bytes 98312 | tf_op jit(solution)/shard_map/ppermute | solution.py:473
  90.3 29.1 %all-to-all-start.2 = ((f32[16,64,128]{2,1,0:T(8,128)}), f32[16,64,128]{2,1,0:T(8,128)S(1)}, u32[]{:S(2)}, u32[]{:S(2)}) async-start(f32[16,64,128]{2,1,0:T(8,128)} %shard_map.157), calls=%async_computation.2 | async-start | bytes 1048576 | tf_op jit(solution)/shard_map/all_to_all | solution.py:469
  107.2 9.3 %copy-start = (bf16[1,128,1024]{2,1,0:T(8,128)(2,1)S(1)}, bf16[1,128,1024]{2,1,0:T(8,128)(2,1)}, u32[]{:S(2)}) copy-start(bf16[1,128,1024]{2,1,0:T(8,128)(2,1)} %param.10) | copy-start | bytes 786436
  107.3 9.3 %copy-start.1 = (bf16[1,128,1024]{2,1,0:T(8,128)(2,1)S(1)}, bf16[1,128,1024]{2,1,0:T(8,128)(2,1)}, u32[]{:S(2)}) copy-start(bf16[1,128,1024]{2,1,0:T(8,128)(2,1)} %param.13) | copy-start | bytes 786436
  107.8 11.6 %collective-permute-start.3 = (f32[72,128]{1,0:T(8,128)S(1)}, f32[72,128]{1,0:T(8,128)S(1)}, u32[]{:S(2)}, u32[]{:S(2)}) collective-permute-start(f32[72,128]{1,0:T(8,128)S(1)} %shard_map.161.parts), channel_id=1, source_target_pairs={{0,1},{1,0},{2,3},{3,2},{4,5},{5,4},{6,7},{7,6},{8,9},{9,8},{10,11... | collective-permute-start | bytes 110600 | tf_op jit(solution)/shard_map/ppermute | solution.py:534

commit v7 on v6

--- a/solution.py
+++ b/solution.py
@@ -385,6 +385,11 @@
     select = selector(places)
     select = jnp.concatenate([select, select, select], axis=0)
     code_grad = head_sums[...]
+    lift = jnp.concatenate([basis[h][6:10] for h in range(HEADS)], axis=1)
+    fix = jnp.zeros((NPOS, WIDE), f32)
+    for r in range(4):
+        fix = fix + code_grad[:, r : r + 1] * lift[r : r + 1]
+    fix = tn(select, third_terms(fix))
     for h in range(HEADS):
         c = head_cols(h)
         table = jnp.where(lower, powers(logs, h, distance), 0.0)
@@ -398,12 +403,8 @@
         inner = tn(grad_mixing, qh)
         grad_k[:, c] = (inner + leave * nn_terms(mh, terms)).astype(bf16)
         inner = tn(mixing, gh)
-        lift = basis[h][6:10]
-        fix = jnp.zeros((NPOS, SIZE), f32)
-        for r in range(4):
-            fix = fix + code_grad[:, r : r + 1] * lift[r : r + 1]
         out = inner + leave * nt_terms(kh, terms)
-        grad_v[:, c] = (out + tn(select, third_terms(fix))).astype(bf16)
+        grad_v[:, c] = (out + fix[:, c]).astype(bf16)
         if h % 2 == 1:
             wide = slice((h - 1) * SIZE, (h + 1) * SIZE)
             for n, (src, dst) in enumerate(((grad_k, grad_k_far), (grad_v, grad_v_far))):

time: 122 us -> 122 us (level)
  no operation moved by 1% of the time
where the time goes in v7:
time: 122 us; the launch traced here: 121 us
  starting transfers between devices  57.2 us (47%)
  blocking collectives  45.5 us (37%)
  Pallas kernels  14.3 us (12%)
  waiting for transfers between devices  2.45 us (2%)
    all_to_all x4, starting transfers between devices, swap(): return lax.all_to_all(x, axes, 0, 0, tiled=False)  35.2 us
    all_gather x1, blocking collectives, shards(): groups = lax.all_gather(own, 'zh')  22 us
    psum x1, blocking collectives, shards(): small = lax.psum(small, 'head')  14 us
    ppermute x3, starting transfers between devices, ahead(): return lax.ppermute(x, 'zh', [(i, i + d) for i in range(4 - d)])  13.3 us
    psum x1, blocking collectives, shards(): head_sums = lax.psum(head_sums, 'head')  9.51 us
    ppermute x1, starting transfers between devices, shards(): others = lax.ppermute(parts, 'dp', [(0, 1), (1, 0)])  8.69 us
    pallas_call x1, Pallas kernels, shards(): call(query_state, 'ssaaaavvv', [((16, 96, 128), f32), ((24, 128), f32), (...  4.24 us
    pallas_call x1, Pallas kernels, shards(): call(backward_rest, 'v' * 9, [(rows, f32)] * 2 + [(rows, bf16)] * 2, [spa...  2.79 us
  transfers between devices with their start and end apart: 8, of which 2 were waited for; matrix products, arithmetic and copies ran while one was open for 0% of the time, Pallas kernels for 6%

profile of v7, /device:TPU:1, one launch (start us, length us, event | category | flops | bytes accessed | tf_op | source)
XLA Modules:
  0.0 121.1 jit_solution(16291691012517109404)
XLA Ops:
  0.6 4.2 %shard_map.153 = (f32[16,96,128]{2,1,0:T(8,128)}, f32[24,128]{1,0:T(8,128)}, f32[8,128]{1,0:T(8,128)}, s32[16,128]{1,0:T(8,128)}) custom-call(f32[8]{0:T(128)} %rate.1, s32[1,16]{1,0:T(1,128)} %positions.1, bf16[128,1024]{1,0:T(8,128)(2,1)} %bitcast.12, bf16[128,1024]{1,0:T(8,128)(2,1)} %bitcast.18, bf16[128,1024]{1,0:T(8,128)(2,1)} %bitcast.15, ...), custom_call_target="tpu_custom_call" | custom-call | flops 100000000 | bytes 2000000 | tf_op jit(solution)/shard_map/pallas_call | solution.py:490
  4.9 0.0 copy-start.9
  4.9 0.0 copy-start.2
  4.9 0.0 copy-start.3
  4.9 0.0 copy-start.7
  4.9 0.0 copy-start.8
  4.9 9.3 %all-to-all-start = ((f32[16,96,128]{2,1,0:T(8,128)}), f32[16,96,128]{2,1,0:T(8,128)S(1)}, u32[]{:S(2)}, u32[]{:S(2)}) async-start(f32[16,96,128]{2,1,0:T(8,128)} %get-tuple-element.32), calls=%async_computation | async-start | bytes 1572864 | tf_op jit(solution)/shard_map/all_to_all | solution.py:470
  14.3 0.0 copy-start.6
  14.3 0.0 copy-done.9
  14.3 0.0 copy-start.10
  14.3 0.0 copy-start.5
  14.3 14.0 %psum.14.small = f32[24,128]{1,0:T(8,128)S(1)} all-reduce(f32[24,128]{1,0:T(8,128)S(1)} %copy-done.9), channel_id=1, replica_groups=mesh['zh'=4,'zl'=4,'y'=4,'head'=4,'dp'=2] {'head'}, use_global_device_ids=true, to_apply=%region_0.1 | all-reduce | flops 3072 | bytes 24576 | tf_op jit(solution)/shard_map/psum | solution.py:499
  28.3 0.0 copy-done.10
  28.3 0.0 copy-done.2
  28.3 0.0 copy-done.3
  28.3 0.0 copy-done.7
  28.3 0.0 copy-done.8
  28.3 0.0 copy-done.6
  28.4 0.0 copy-done.5
  28.4 0.6 copy-done.4
  29.0 2.1 %shard_map.154 = (bf16[128,1024]{1,0:T(8,128)(2,1)S(1)}, f32[16,64,128]{2,1,0:T(8,128)}, f32[8,16,128]{2,1,0:T(8,128)S(1)}) custom-call(f32[8,128]{1,0:T(8,128)S(1)} %copy-done.4, s32[16,128]{1,0:T(8,128)S(1)} %copy-done.8, f32[24,128]{1,0:T(8,128)S(1)} %psum.14.small, bf16[128,1024]{1,0:T(8,128)(2,1)S(1)} %bitcast.22, bf16[128,1024]{1,0:T(8,128)(2,1)S(1)} %bitcast.19, ...), custom_call_target="tpu_custom_call" | custom-call | flops 100000000 | bytes 2000000 | tf_op jit(solution)/shard_map/pallas_call | solution.py:500
  31.1 1.0 all-to-all-done.later
  32.1 6.4 %all-to-all-start.1 = ((f32[16,64,128]{2,1,0:T(8,128)}), f32[16,64,128]{2,1,0:T(8,128)S(1)}, u32[]{:S(2)}, u32[]{:S(2)}) async-start(f32[16,64,128]{2,1,0:T(8,128)} %get-tuple-element.34), calls=%async_computation.1 | async-start | bytes 1048576 | tf_op jit(solution)/shard_map/all_to_all | solution.py:470
  38.5 0.5 shard_map.155
  39.0 22.0 %all-gather = f32[384,128]{1,0:T(8,128)S(1)} all-gather(f32[96,128]{1,0:T(8,128)S(1)} %shard_map.155), channel_id=2, replica_groups=mesh['zh'=4,'zl'=4,'y'=4,'head'=4,'dp'=2] {'zh'}, dimensions={0}, use_global_device_ids=true | all-gather | bytes 245760 | tf_op jit(solution)/shard_map/all_gather | solution.py:510
  61.0 0.0 all-to-all-done.1.earlier
  61.0 0.1 shard_map.156
  61.1 1.4 %shard_map.158 = f32[16,88,128]{2,1,0:T(8,128)} custom-call(f32[8,128]{1,0:T(8,128)S(1)} %copy-done.4, f32[16,96,128]{2,1,0:T(8,128)S(1)} %all-to-all-done.later, f32[4,96,128]{2,1,0:T(8,128)S(1)} %bitcast.23, f32[8,16,128]{2,1,0:T(8,128)S(1)} %get-tuple-element.38.basis), custom_call_target="tpu_custom_call" | custom-call | flops 100000000 | bytes 2000000 | tf_op jit(solution)/shard_map/pallas_call | solution.py:515
  62.4 12.2 %all-to-all-start.3 = ((f32[16,88,128]{2,1,0:T(8,128)}), f32[16,88,128]{2,1,0:T(8,128)S(1)}, u32[]{:S(2)}, u32[]{:S(2)}) async-start(f32[16,88,128]{2,1,0:T(8,128)} %shard_map.158), calls=%async_computation.3 | async-start | bytes 1441792 | tf_op jit(solution)/shard_map/all_to_all | solution.py:470
  74.6 5.1 %collective-permute-start = (f32[64,128]{1,0:T(8,128)S(1)}, f32[64,128]{1,0:T(8,128)S(1)}, u32[]{:S(2)}, u32[]{:S(2)}) collective-permute-start(f32[64,128]{1,0:T(8,128)S(1)} %shard_map.156), channel_id=1, source_target_pairs={{0,128},{128,256},{256,384},{1,129},{129,257},{257,385},{2,130},{1... | collective-permute-start | bytes 98312 | tf_op jit(solution)/shard_map/ppermute | solution.py:474
  79.7 6.9 %collective-permute-start.1 = (f32[64,128]{1,0:T(8,128)S(1)}, f32[64,128]{1,0:T(8,128)S(1)}, u32[]{:S(2)}, u32[]{:S(2)}) collective-permute-start(f32[64,128]{1,0:T(8,128)S(1)} %shard_map.156), channel_id=1, source_target_pairs={{0,256},{128,384},{1,257},{129,385},{2,258},{130,386},{3,259},{131... | collective-permute-start | bytes 98312 | tf_op jit(solution)/shard_map/ppermute | solution.py:474
  86.7 1.3 %collective-permute-start.2 = (f32[64,128]{1,0:T(8,128)S(1)}, f32[64,128]{1,0:T(8,128)S(1)}, u32[]{:S(2)}, u32[]{:S(2)}) collective-permute-start(f32[64,128]{1,0:T(8,128)S(1)} %shard_map.156), channel_id=1, source_target_pairs={{0,384},{1,385},{2,386},{3,387},{4,388},{5,389},{6,390},{7,391},{8... | collective-permute-start | bytes 98312 | tf_op jit(solution)/shard_map/ppermute | solution.py:474
  88.0 0.0 collective-permute-done.one
  88.0 0.0 collective-permute-done.1.two
  88.0 1.5 %collective-permute-done.2.three = f32[64,128]{1,0:T(8,128)S(1)} collective-permute-done((f32[64,128]{1,0:T(8,128)S(1)}, f32[64,128]{1,0:T(8,128)S(1)}, u32[]{:S(2)}, u32[]{:S(2)}) %collective-permute-start.2) | collective-permute-done | bytes 32800 | tf_op jit(solution)/shard_map/ppermute | solution.py:474
  89.4 0.9 shard_map.157
  90.3 0.0 all-to-all-done.3.x.state
  90.3 7.3 %all-to-all-start.2 = ((f32[16,64,128]{2,1,0:T(8,128)}), f32[16,64,128]{2,1,0:T(8,128)S(1)}, u32[]{:S(2)}, u32[]{:S(2)}) async-start(f32[16,64,128]{2,1,0:T(8,128)} %shard_map.157), calls=%async_computation.2 | async-start | bytes 1048576 | tf_op jit(solution)/shard_map/all_to_all | solution.py:470
  97.6 0.1 shard_map.159
  97.7 9.5 %psum.15.head_sums = f32[16,128]{1,0:T(8,128)S(1)} all-reduce(f32[16,128]{1,0:T(8,128)S(1)} %shard_map.159), channel_id=1, replica_groups=mesh['zh'=4,'zl'=4,'y'=4,'head'=4,'dp'=2] {'head'}, use_global_device_ids=true, to_apply=%region_1.2 | all-reduce | flops 2048 | bytes 16384 | tf_op jit(solution)/shard_map/psum | solution.py:532
  107.2 0.0 copy-start
  107.3 0.0 copy-start.1
  107.3 0.5 shard_map.161.parts
  107.8 8.7 %collective-permute-start.3 = (f32[72,128]{1,0:T(8,128)S(1)}, f32[72,128]{1,0:T(8,128)S(1)}, u32[]{:S(2)}, u32[]{:S(2)}) collective-permute-start(f32[72,128]{1,0:T(8,128)S(1)} %shard_map.161.parts), channel_id=1, source_target_pairs={{0,1},{1,0},{2,3},{3,2},{4,5},{5,4},{6,7},{7,6},{8,9},{9,8},{10,11... | collective-permute-start | bytes 110600 | tf_op jit(solution)/shard_map/ppermute | solution.py:535
  116.5 2.8 %shard_map.160 = (f32[128,1024]{1,0:T(8,128)S(1)}, f32[128,1024]{1,0:T(8,128)S(1)}, bf16[128,1024]{1,0:T(8,128)(2,1)}, bf16[128,1024]{1,0:T(8,128)(2,1)}) custom-call(f32[8,128]{1,0:T(8,128)S(1)} %copy-done.4, s32[16,128]{1,0:T(8,128)S(1)} %copy-done.8, bf16[128,1024]{1,0:T(8,128)(2,1)S(1)} %bitcast.13, bf16[128,1024]{1,0:T(8,128)(2,1)S(1)} %bitcast.20, ...), custom_call_target="tpu_custom_call" | custom-call | flops 100000000 | bytes 2000000 | tf_op jit(solution)/shard_map/pallas_call | solution.py:536
  119.3 0.0 all-to-all-done.2.state
  119.4 0.0 collective-permute-done.3.others
  119.4 1.8 %shard_map.162 = (bf16[128,1024]{1,0:T(8,128)(2,1)}, bf16[128,1024]{1,0:T(8,128)(2,1)}, f32[4,1024]{1,0:T(4,128)}, f32[4,1024]{1,0:T(4,128)}, f32[4]{0:T(128)}) custom-call(f32[8,128]{1,0:T(8,128)S(1)} %copy-done.4, bf16[128,1024]{1,0:T(8,128)(2,1)S(1)} %bitcast.14, bf16[128,1024]{1,0:T(8,128)(2,1)S(1)} %bitcast.17, ...), custom_call_target="tpu_custom_call" | custom-call | flops 100000000 | bytes 2000000 | tf_op jit(solution)/shard_map/pallas_call | solution.py:543
  (4 shorter events, 0.0 us)
Async XLA Ops:
  4.9 9.4 %copy-start.9 = (f32[24,128]{1,0:T(8,128)S(1)}, f32[24,128]{1,0:T(8,128)}, u32[]{:S(2)}) copy-start(f32[24,128]{1,0:T(8,128)} %get-tuple-element.30) | copy-start | bytes 36868
  4.9 23.4 %copy-start.2 = (bf16[1,128,1024]{2,1,0:T(8,128)(2,1)S(1)}, bf16[1,128,1024]{2,1,0:T(8,128)(2,1)}, u32[]{:S(2)}) copy-start(bf16[1,128,1024]{2,1,0:T(8,128)(2,1)} %param.11) | copy-start | bytes 786436
  4.9 23.4 %copy-start.3 = (bf16[1,128,1024]{2,1,0:T(8,128)(2,1)S(1)}, bf16[1,128,1024]{2,1,0:T(8,128)(2,1)}, u32[]{:S(2)}) copy-start(bf16[1,128,1024]{2,1,0:T(8,128)(2,1)} %param.12) | copy-start | bytes 786436
  4.9 23.4 %copy-start.7 = (f32[4,1024]{1,0:T(4,128)S(1)}, f32[4,1024]{1,0:T(4,128)}, u32[]{:S(2)}) copy-start(f32[4,1024]{1,0:T(4,128)} %proj.3) | copy-start | bytes 49156
  4.9 23.4 %copy-start.8 = (s32[16,128]{1,0:T(8,128)S(1)}, s32[16,128]{1,0:T(8,128)}, u32[]{:S(2)}) copy-start(s32[16,128]{1,0:T(8,128)} %get-tuple-element.29.places) | copy-start | bytes 24580
  4.9 27.1 %all-to-all-start = ((f32[16,96,128]{2,1,0:T(8,128)}), f32[16,96,128]{2,1,0:T(8,128)S(1)}, u32[]{:S(2)}, u32[]{:S(2)}) async-start(f32[16,96,128]{2,1,0:T(8,128)} %get-tuple-element.32), calls=%async_computation | async-start | bytes 1572864 | tf_op jit(solution)/shard_map/all_to_all | solution.py:470
  14.3 14.1 %copy-start.6 = (f32[4,1024]{1,0:T(4,128)S(1)}, f32[4,1024]{1,0:T(4,128)}, u32[]{:S(2)}) copy-start(f32[4,1024]{1,0:T(4,128)} %rot.3) | copy-start | bytes 49156
  14.3 14.0 %copy-start.10 = (f32[4]{0:T(128)S(1)}, f32[4]{0:T(128)}, u32[]{:S(2)}) copy-start(f32[4]{0:T(128)} %param.18) | copy-start | bytes 52
  14.3 14.0 %copy-start.5 = (f32[1024,2]{0,1:T(2,128)S(1)}, f32[1024,2]{0,1:T(2,128)}, u32[]{:S(2)}) copy-start(f32[1024,2]{0,1:T(2,128)} %param.16) | copy-start | bytes 24580
  28.3 0.7 copy-start.4
  32.1 29.0 %all-to-all-start.1 = ((f32[16,64,128]{2,1,0:T(8,128)}), f32[16,64,128]{2,1,0:T(8,128)S(1)}, u32[]{:S(2)}, u32[]{:S(2)}) async-start(f32[16,64,128]{2,1,0:T(8,128)} %get-tuple-element.34), calls=%async_computation.1 | async-start | bytes 1048576 | tf_op jit(solution)/shard_map/all_to_all | solution.py:470
  62.4 27.9 %all-to-all-start.3 = ((f32[16,88,128]{2,1,0:T(8,128)}), f32[16,88,128]{2,1,0:T(8,128)S(1)}, u32[]{:S(2)}, u32[]{:S(2)}) async-start(f32[16,88,128]{2,1,0:T(8,128)} %shard_map.158), calls=%async_computation.3 | async-start | bytes 1441792 | tf_op jit(solution)/shard_map/all_to_all | solution.py:470
  74.6 13.3 %collective-permute-start = (f32[64,128]{1,0:T(8,128)S(1)}, f32[64,128]{1,0:T(8,128)S(1)}, u32[]{:S(2)}, u32[]{:S(2)}) collective-permute-start(f32[64,128]{1,0:T(8,128)S(1)} %shard_map.156), channel_id=1, source_target_pairs={{0,128},{128,256},{256,384},{1,129},{129,257},{257,385},{2,130},{1... | collective-permute-start | bytes 98312 | tf_op jit(solution)/shard_map/ppermute | solution.py:474
  79.7 8.3 %collective-permute-start.1 = (f32[64,128]{1,0:T(8,128)S(1)}, f32[64,128]{1,0:T(8,128)S(1)}, u32[]{:S(2)}, u32[]{:S(2)}) collective-permute-start(f32[64,128]{1,0:T(8,128)S(1)} %shard_map.156), channel_id=1, source_target_pairs={{0,256},{128,384},{1,257},{129,385},{2,258},{130,386},{3,259},{131... | collective-permute-start | bytes 98312 | tf_op jit(solution)/shard_map/ppermute | solution.py:474
  86.7 2.8 %collective-permute-start.2 = (f32[64,128]{1,0:T(8,128)S(1)}, f32[64,128]{1,0:T(8,128)S(1)}, u32[]{:S(2)}, u32[]{:S(2)}) collective-permute-start(f32[64,128]{1,0:T(8,128)S(1)} %shard_map.156), channel_id=1, source_target_pairs={{0,384},{1,385},{2,386},{3,387},{4,388},{5,389},{6,390},{7,391},{8... | collective-permute-start | bytes 98312 | tf_op jit(solution)/shard_map/ppermute | solution.py:474
  90.3 29.0 %all-to-all-start.2 = ((f32[16,64,128]{2,1,0:T(8,128)}), f32[16,64,128]{2,1,0:T(8,128)S(1)}, u32[]{:S(2)}, u32[]{:S(2)}) async-start(f32[16,64,128]{2,1,0:T(8,128)} %shard_map.157), calls=%async_computation.2 | async-start | bytes 1048576 | tf_op jit(solution)/shard_map/all_to_all | solution.py:470
  107.2 9.3 %copy-start = (bf16[1,128,1024]{2,1,0:T(8,128)(2,1)S(1)}, bf16[1,128,1024]{2,1,0:T(8,128)(2,1)}, u32[]{:S(2)}) copy-start(bf16[1,128,1024]{2,1,0:T(8,128)(2,1)} %param.10) | copy-start | bytes 786436
  107.3 9.3 %copy-start.1 = (bf16[1,128,1024]{2,1,0:T(8,128)(2,1)S(1)}, bf16[1,128,1024]{2,1,0:T(8,128)(2,1)}, u32[]{:S(2)}) copy-start(bf16[1,128,1024]{2,1,0:T(8,128)(2,1)} %param.13) | copy-start | bytes 786436
  107.8 11.5 %collective-permute-start.3 = (f32[72,128]{1,0:T(8,128)S(1)}, f32[72,128]{1,0:T(8,128)S(1)}, u32[]{:S(2)}, u32[]{:S(2)}) collective-permute-start(f32[72,128]{1,0:T(8,128)S(1)} %shard_map.161.parts), channel_id=1, source_target_pairs={{0,1},{1,0},{2,3},{3,2},{4,5},{5,4},{6,7},{7,6},{8,9},{9,8},{10,11... | collective-permute-start | bytes 110600 | tf_op jit(solution)/shard_map/ppermute | solution.py:535
